TPU v7x, 512 devices: a whole 4x8x8 slice. The times are simulated.
512 devices in a mesh: chan: 64 (over y_lo, z, x), freq: 8 (over y_hi, core).
Axes of the slice: x: 4, y: 8 (y_hi: 4, y_lo: 2; y = y_hi * 2 + y_lo), z: 8, core: 2. Of those that a mesh axis runs over, the one named last changes fastest.
Arguments:
- spectra: bfloat16 [20480, 2, 2, 2048], P('chan', None, None, 'freq'), may hold values from -60 to 60
- validity: int32 [20480, 2], P('chan'), may hold values from 0 to 1, as said below
- pair_mask: int32 [64, 2, 5, 5], replicated, may hold values from 0 to 1, as said below
- owners: int32 [64, 50], replicated, may hold values from 0 to 63, as said below
Outputs:
- stacked: bfloat16 [64, 64, 1, 64, 256], P('chan', None, None, 'freq')
Inputs may be any that keep to these rules, and one draw needn't show every extreme that they name: `validity`: some channels have no usable segment. `pair_mask`: entry [b, d, u, v] pairs sub-block u of block b with sub-block v of block (b + d + 1) mod 64. Each block lists the distances 1 up to a level of its own, at least distance 1; some block lists all 2. A row gives the owners of one block's candidate sub-tiles in order, in runs of 1 consecutive entries; the runs of a row go to distinct owners, so one owner gets at most 1 of one block's sub-tiles, and the first run reaches it.
All inputs are finite; a program needn't handle non-finite values.
Results may differ from a plain program's by a relative error of at most 0.02.
Values may be sent and summed in bfloat16 or wider, within the bound.
No kernel may reach another device: no remote copies, remote signals or barrier semaphores. Data moves between devices by JAX's collectives and lax.ppermute only.
A program may use at most 64 MiB of HBM per device.

v0:
```python
import math

import jax
import jax.numpy as jnp
from jax import lax
from jax.sharding import PartitionSpec as P

FREQS = 2048
LAGS = 4
LAG_STEP = 25
HALF = 32


EPS = 1e-06


def extended(block, sides, width):
    for axis, dim in sides:
        count = lax.axis_size(axis)
        forward = [(i, i + 1) for i in range(count - 1)]
        backward = [(target, source) for source, target in forward]
        low = lax.ppermute(
            lax.slice_in_dim(block, block.shape[dim] - width, None, axis=dim), axis, forward
        )
        high = lax.ppermute(lax.slice_in_dim(block, 0, width, axis=dim), axis, backward)
        block = jnp.concatenate([low, block, high], axis=dim)
    return block


def shortened(x):
    return jax.tree.map(lambda a: a.astype(jnp.bfloat16) if a.dtype == jnp.float32 else a, x)


def shifted(block, axis, distance):
    devices = range(lax.axis_size(axis))
    route = [((i - distance) % len(devices), i) for i in devices]
    return lax.ppermute(block, axis, route)


def lag_tables(first_bin, count):
    bin_index = first_bin + jnp.arange(count, dtype=jnp.int32)
    lag_values = (jnp.arange(LAGS, dtype=jnp.int32) - LAGS // 2) * LAG_STEP
    turn_count = lag_values[:, None] * bin_index[None, :] % (2 * FREQS)
    phase_angle = turn_count.astype(jnp.float32) * (math.pi / FREQS)
    return (jnp.cos(phase_angle), jnp.sin(phase_angle))


def amplitude_sum(values, weights):
    magnitude = jnp.sqrt(values[:, 0] ** 2 + values[:, 1] ** 2)
    return jnp.sum(magnitude * weights[:, :, None], axis=1)


def whiten(values, weights, padded, first_bin, count):
    cumulate = jnp.cumsum(padded, axis=1)
    cumulate = jnp.concatenate([jnp.zeros((padded.shape[0], 1), jnp.float32), cumulate], axis=1)
    window = cumulate[:, 2 * HALF + 1 :] - cumulate[:, :count]
    bin_index = first_bin + jnp.arange(count, dtype=jnp.int32)
    lower = jnp.maximum(bin_index - HALF, 0)
    upper = jnp.minimum(bin_index + HALF, FREQS - 1)
    bin_count = (upper - lower + 1).astype(jnp.float32)
    seg_count = jnp.maximum(jnp.sum(weights, axis=1), 1.0)
    mean_level = window / (bin_count[None, :] * seg_count[:, None])
    scaled = values * weights[:, None, :, None] / (mean_level[:, None, None, :] + EPS)
    return scaled.astype(jnp.bfloat16)


def rotate(right_block, cosine_table, sine_table):
    right_float = right_block.astype(jnp.float32)
    real_part = (
        right_float[None, :, 0] * cosine_table[:, None, None, :]
        + right_float[None, :, 1] * sine_table[:, None, None, :]
    )
    imag_part = (
        right_float[None, :, 1] * cosine_table[:, None, None, :]
        - right_float[None, :, 0] * sine_table[:, None, None, :]
    )
    return jnp.stack([real_part, imag_part], axis=2).astype(jnp.bfloat16)


def local_tile(left_block, right_block, cosine_table, sine_table):
    rotated = rotate(right_block, cosine_table, sine_table)
    flat_left = left_block.reshape(left_block.shape[0], -1)
    flat_right = rotated.reshape(rotated.shape[0] * rotated.shape[1], -1)
    return lax.dot_general(
        flat_left, flat_right, (((1,), (1,)), ((), ())), preferred_element_type=jnp.float32
    )


def body(spectra, validity, pair_mask, owners):
    channels = spectra.shape[0]
    bins_dev = spectra.shape[3]
    pair_reach = pair_mask.shape[1]
    sub_count = pair_mask.shape[2]
    sub_size = channels // sub_count
    per_block = sub_count * sub_count
    chan_count = lax.axis_size("chan")
    chan_here = lax.axis_index("chan")
    freq_count = lax.axis_size("freq")
    freq_here = lax.axis_index("freq")
    first_bin = freq_here * bins_dev
    values = spectra.astype(jnp.float32)
    weights = validity.astype(jnp.float32)
    padded = extended(
        amplitude_sum(values, weights).astype(jnp.bfloat16), (("freq", 1),), HALF
    ).astype(jnp.float32)
    whitened = whiten(values, weights, padded, first_bin, bins_dev)
    nearby = {0: (whitened, validity)}
    forward_block = nearby[0]
    for hop_index in range(1, pair_reach + 1):
        forward_block = shifted((forward_block[0], shortened(forward_block[1])), "chan", -1)
        nearby[hop_index] = forward_block
    layout = [(0, distance) for distance in range(1, pair_reach + 1)]
    cosine_table, sine_table = lag_tables(first_bin, bins_dev)
    tile_list = []
    joint_list = []
    listed_list = []
    block_list = []
    for distance in range(1, pair_reach + 1):
        left_pos, right_pos = layout[distance - 1]
        left_white, left_valid = nearby[left_pos]
        right_white, right_valid = nearby[right_pos]
        block_id = (chan_here + left_pos) % chan_count
        listed = lax.dynamic_index_in_dim(pair_mask, block_id, 0, keepdims=False)[
            distance - 1
        ].reshape(-1)
        pair_tile = lax.cond(
            jnp.sum(listed) > 0,
            lambda: local_tile(left_white, right_white, cosine_table, sine_table),
            lambda: jnp.zeros((channels, LAGS * channels), jnp.float32),
        )
        joint_count = jnp.dot(
            left_valid.astype(jnp.float32),
            right_valid.astype(jnp.float32).T,
            precision=lax.Precision.HIGHEST,
        )
        tile_list.append(pair_tile)
        joint_list.append(joint_count)
        listed_list.append(listed)
        block_list.append(block_id)
    band_term = jnp.stack(tile_list).reshape(pair_reach, sub_count, sub_size, LAGS * channels)
    summed = lax.psum_scatter(
        band_term.astype(jnp.bfloat16), "freq", scatter_dimension=2, tiled=True
    ).astype(jnp.float32)
    row_share = sub_size // freq_count
    joint_all = jnp.stack(joint_list).reshape(pair_reach, sub_count, sub_size, channels)
    joint_rows = lax.dynamic_slice_in_dim(joint_all, freq_here * row_share, row_share, 2)
    scaling = 1.0 / jnp.sqrt(jnp.maximum(joint_rows, 1.0) * FREQS)
    correlated = (
        summed.reshape(pair_reach, sub_count, row_share, LAGS, channels) * scaling[:, :, :, None, :]
    ).astype(jnp.bfloat16)
    pieces = correlated.reshape(
        pair_reach, sub_count, row_share, LAGS, sub_count, sub_size
    ).transpose(0, 1, 4, 2, 3, 5)
    pieces = pieces.reshape(pair_reach, per_block, row_share * LAGS * sub_size)
    slot_caps = (owners.shape[1] + chan_count - 1) // chan_count
    dest_rows = chan_count * slot_caps
    buffers = []
    for distance in range(1, pair_reach + 1):
        owner_row = lax.dynamic_index_in_dim(owners, block_list[distance - 1], 0, keepdims=False)
        owner_row = owner_row[(distance - 1) * per_block : distance * per_block]
        slot_index = (
            jnp.arange(per_block, dtype=jnp.int32) + (distance - 1) * per_block
        ) % slot_caps
        target = owner_row * slot_caps + slot_index
        select = (jnp.arange(dest_rows, dtype=jnp.int32)[:, None] == target[None, :]) & (
            listed_list[distance - 1][None, :] > 0
        )
        buffers.append(
            jnp.dot(
                select.astype(jnp.bfloat16),
                pieces[distance - 1],
                preferred_element_type=jnp.float32,
            )
        )
    outgoing = sum(buffers).reshape(chan_count, slot_caps, -1).astype(jnp.bfloat16)
    received = lax.all_to_all(outgoing, "chan", split_axis=0, concat_axis=0, tiled=True)
    return received.reshape(1, chan_count, slot_caps, row_share, LAGS * sub_size)


def solution(mesh):
    return jax.shard_map(
        body,
        mesh=mesh,
        in_specs=(P("chan", None, None, "freq"), P("chan", None), P(), P()),
        out_specs=P("chan", None, None, "freq", None),
        check_vma=False,
    )
```

profile of v0, /device:TPU:17, one launch (start us, length us, event | category | flops | bytes accessed | tf_op | source)
XLA Modules:
  0.0 172.0 jit_solution(6085144950897979123)
XLA Ops:
  7.4 1.5 convert_element_type.80
  9.0 1.7 fusion.10
  10.8 6.0 %collective-permute-start = (bf16[320,32]{1,0:T(8,128)(2,1)S(1)}, bf16[320,32]{1,0:T(8,128)(2,1)S(1)}, u32[]{:S(2)}, u32[]{:S(2)}) collective-permute-start(bf16[320,32]{1,0:T(8,128)(2,1)S(1)} %get-tuple-element.53), channel_id=1, source_target_pairs={{0,1},{1,2},{2,3},{3,4},{4,5},{5,6},{6,7},{8,9},{9,10},{10,11},{11... | collective-permute-start | bytes 61448 | tf_op jit(solution)/shard_map/ppermute | solution.py:22
  16.8 1.9 %collective-permute-start.1 = (bf16[320,32]{1,0:T(8,128)(2,1)S(1)}, bf16[320,32]{1,0:T(8,128)(2,1)S(1)}, u32[]{:S(2)}, u32[]{:S(2)}) collective-permute-start(bf16[320,32]{1,0:T(8,128)(2,1)S(1)} %get-tuple-element.54), channel_id=1, source_target_pairs={{1,0},{2,1},{3,2},{4,3},{5,4},{6,5},{7,6},{9,8},{10,9},{11,10},{12... | collective-permute-start | bytes 61448 | tf_op jit(solution)/shard_map/ppermute | solution.py:25
  18.8 6.7 %collective-permute-done.1 = bf16[320,32]{1,0:T(8,128)(2,1)S(1)} collective-permute-done((bf16[320,32]{1,0:T(8,128)(2,1)S(1)}, bf16[320,32]{1,0:T(8,128)(2,1)S(1)}, u32[]{:S(2)}, u32[]{:S(2)}) %collective-permute-start.1) | collective-permute-done | bytes 20512 | tf_op jit(solution)/shard_map/ppermute | solution.py:25
  27.5 0.9 fusion.2
  28.4 12.9 %collective-permute-start.2 = (bf16[320,2,2,256]{3,2,1,0:T(2,128)(2,1)S(1)}, bf16[320,2,2,256]{3,2,1,0:T(2,128)(2,1)}, u32[]{:S(2)}, u32[]{:S(2)}) collective-permute-start(bf16[320,2,2,256]{3,2,1,0:T(2,128)(2,1)S(1)} %fusion.2), channel_id=1, source_target_pairs={{8,0},{16,8},{24,16},{32,24},{40,32},{48,40},{56,48},{64,56},{72,6... | collective-permute-start | bytes 1966088 | tf_op jit(solution)/shard_map/ppermute | solution.py:37
  41.3 10.5 %collective-permute-done.2 = bf16[320,2,2,256]{3,2,1,0:T(2,128)(2,1)} collective-permute-done((bf16[320,2,2,256]{3,2,1,0:T(2,128)(2,1)S(1)}, bf16[320,2,2,256]{3,2,1,0:T(2,128)(2,1)}, u32[]{:S(2)}, u32[]{:S(2)}) %collective-permute-start.2) | collective-permute-done | bytes 655392 | tf_op jit(solution)/shard_map/ppermute | solution.py:37
  51.7 8.1 %collective-permute-start.3 = (bf16[320,2,2,256]{3,2,1,0:T(2,128)(2,1)}, bf16[320,2,2,256]{3,2,1,0:T(2,128)(2,1)}, u32[]{:S(2)}, u32[]{:S(2)}) collective-permute-start(bf16[320,2,2,256]{3,2,1,0:T(2,128)(2,1)} %collective-permute-done.2), channel_id=1, source_target_pairs={{8,0},{16,8},{24,16},{32,24},{40,32},{48,40},{56,48},{64,56},{72,6... | collective-permute-start | bytes 1966088 | tf_op jit(solution)/shard_map/ppermute | solution.py:37
  62.1 15.2 %conditional.2 = (bf16[1,5,64,1280]{3,2,1,0:T(8,128)(2,1)S(1)}) conditional(s32[]{:T(128)} %convert_element_type.79, () %tuple.21, (bf16[320,2,2,256]{3,2,1,0:T(2,128)(2,1)}, f32[4,256]{1,0:T(4,128)S(1)}, f32[4,256]{1,0:T(4,128)S(1)}, bf16[320,2,2,256]{3,2,1,0:T(2,128)(2,1)S(1)}) %tuple.22), branch_computations={%region_5.6_spmd, %region_6.7_spmd} | conditional | flops 845742080 | bytes 24420360 | solution.py:126
  62.3 1.5 convert_element_type.62
  64.3 2.8 %add_convert_fusion = (bf16[4,320,1,2,256]{4,3,2,1,0:T(2,128)(2,1)S(1)}, bf16[4,320,1,2,256]{4,3,2,1,0:T(2,128)(2,1)S(1)}) fusion(f32[4,256]{1,0:T(4,128)S(1)} %get-tuple-element.31, f32[320,2,256]{2,1,0:T(2,128)S(1)} %get-tuple-element.46, f32[4,256]{1,0:T(4,128)S(1)} %get-tuple-element.30, f32[320,2,256]{2,1,0:T(2,128)S(1)} %get-tuple-element.45), kind=kLoop, calls=%fused_computation.2 | loop fusion | flops 5242880 | bytes 3940352 | tf_op jit(solution)/shard_map/convert
  67.1 3.4 %pad_maximum_fusion = bf16[4,320,2,2,256]{4,3,2,1,0:T(2,128)(2,1)S(1)} fusion(bf16[4,320,1,2,256]{4,3,2,1,0:T(2,128)(2,1)S(1)} %get-tuple-element.44, bf16[4,320,1,2,256]{4,3,2,1,0:T(2,128)(2,1)S(1)} %get-tuple-element.43), kind=kLoop, calls=%fused_computation | loop fusion | flops 1310720 | bytes 5242880 | tf_op jit(solution)/shard_map/cond/branch_1_fun/stack | solution.py:77
  70.5 3.5 %convert_element_type.63 = bf16[1280,1024]{1,0:T(8,128)(2,1)} reshape(bf16[4,320,2,2,256]{4,3,2,1,0:T(2,128)(2,1)S(1)} %pad_maximum_fusion) | data formatting | bytes 5242880 | tf_op jit(solution)/shard_map/cond/branch_1_fun/convert_element_type | solution.py:77
  74.5 2.8 %fusion.46 = bf16[1280,320]{0,1:T(8,128)(2,1)S(1)} fusion(bf16[1280,1024]{1,0:T(8,128)(2,1)} %convert_element_type.63, bf16[320,1024]{1,0:T(8,128)(2,1)S(1)} %reshape.163), kind=kOutput, calls=%fused_computation.86 | convolution fusion | flops 838860800 | bytes 4096000 | tf_op jit(solution)/shard_map/cond/branch_1_fun/dot_general | solution.py:84
  78.5 1.3 pad_maximum_fusion.2
  80.7 3.5 %reshape.178 = bf16[64,12800]{1,0:T(8,128)(2,1)} reshape(bf16[64,2,5,1280]{3,2,1,0:T(8,128)(2,1)S(1)} %bitcast.51) | data formatting | bytes 3276800
  84.2 16.6 %collective-permute-start.4 = (s32[320,2]{0,1:T(2,128)S(1)}, s32[320,2]{0,1:T(2,128)S(1)}, u32[]{:S(2)}, u32[]{:S(2)}) collective-permute-start(s32[320,2]{0,1:T(2,128)S(1)} %copy-done.3), channel_id=1, source_target_pairs={{8,0},{16,8},{24,16},{32,24},{40,32},{48,40},{56,48},{64,56},{72,6... | collective-permute-start | bytes 7688 | tf_op jit(solution)/shard_map/ppermute | solution.py:37
  100.9 1.1 compare_reduce_fusion
  102.3 7.4 %collective-permute-start.5 = (s32[320,2]{0,1:T(2,128)S(1)}, s32[320,2]{0,1:T(2,128)S(1)}, u32[]{:S(2)}, u32[]{:S(2)}) collective-permute-start(s32[320,2]{0,1:T(2,128)S(1)} %collective-permute-done.4), channel_id=1, source_target_pairs={{8,0},{16,8},{24,16},{32,24},{40,32},{48,40},{56,48},{64,56},{72,6... | collective-permute-start | bytes 7688 | tf_op jit(solution)/shard_map/ppermute | solution.py:37
  111.3 25.1 %reduce-scatter.4.cloned.1.call-done = bf16[8,12800]{1,0:T(8,128)(2,1)} async-done(((bf16[64,12800]{1,0:T(8,128)(2,1)}), bf16[8,12800]{1,0:T(8,128)(2,1)}) %reduce-scatter.4.cloned.1.call-update) | async-done | bytes 204816
  136.4 1.3 reshape.179
  141.0 21.6 %all_to_all.5 = bf16[64,2,1024]{2,1,0:T(2,128)(2,1)S(1)} all-to-all(bf16[64,2,1024]{2,1,0:T(2,128)(2,1)S(1)} %reshape.186), channel_id=1, replica_groups=mesh['chan'=64,'freq'=8] {'chan'}, dimensions={0} | all-to-all | bytes 524288 | tf_op jit(solution)/shard_map/all_to_all | solution.py:176
  162.8 1.5 reduce.6
  (62 shorter events, 13.1 us)
Async XLA Ops:
  6.5 12.2 %copy-start.3 = (s32[320,2]{0,1:T(2,128)S(1)}, s32[320,2]{0,1:T(2,128)}, u32[]{:S(2)}) copy-start(s32[320,2]{0,1:T(2,128)} %param.9) | copy-start | bytes 7684
  6.5 129.9 %reduce-scatter.4.cloned.1.call-start = ((), (), s32[]{:S(2)}) async-start(), calls=%async_computation.2 | async-start | bytes 1843200
  10.8 8.0 %collective-permute-start = (bf16[320,32]{1,0:T(8,128)(2,1)S(1)}, bf16[320,32]{1,0:T(8,128)(2,1)S(1)}, u32[]{:S(2)}, u32[]{:S(2)}) collective-permute-start(bf16[320,32]{1,0:T(8,128)(2,1)S(1)} %get-tuple-element.53), channel_id=1, source_target_pairs={{0,1},{1,2},{2,3},{3,4},{4,5},{5,6},{6,7},{8,9},{9,10},{10,11},{11... | collective-permute-start | bytes 61448 | tf_op jit(solution)/shard_map/ppermute | solution.py:22
  16.8 8.7 %collective-permute-start.1 = (bf16[320,32]{1,0:T(8,128)(2,1)S(1)}, bf16[320,32]{1,0:T(8,128)(2,1)S(1)}, u32[]{:S(2)}, u32[]{:S(2)}) collective-permute-start(bf16[320,32]{1,0:T(8,128)(2,1)S(1)} %get-tuple-element.54), channel_id=1, source_target_pairs={{1,0},{2,1},{3,2},{4,3},{5,4},{6,5},{7,6},{9,8},{10,9},{11,10},{12... | collective-permute-start | bytes 61448 | tf_op jit(solution)/shard_map/ppermute | solution.py:25
  26.4 1.1 copy-start.1
  26.6 33.3 %copy-start.2 = (s32[64,2,5,5]{0,1,3,2:T(2,128)S(1)}, s32[64,2,5,5]{0,1,3,2:T(2,128)}, u32[]{:S(2)}) copy-start(s32[64,2,5,5]{0,1,3,2:T(2,128)} %param.10) | copy-start | bytes 38404
  28.4 23.3 %collective-permute-start.2 = (bf16[320,2,2,256]{3,2,1,0:T(2,128)(2,1)S(1)}, bf16[320,2,2,256]{3,2,1,0:T(2,128)(2,1)}, u32[]{:S(2)}, u32[]{:S(2)}) collective-permute-start(bf16[320,2,2,256]{3,2,1,0:T(2,128)(2,1)S(1)} %fusion.2), channel_id=1, source_target_pairs={{8,0},{16,8},{24,16},{32,24},{40,32},{48,40},{56,48},{64,56},{72,6... | collective-permute-start | bytes 1966088 | tf_op jit(solution)/shard_map/ppermute | solution.py:37
  51.7 25.6 %collective-permute-start.3 = (bf16[320,2,2,256]{3,2,1,0:T(2,128)(2,1)}, bf16[320,2,2,256]{3,2,1,0:T(2,128)(2,1)}, u32[]{:S(2)}, u32[]{:S(2)}) collective-permute-start(bf16[320,2,2,256]{3,2,1,0:T(2,128)(2,1)} %collective-permute-done.2), channel_id=1, source_target_pairs={{8,0},{16,8},{24,16},{32,24},{40,32},{48,40},{56,48},{64,56},{72,6... | collective-permute-start | bytes 1966088 | tf_op jit(solution)/shard_map/ppermute | solution.py:37
  77.3 0.9 copy-start
  80.7 21.4 %copy-start.4 = (s32[64,50]{0,1:T(8,128)S(1)}, s32[64,50]{0,1:T(8,128)}, u32[]{:S(2)}) copy-start(s32[64,50]{0,1:T(8,128)} %param.11) | copy-start | bytes 38404
  84.2 18.0 %collective-permute-start.4 = (s32[320,2]{0,1:T(2,128)S(1)}, s32[320,2]{0,1:T(2,128)S(1)}, u32[]{:S(2)}, u32[]{:S(2)}) collective-permute-start(s32[320,2]{0,1:T(2,128)S(1)} %copy-done.3), channel_id=1, source_target_pairs={{8,0},{16,8},{24,16},{32,24},{40,32},{48,40},{56,48},{64,56},{72,6... | collective-permute-start | bytes 7688 | tf_op jit(solution)/shard_map/ppermute | solution.py:37
  102.3 8.1 %collective-permute-start.5 = (s32[320,2]{0,1:T(2,128)S(1)}, s32[320,2]{0,1:T(2,128)S(1)}, u32[]{:S(2)}, u32[]{:S(2)}) collective-permute-start(s32[320,2]{0,1:T(2,128)S(1)} %collective-permute-done.4), channel_id=1, source_target_pairs={{8,0},{16,8},{24,16},{32,24},{40,32},{48,40},{56,48},{64,56},{72,6... | collective-permute-start | bytes 7688 | tf_op jit(solution)/shard_map/ppermute | solution.py:37
Sparse Core Ops, SparseCore 0:
  84.4 51.9 reduce-scatter.3
where the time goes:
time: 173 us; the launch traced here: 172 us
  starting transfers between devices  52.9 us (31%)
  waiting for transfers between devices  42.4 us (25%)
  blocking collectives  21.6 us (12%)
  other arithmetic  19.4 us (11%)
  local copies, waits for them, and re-layouts  15.5 us (9%)
  between operations  15.1 us (9%)
  matrix products  4.67 us (3%)
    ppermute x4, starting transfers between devices, shifted(): return lax.ppermute(block, axis, route)  45 us
    unnamed x2, waiting for transfers between devices  25.1 us
    all_to_all x1, blocking collectives, body(): lax.all_to_all(outgoing, 'chan', split_axis=0, concat_axis=0, tiled=True)  21.6 us
    ppermute x4, waiting for transfers between devices, shifted(): return lax.ppermute(block, axis, route)  10.5 us
    unnamed x16, local copies, waits for them, and re-layouts  8.27 us
    ppermute x1, waiting for transfers between devices, extended(): lax.ppermute(lax.slice_in_dim(block, 0, width, axis=dim), axis, backward)  6.74 us
    ppermute x1, starting transfers between devices, extended(): lax.ppermute(lax.slice_in_dim(block, block.shape[dim] - width, None, axis...  5.99 us
    another operation x5, other arithmetic  3.55 us
  transfers between devices with their start and end apart: 7, of which 3 were waited for; matrix products, arithmetic and copies ran while one was open for 11% of the time, Pallas kernels for 0%

commit v1 on v0

v1 whole, which is shorter than its diff:
```python
import functools

import jax
import jax.numpy as jnp
import numpy as np
from jax import lax
from jax.experimental import pallas as pl
from jax.experimental.pallas import tpu as pltpu
from jax.sharding import PartitionSpec as P

FREQS = 2048
LAGS = 4
LAG_STEP = 25
HALF = 32
EPS = 1e-06

SUB = 5
SB = 64
CH = 320
BAND = 256
PARTS = 4
REACH = 2
N_FREQ = 8
BLOCKS = 64
SHARE = SB // N_FREQ
ROWS = REACH * SUB * SHARE
COLS = SUB * LAGS * SB
VALID_LANE = 2 * HALF
MIB = 1 << 20

VMEM = pl.BlockSpec(memory_space=pltpu.VMEM)
SMEM = pl.BlockSpec(memory_space=pltpu.SMEM)


def bin_tables():
    bins = np.arange(FREQS)
    lags = (np.arange(LAGS) - LAGS // 2) * LAG_STEP
    angle = np.pi * ((lags[:, None] * bins[None, :]) % (2 * FREQS)) / FREQS
    count = np.minimum(bins + HALF, FREQS - 1) - np.maximum(bins - HALF, 0) + 1
    rows = np.concatenate([np.cos(angle), np.sin(angle), np.tile(count, (8, 1))])
    return np.ascontiguousarray(
        rows.reshape(16, N_FREQ, BAND).transpose(1, 0, 2).astype(np.float32)
    )


def window_tables():
    out_bin = np.arange(BAND)[None, :]
    inner = np.abs(np.arange(BAND)[:, None] - out_bin) <= HALF
    low = np.abs(np.arange(-HALF, 0)[:, None] - out_bin) <= HALF
    high = np.abs(np.arange(BAND, BAND + HALF)[:, None] - out_bin) <= HALF
    message = np.zeros((128, 3 * BAND))
    message[:HALF, :BAND] = low
    message[HALF : 2 * HALF, :BAND] = high
    message[VALID_LANE, BAND : 2 * BAND] = 1
    message[VALID_LANE + 1, 2 * BAND :] = 1
    return inner.astype(jnp.bfloat16), message.astype(jnp.bfloat16)


def part(ref, rows, index):
    return ref[rows, index * BAND : (index + 1) * BAND].astype(jnp.float32)


def amplitude(ref, rows, weight_one, weight_two):
    first = jnp.sqrt(part(ref, rows, 0) ** 2 + part(ref, rows, 2) ** 2)
    second = jnp.sqrt(part(ref, rows, 1) ** 2 + part(ref, rows, 3) ** 2)
    return first * weight_one + second * weight_two


def edges_kernel(raw, valid, low, high):
    for start in range(0, CH, SB):
        rows = slice(start, start + SB)
        weight = valid[rows, :].astype(jnp.float32)
        level = amplitude(raw, rows, weight[:, 0:1], weight[:, 1:2]).astype(jnp.bfloat16)
        low[rows, :] = level[:, :HALF]
        high[rows, :] = level[:, BAND - HALF :]


def tiles_kernel(
    odd, here, before, after, note_here, note_before, note_after, table, inner, spread,
    mine, theirs, level, gains, left, right,
):
    def prepare(raw, note):
        wide = jnp.dot(note[...], spread[...], preferred_element_type=jnp.float32)
        gains[...] = wide
        for start in range(0, CH, SB):
            rows = slice(start, start + SB)
            level[rows, :] = amplitude(
                raw, rows, gains[rows, BAND : 2 * BAND], gains[rows, 2 * BAND :]
            ).astype(jnp.bfloat16)
        gains[:, :BAND] += jnp.dot(
            level[...], inner[...], preferred_element_type=jnp.float32
        )

    def whitened(raw, rows):
        one, two = gains[rows, BAND : 2 * BAND], gains[rows, 2 * BAND :]
        mean = gains[rows, :BAND] / (table[8:9, :] * jnp.maximum(one + two, 1.0))
        scale = 1.0 / (mean + EPS)
        one, two = one * scale, two * scale
        return [part(raw, rows, i) * (two if i % 2 else one) for i in range(PARTS)]

    prepare(after, note_after)
    for u in range(SUB):
        rows = slice(u * SB, (u + 1) * SB)
        white = [x.astype(jnp.bfloat16) for x in whitened(after, rows)]
        for lag in range(LAGS):
            dest = slice(u * LAGS * SB + lag * SB, u * LAGS * SB + (lag + 1) * SB)
            for s in range(2):
                real, imag = white[s], white[2 + s]
                if lag != LAGS // 2:
                    cosine, sine = table[lag : lag + 1, :], table[4 + lag : 5 + lag, :]
                    real, imag = real.astype(jnp.float32), imag.astype(jnp.float32)
                    real, imag = (
                        (real * cosine + imag * sine).astype(jnp.bfloat16),
                        (imag * cosine - real * sine).astype(jnp.bfloat16),
                    )
                right[dest, s * BAND : (s + 1) * BAND] = real
                right[dest, (2 + s) * BAND : (3 + s) * BAND] = imag

    for d, (raw, note) in enumerate(((here, note_here), (before, note_before))):
        prepare(raw, note)
        for u in range(SUB):
            white = whitened(raw, slice(u * SB, (u + 1) * SB))
            for target in range(N_FREQ):
                half = lax.rem(odd[0] + target, 2)
                row = half * (ROWS * N_FREQ // 2) + (target // 2) * ROWS + (d * SUB + u) * SHARE
                row = pl.multiple_of(row, SHARE)
                for i in range(PARTS):
                    left[pl.ds(row, SHARE), i * BAND : (i + 1) * BAND] = white[i][
                        target * SHARE : (target + 1) * SHARE
                    ]

    half_rows = ROWS * N_FREQ // 2
    for out, start in ((theirs, half_rows), (mine, 0)):
        product = lax.dot_general(
            left[start : start + half_rows, :].astype(jnp.bfloat16),
            right[...],
            (((1,), (1,)), ((), ())),
            preferred_element_type=jnp.float32,
        )
        out[...] = product.astype(jnp.bfloat16)


def dispatch_kernel(
    spot, owner, listed, parts, note_here, note_before, note_after, outgoing, right, total
):
    freq = spot[0]
    lane = lax.broadcasted_iota(jnp.int32, (1, 128), 1)
    is_valid = ((lane == VALID_LANE) | (lane == VALID_LANE + 1)).astype(jnp.float32)
    outgoing[...] = jnp.zeros_like(outgoing)
    for u in range(SUB):
        chunk = note_after[u * SB : (u + 1) * SB, :]
        for lag in range(LAGS):
            right[(u * LAGS + lag) * SB : (u * LAGS + lag + 1) * SB, :] = chunk
    for d, note in enumerate((note_here, note_before)):
        wide = note[...].astype(jnp.float32) * is_valid
        picked = []
        for u in range(SUB):
            share = wide[u * SB : u * SB + SHARE]
            for target in range(1, N_FREQ):
                rows = slice(u * SB + target * SHARE, u * SB + (target + 1) * SHARE)
                share = jnp.where(freq == target, wide[rows], share)
            picked.append(share)
        joint = lax.dot_general(
            jnp.concatenate(picked).astype(jnp.bfloat16),
            right[...],
            (((1,), (1,)), ((), ())),
            preferred_element_type=jnp.float32,
        )
        scaling = 1.0 / jnp.sqrt(jnp.maximum(joint, 1.0) * FREQS)
        half = slice(d * SUB * SHARE, (d + 1) * SUB * SHARE)
        cross = parts[0, half, :].astype(jnp.float32)
        for i in range(1, N_FREQ // 2):
            cross += parts[i, half, :].astype(jnp.float32)
        total[half, :] = cross * scaling
    for d in range(REACH):
        for u in range(SUB):
            for v in range(SUB):
                slot = (d * SUB + u) * SUB + v

                @pl.when(listed[slot] > 0)
                def _():
                    outgoing[owner[slot], d] = total[
                        (d * SUB + u) * SHARE : (d * SUB + u + 1) * SHARE,
                        v * LAGS * SB : (v + 1) * LAGS * SB,
                    ].astype(jnp.bfloat16)


def merge_kernel(received, out):
    for b in range(BLOCKS):
        out[b] = received[b, 0] + received[(b + 1) % BLOCKS, 1]


def ring(x, axis, step):
    count = lax.axis_size(axis)
    return lax.ppermute(x, axis, [(i, (i + step) % count) for i in range(count)])


def line(x, axis, step):
    count = lax.axis_size(axis)
    return lax.ppermute(
        x, axis, [(i, i + step) for i in range(count) if 0 <= i + step < count]
    )


def bf16(*shape):
    return jax.ShapeDtypeStruct(shape, jnp.bfloat16)


def params(mib):
    return pltpu.CompilerParams(vmem_limit_bytes=mib * MIB)


def body(spectra, validity, pair_mask, owners):
    chan, freq = lax.axis_index("chan"), lax.axis_index("freq")
    raw = spectra.reshape(CH, PARTS * BAND)
    raw_before = ring(raw, "chan", 1)
    raw_after = ring(raw, "chan", -1)

    low_edge, high_edge = pl.pallas_call(
        edges_kernel,
        out_shape=(bf16(CH, HALF), bf16(CH, HALF)),
        in_specs=[VMEM, VMEM],
        out_specs=(VMEM, VMEM),
        compiler_params=params(16),
        name="edges",
    )(raw, validity)
    low = line(high_edge, "freq", 1)
    high = line(low_edge, "freq", -1)
    note = jnp.concatenate(
        [low, high, validity.astype(jnp.bfloat16), jnp.zeros((CH, 62), jnp.bfloat16)], axis=1
    )
    note_before = ring(note, "chan", 1)
    note_after = ring(note, "chan", -1)

    table = lax.dynamic_index_in_dim(jnp.asarray(bin_tables()), freq, 0, keepdims=False)
    inner, spread = (jnp.asarray(a) for a in window_tables())
    half = (N_FREQ // 2, ROWS, COLS)
    mine, theirs = pl.pallas_call(
        tiles_kernel,
        out_shape=(bf16(half[0] * ROWS, COLS), bf16(half[0] * ROWS, COLS)),
        in_specs=[SMEM] + [VMEM] * 9,
        out_specs=(VMEM, VMEM),
        scratch_shapes=[
            pltpu.VMEM((CH, BAND), jnp.bfloat16),
            pltpu.VMEM((CH, 3 * BAND), jnp.float32),
            pltpu.VMEM((ROWS * N_FREQ, PARTS * BAND), jnp.float32),
            pltpu.VMEM((COLS, PARTS * BAND), jnp.bfloat16),
        ],
        compiler_params=params(40),
        name="tiles",
    )((freq % 2)[None], raw, raw_before, raw_after, note, note_before, note_after, table, inner, spread)

    count = lax.axis_size("freq")
    other = lax.ppermute(theirs, "freq", [(k, k ^ 1) for k in range(count)])
    pair = (mine.astype(jnp.float32) + other.astype(jnp.float32)).astype(jnp.bfloat16)
    groups = [[k for k in range(count) if k % 2 == core] for core in range(2)]
    parts = lax.all_to_all(
        pair.reshape(half), "freq", 0, 0, tiled=True, axis_index_groups=groups
    )

    behind = (chan + BLOCKS - 1) % BLOCKS
    listed = jnp.concatenate(
        [pair_mask[chan, 0].reshape(-1), pair_mask[behind, 1].reshape(-1)]
    )
    owner = jnp.concatenate([owners[chan, : SUB * SUB], owners[behind, SUB * SUB :]])
    outgoing = pl.pallas_call(
        dispatch_kernel,
        out_shape=bf16(BLOCKS, REACH, SHARE, LAGS * SB),
        in_specs=[SMEM] * 3 + [VMEM] * 4,
        out_specs=VMEM,
        scratch_shapes=[
            pltpu.VMEM((COLS, 128), jnp.bfloat16),
            pltpu.VMEM((ROWS, COLS), jnp.float32),
        ],
        compiler_params=params(16),
        name="dispatch",
    )(freq[None], owner, listed, parts, note, note_before, note_after)
    received = lax.all_to_all(outgoing, "chan", 0, 0, tiled=True)
    merged = pl.pallas_call(
        merge_kernel,
        out_shape=bf16(BLOCKS, SHARE, LAGS * SB),
        in_specs=[VMEM],
        out_specs=VMEM,
        compiler_params=params(8),
        name="merge",
    )(received)
    return merged[None, :, None]


def solution(mesh):
    return jax.shard_map(
        body,
        mesh=mesh,
        in_specs=(P("chan", None, None, "freq"), P("chan", None), P(), P()),
        out_specs=P("chan", None, None, "freq", None),
        check_vma=False,
    )
```

time: 173 us -> 113 us (0.65)
  the two profiles are of different devices: /device:TPU:17 before, /device:TPU:8 now
where the time goes in v1:
time: 113 us; the launch traced here: 112 us
  starting transfers between devices  45.3 us (40%)
  blocking collectives  28.3 us (25%)
  waiting for transfers between devices  26.4 us (23%)
  Pallas kernels  6.14 us (5%)
  local copies, waits for them, and re-layouts  4.73 us (4%)
  other arithmetic  1.29 us (1%)
    all_to_all x1, blocking collectives, body(): received = lax.all_to_all(outgoing, 'chan', 0, 0, tiled=True)  28.3 us
    ppermute x4, starting transfers between devices, ring(): lax.ppermute(x, axis, [(i, (i + step) % count) for i in range(count)])  25.1 us
    all_to_all x1, waiting for transfers between devices, body(): lax.all_to_all(pair.reshape(half), 'freq', 0, 0, tiled=True, axis_index_g...  18.9 us
    ppermute x1, starting transfers between devices, body(): other = lax.ppermute(theirs, 'freq', [(k, k ^ 1) for k in range(count)])  11.6 us
    all_to_all x1, starting transfers between devices, body(): lax.all_to_all(pair.reshape(half), 'freq', 0, 0, tiled=True, axis_index_g...  5.85 us
    ppermute x2, waiting for transfers between devices, line(): lax.ppermute(x, axis, [(i, i + step) for i in range(count) if 0 <= i + st...  4.25 us
    pallas_call x1, Pallas kernels, body(): pl.pallas_call(tiles_kernel, out_shape=(bf16(half[0] * ROWS, COLS), bf16(...  3.6 us
    ppermute x2, starting transfers between devices, line(): lax.ppermute(x, axis, [(i, i + step) for i in range(count) if 0 <= i + st...  2.75 us
  transfers between devices with their start and end apart: 8, of which 4 were waited for; matrix products, arithmetic and copies ran while one was open for 2% of the time, Pallas kernels for 0%

profile of v1, /device:TPU:8, one launch (start us, length us, event | category | flops | bytes accessed | tf_op | source)
XLA Modules:
  0.0 112.4 jit_solution(3640126787339411119)
XLA Ops:
  0.0 2.2 %reshape.6.raw.here = bf16[320,1024]{1,0:T(8,128)(2,1)S(1)} reshape(bf16[320,2,2,256]{3,2,1,0:T(2,128)(2,1)} %param.7) | data formatting | bytes 1310720 | tf_op jit(solution)/shard_map/reshape | solution.py:215
  2.3 3.5 %collective-permute-start = (bf16[320,1024]{1,0:T(8,128)(2,1)S(1)}, bf16[320,1024]{1,0:T(8,128)(2,1)S(1)}, u32[]{:S(2)}, u32[]{:S(2)}) collective-permute-start(bf16[320,1024]{1,0:T(8,128)(2,1)S(1)} %reshape.6.raw.here), channel_id=1, source_target_pairs={{0,8},{8,16},{16,24},{24,32},{32,40},{40,48},{48,56},{56,64},{64,7... | collective-permute-start | bytes 1966088 | tf_op jit(solution)/shard_map/ppermute | solution.py:195
  5.8 11.6 %collective-permute-start.1 = (bf16[320,1024]{1,0:T(8,128)(2,1)S(1)}, bf16[320,1024]{1,0:T(8,128)(2,1)S(1)}, u32[]{:S(2)}, u32[]{:S(2)}) collective-permute-start(bf16[320,1024]{1,0:T(8,128)(2,1)S(1)} %reshape.6.raw.here), channel_id=1, source_target_pairs={{0,504},{8,0},{16,8},{24,16},{32,24},{40,32},{48,40},{56,48},{64,5... | collective-permute-start | bytes 1966088 | tf_op jit(solution)/shard_map/ppermute | solution.py:195
  17.4 0.1 copy.11.valid
  17.5 0.4 edges.1
  17.9 1.5 %collective-permute-start.2 = (bf16[320,32]{1,0:T(8,128)(2,1)S(1)}, bf16[320,32]{1,0:T(8,128)(2,1)S(1)}, u32[]{:S(2)}, u32[]{:S(2)}) collective-permute-start(bf16[320,32]{1,0:T(8,128)(2,1)S(1)} %get-tuple-element.9), channel_id=1, source_target_pairs={{0,1},{1,2},{2,3},{3,4},{4,5},{5,6},{6,7},{8,9},{9,10},{10,11},{11... | collective-permute-start | bytes 61448 | tf_op jit(solution)/shard_map/ppermute | solution.py:200
  19.4 1.3 %collective-permute-start.3 = (bf16[320,32]{1,0:T(8,128)(2,1)S(1)}, bf16[320,32]{1,0:T(8,128)(2,1)S(1)}, u32[]{:S(2)}, u32[]{:S(2)}) collective-permute-start(bf16[320,32]{1,0:T(8,128)(2,1)S(1)} %get-tuple-element.10), channel_id=1, source_target_pairs={{1,0},{2,1},{3,2},{4,3},{5,4},{6,5},{7,6},{9,8},{10,9},{11,10},{12... | collective-permute-start | bytes 61448 | tf_op jit(solution)/shard_map/ppermute | solution.py:200
  20.7 0.2 copy.12
  20.9 4.2 %collective-permute-done.3 = bf16[320,32]{1,0:T(8,128)(2,1)S(1)} collective-permute-done((bf16[320,32]{1,0:T(8,128)(2,1)S(1)}, bf16[320,32]{1,0:T(8,128)(2,1)S(1)}, u32[]{:S(2)}, u32[]{:S(2)}) %collective-permute-start.3) | collective-permute-done | bytes 20512 | tf_op jit(solution)/shard_map/ppermute | solution.py:200
  25.3 1.9 %collective-permute-start.4 = (bf16[320,128]{1,0:T(8,128)(2,1)S(1)}, bf16[320,128]{1,0:T(8,128)(2,1)S(1)}, u32[]{:S(2)}, u32[]{:S(2)}) collective-permute-start(bf16[320,128]{1,0:T(8,128)(2,1)S(1)} %maximum_maximum_fusion.note_here), channel_id=1, source_target_pairs={{0,8},{8,16},{16,24},{24,32},{32,40},{40,48},{48,56},{56,64},{64,7... | collective-permute-start | bytes 245768 | tf_op jit(solution)/shard_map/ppermute | solution.py:195
  27.2 8.1 %collective-permute-start.5 = (bf16[320,128]{1,0:T(8,128)(2,1)S(1)}, bf16[320,128]{1,0:T(8,128)(2,1)S(1)}, u32[]{:S(2)}, u32[]{:S(2)}) collective-permute-start(bf16[320,128]{1,0:T(8,128)(2,1)S(1)} %maximum_maximum_fusion.note_here), channel_id=1, source_target_pairs={{0,504},{8,0},{16,8},{24,16},{32,24},{40,32},{48,40},{56,48},{64,5... | collective-permute-start | bytes 245768 | tf_op jit(solution)/shard_map/ppermute | solution.py:195
  35.4 0.7 dynamic-slice_bitcast_fusion.table
  36.1 1.3 %collective-permute-done.5.note_after = bf16[320,128]{1,0:T(8,128)(2,1)S(1)} collective-permute-done((bf16[320,128]{1,0:T(8,128)(2,1)S(1)}, bf16[320,128]{1,0:T(8,128)(2,1)S(1)}, u32[]{:S(2)}, u32[]{:S(2)}) %collective-permute-start.5) | collective-permute-done | bytes 81952 | tf_op jit(solution)/shard_map/ppermute | solution.py:195
  37.5 3.6 %tiles.1 = (bf16[320,1280]{1,0:T(8,128)(2,1)S(1)}, bf16[320,1280]{1,0:T(8,128)(2,1)S(1)}) custom-call(s32[1]{0:T(128)} %bitcast.1.odd, bf16[320,1024]{1,0:T(8,128)(2,1)S(1)} %reshape.6.raw.here, bf16[320,1024]{1,0:T(8,128)(2,1)S(1)} %collective-permute-done.before, bf16[320,1024]{1,0:T(8,128)(2,1)S(1)} %collective-permute-done.1.after, ...), custom_call_target="tpu_custom_call" | custom-call | tf_op jit(solution)/shard_map/tiles/pallas_call | solution.py:238
  41.1 11.6 %collective-permute-start.6 = (bf16[320,1280]{1,0:T(8,128)(2,1)S(1)}, bf16[320,1280]{1,0:T(8,128)(2,1)S(1)}, u32[]{:S(2)}, u32[]{:S(2)}) collective-permute-start(bf16[320,1280]{1,0:T(8,128)(2,1)S(1)} %get-tuple-element.12), channel_id=1, source_target_pairs={{0,1},{1,0},{2,3},{3,2},{4,5},{5,4},{6,7},{7,6},{8,9},{9,8},{10,11... | collective-permute-start | bytes 2457608 | tf_op jit(solution)/shard_map/ppermute | solution.py:254
  52.6 1.9 %collective-permute-done.6 = bf16[320,1280]{1,0:T(8,128)(2,1)S(1)} collective-permute-done((bf16[320,1280]{1,0:T(8,128)(2,1)S(1)}, bf16[320,1280]{1,0:T(8,128)(2,1)S(1)}, u32[]{:S(2)}, u32[]{:S(2)}) %collective-permute-start.6) | collective-permute-done | bytes 819232 | tf_op jit(solution)/shard_map/ppermute | solution.py:254
  54.6 1.1 add_convert_fusion
  55.7 5.8 %all-to-all-start = ((bf16[4,80,1280]{2,1,0:T(8,128)(2,1)}), bf16[4,80,1280]{2,1,0:T(8,128)(2,1)S(1)}, u32[]{:S(2)}, u32[]{:S(2)}) async-start(bf16[4,80,1280]{2,1,0:T(8,128)(2,1)} %bitcast.3), calls=%async_computation | async-start | bytes 1638400 | tf_op jit(solution)/shard_map/all_to_all | solution.py:257
  61.5 1.0 dynamic-slice_reduce_fusion.3
  62.7 0.2 dynamic-slice_reduce_fusion.1
  63.0 18.9 %all-to-all-done.parts = bf16[4,80,1280]{2,1,0:T(8,128)(2,1)S(1)} async-done(((bf16[4,80,1280]{2,1,0:T(8,128)(2,1)}), bf16[4,80,1280]{2,1,0:T(8,128)(2,1)S(1)}, u32[]{:S(2)}, u32[]{:S(2)}) %all-to-all-start) | async-done | bytes 819232 | tf_op jit(solution)/shard_map/all_to_all | solution.py:257
  81.9 1.4 %dispatch.1 = bf16[64,2,8,256]{3,2,1,0:T(8,128)(2,1)S(1)} custom-call(s32[1]{0:T(128)} %bitcast.spot, s32[50]{0:T(128)S(1)} %get-tuple-element.17.owner, s32[50]{0:T(128)S(1)} %get-tuple-element.18.listed, bf16[4,80,1280]{2,1,0:T(8,128)(2,1)S(1)} %all-to-all-done.parts, bf16[320,128]{1,0:T(8,128)(2,1)S(1)} %maximum_maximum_fusion.note_here, ...), custom_call_target="tpu_custom_call" | custom-call | tf_op jit(solution)/shard_map/dispatch/pallas_call | solution.py:266
  83.3 28.3 %all_to_all.10.received = bf16[64,2,8,256]{3,2,1,0:T(8,128)(2,1)S(1)} all-to-all(bf16[64,2,8,256]{3,2,1,0:T(8,128)(2,1)S(1)} %dispatch.1), channel_id=1, replica_groups=mesh['chan'=64,'freq'=8] {'chan'}, dimensions={0} | all-to-all | bytes 1048576 | tf_op jit(solution)/shard_map/all_to_all | solution.py:278
  111.7 0.7 merge.1
  (21 shorter events, 0.5 us)
Async XLA Ops:
  0.0 17.4 %copy-start.4 = (s32[320,2]{0,1:T(2,128)S(1)}, s32[320,2]{0,1:T(2,128)}, u32[]{:S(2)}) copy-start(s32[320,2]{0,1:T(2,128)} %param.8) | copy-start | bytes 7684
  2.2 35.2 %copy-start = (bf16[128,768]{1,0:T(8,128)(2,1)S(1)}, bf16[128,768]{1,0:T(8,128)(2,1)}, u32[]{:S(2)}) copy-start(bf16[128,768]{1,0:T(8,128)(2,1)} %constant.53.clone.spread) | copy-start | bytes 589828
  2.3 35.2 %copy-start.1 = (bf16[256,256]{1,0:T(8,128)(2,1)S(1)}, bf16[256,256]{1,0:T(8,128)(2,1)}, u32[]{:S(2)}) copy-start(bf16[256,256]{1,0:T(8,128)(2,1)} %constant.52.clone.inner) | copy-start | bytes 393220
  2.3 35.2 %collective-permute-start = (bf16[320,1024]{1,0:T(8,128)(2,1)S(1)}, bf16[320,1024]{1,0:T(8,128)(2,1)S(1)}, u32[]{:S(2)}, u32[]{:S(2)}) collective-permute-start(bf16[320,1024]{1,0:T(8,128)(2,1)S(1)} %reshape.6.raw.here), channel_id=1, source_target_pairs={{0,8},{8,16},{16,24},{24,32},{32,40},{40,48},{48,56},{56,64},{64,7... | collective-permute-start | bytes 1966088 | tf_op jit(solution)/shard_map/ppermute | solution.py:195
  5.8 31.6 %collective-permute-start.1 = (bf16[320,1024]{1,0:T(8,128)(2,1)S(1)}, bf16[320,1024]{1,0:T(8,128)(2,1)S(1)}, u32[]{:S(2)}, u32[]{:S(2)}) collective-permute-start(bf16[320,1024]{1,0:T(8,128)(2,1)S(1)} %reshape.6.raw.here), channel_id=1, source_target_pairs={{0,504},{8,0},{16,8},{24,16},{32,24},{40,32},{48,40},{56,48},{64,5... | collective-permute-start | bytes 1966088 | tf_op jit(solution)/shard_map/ppermute | solution.py:195
  17.9 3.0 %collective-permute-start.2 = (bf16[320,32]{1,0:T(8,128)(2,1)S(1)}, bf16[320,32]{1,0:T(8,128)(2,1)S(1)}, u32[]{:S(2)}, u32[]{:S(2)}) collective-permute-start(bf16[320,32]{1,0:T(8,128)(2,1)S(1)} %get-tuple-element.9), channel_id=1, source_target_pairs={{0,1},{1,2},{2,3},{3,4},{4,5},{5,6},{6,7},{8,9},{9,10},{10,11},{11... | collective-permute-start | bytes 61448 | tf_op jit(solution)/shard_map/ppermute | solution.py:200
  19.4 5.8 %collective-permute-start.3 = (bf16[320,32]{1,0:T(8,128)(2,1)S(1)}, bf16[320,32]{1,0:T(8,128)(2,1)S(1)}, u32[]{:S(2)}, u32[]{:S(2)}) collective-permute-start(bf16[320,32]{1,0:T(8,128)(2,1)S(1)} %get-tuple-element.10), channel_id=1, source_target_pairs={{1,0},{2,1},{3,2},{4,3},{5,4},{6,5},{7,6},{9,8},{10,9},{11,10},{12... | collective-permute-start | bytes 61448 | tf_op jit(solution)/shard_map/ppermute | solution.py:200
  25.3 10.8 %collective-permute-start.4 = (bf16[320,128]{1,0:T(8,128)(2,1)S(1)}, bf16[320,128]{1,0:T(8,128)(2,1)S(1)}, u32[]{:S(2)}, u32[]{:S(2)}) collective-permute-start(bf16[320,128]{1,0:T(8,128)(2,1)S(1)} %maximum_maximum_fusion.note_here), channel_id=1, source_target_pairs={{0,8},{8,16},{16,24},{24,32},{32,40},{40,48},{48,56},{56,64},{64,7... | collective-permute-start | bytes 245768 | tf_op jit(solution)/shard_map/ppermute | solution.py:195
  27.2 10.2 %collective-permute-start.5 = (bf16[320,128]{1,0:T(8,128)(2,1)S(1)}, bf16[320,128]{1,0:T(8,128)(2,1)S(1)}, u32[]{:S(2)}, u32[]{:S(2)}) collective-permute-start(bf16[320,128]{1,0:T(8,128)(2,1)S(1)} %maximum_maximum_fusion.note_here), channel_id=1, source_target_pairs={{0,504},{8,0},{16,8},{24,16},{32,24},{40,32},{48,40},{56,48},{64,5... | collective-permute-start | bytes 245768 | tf_op jit(solution)/shard_map/ppermute | solution.py:195
  41.1 13.5 %collective-permute-start.6 = (bf16[320,1280]{1,0:T(8,128)(2,1)S(1)}, bf16[320,1280]{1,0:T(8,128)(2,1)S(1)}, u32[]{:S(2)}, u32[]{:S(2)}) collective-permute-start(bf16[320,1280]{1,0:T(8,128)(2,1)S(1)} %get-tuple-element.12), channel_id=1, source_target_pairs={{0,1},{1,0},{2,3},{3,2},{4,5},{5,4},{6,7},{7,6},{8,9},{9,8},{10,11... | collective-permute-start | bytes 2457608 | tf_op jit(solution)/shard_map/ppermute | solution.py:254
  55.6 5.9 %copy-start.3 = (s32[64,2,5,5]{0,1,3,2:T(2,128)S(1)}, s32[64,2,5,5]{0,1,3,2:T(2,128)}, u32[]{:S(2)}) copy-start(s32[64,2,5,5]{0,1,3,2:T(2,128)} %param.9) | copy-start | bytes 38404
  55.6 7.0 %copy-start.2 = (s32[64,50]{0,1:T(8,128)S(1)}, s32[64,50]{0,1:T(8,128)}, u32[]{:S(2)}) copy-start(s32[64,50]{0,1:T(8,128)} %param.10) | copy-start | bytes 38404
  55.7 26.2 %all-to-all-start = ((bf16[4,80,1280]{2,1,0:T(8,128)(2,1)}), bf16[4,80,1280]{2,1,0:T(8,128)(2,1)S(1)}, u32[]{:S(2)}, u32[]{:S(2)}) async-start(bf16[4,80,1280]{2,1,0:T(8,128)(2,1)} %bitcast.3), calls=%async_computation | async-start | bytes 1638400 | tf_op jit(solution)/shard_map/all_to_all | solution.py:257

commit v2 on v1

v2 whole, which is shorter than its diff:
```python
import jax
import jax.numpy as jnp
import numpy as np
from jax import lax
from jax.experimental import pallas as pl
from jax.experimental.pallas import tpu as pltpu
from jax.sharding import PartitionSpec as P

FREQS = 2048
LAGS = 4
LAG_STEP = 25
HALF = 32
EPS = 1e-06

SUB = 5
SB = 64
CH = 320
BAND = 256
PARTS = 4
REACH = 2
N_FREQ = 8
BLOCKS = 64
SHARE = SB // N_FREQ
ROWS = SUB * SHARE
CHIPS = N_FREQ // 2
HALF_ROWS = CHIPS * ROWS
COLS = SUB * LAGS * SB
MIB = 1 << 20

VMEM = pl.BlockSpec(memory_space=pltpu.VMEM)
SMEM = pl.BlockSpec(memory_space=pltpu.SMEM)


def bin_tables():
    bins = np.arange(FREQS)
    lags = (np.arange(LAGS) - LAGS // 2) * LAG_STEP
    angle = np.pi * ((lags[:, None] * bins[None, :]) % (2 * FREQS)) / FREQS
    count = np.minimum(bins + HALF, FREQS - 1) - np.maximum(bins - HALF, 0) + 1
    rows = np.concatenate([np.cos(angle), np.sin(angle), np.tile(count, (8, 1))])
    return np.ascontiguousarray(
        rows.reshape(16, N_FREQ, BAND).transpose(1, 0, 2).astype(np.float32)
    )


def window_tables():
    out_bin = np.arange(BAND)[None, :]
    ranges = (np.arange(BAND), np.arange(-HALF, 0), np.arange(BAND, BAND + HALF))
    return [(np.abs(r[:, None] - out_bin) <= HALF).astype(jnp.bfloat16) for r in ranges]


def part(ref, rows, index):
    return ref[rows, index * BAND : (index + 1) * BAND].astype(jnp.float32)


def amplitude(ref, rows, weight_one, weight_two):
    first = jnp.sqrt(part(ref, rows, 0) ** 2 + part(ref, rows, 2) ** 2)
    second = jnp.sqrt(part(ref, rows, 1) ** 2 + part(ref, rows, 3) ** 2)
    return first * weight_one + second * weight_two


def edges_kernel(raw, valid, low, high):
    for start in range(0, CH, SB):
        rows = slice(start, start + SB)
        weight = valid[rows, :].astype(jnp.float32)
        level = amplitude(raw, rows, weight[:, 0:1], weight[:, 1:2]).astype(jnp.bfloat16)
        low[rows, :] = level[:, :HALF]
        high[rows, :] = level[:, BAND - HALF :]


def whiten_kernel(raw, low, high, valid, table, inner, below, above, out, level, window):
    for start in range(0, CH, SB):
        rows = slice(start, start + SB)
        weight = valid[rows, :].astype(jnp.float32)
        level[rows, :] = amplitude(raw, rows, weight[:, 0:1], weight[:, 1:2]).astype(jnp.bfloat16)
    window[...] = (
        jnp.dot(level[...], inner[...], preferred_element_type=jnp.float32)
        + jnp.dot(low[...], below[...], preferred_element_type=jnp.float32)
        + jnp.dot(high[...], above[...], preferred_element_type=jnp.float32)
    )
    for start in range(0, CH, SB):
        rows = slice(start, start + SB)
        weight = valid[rows, :].astype(jnp.float32)
        one, two = weight[:, 0:1], weight[:, 1:2]
        mean = window[rows, :] / (table[8:9, :] * jnp.maximum(one + two, 1.0))
        scale = 1.0 / (mean + EPS)
        one, two = one * scale, two * scale
        for i in range(PARTS):
            white = part(raw, rows, i) * (two if i % 2 else one)
            out[rows, i * BAND : (i + 1) * BAND] = white.astype(jnp.bfloat16)


def rotate(white, table, out):
    for u in range(SUB):
        rows = slice(u * SB, (u + 1) * SB)
        for lag in range(LAGS):
            dest = slice((u * LAGS + lag) * SB, (u * LAGS + lag + 1) * SB)
            if lag == LAGS // 2:
                out[dest, :] = white[rows, :]
                continue
            cosine, sine = table[lag : lag + 1, :], table[4 + lag : 5 + lag, :]
            for s in range(2):
                real, imag = part(white, rows, s), part(white, rows, 2 + s)
                out[dest, s * BAND : (s + 1) * BAND] = (
                    real * cosine + imag * sine
                ).astype(jnp.bfloat16)
                out[dest, (2 + s) * BAND : (3 + s) * BAND] = (
                    imag * cosine - real * sine
                ).astype(jnp.bfloat16)


def rotate_kernel(white, table, out):
    rotate(white, table, out)


def place(out, odd, block):
    for u in range(SUB):
        wide = block[u * SB : (u + 1) * SB, :].astype(jnp.float32)
        for target in range(N_FREQ):
            half = lax.rem(odd + target, 2)
            row = half * HALF_ROWS + (target // 2) * ROWS + u * SHARE
            out[pl.ds(pl.multiple_of(row, SHARE), SHARE), :] = wide[
                target * SHARE : (target + 1) * SHARE
            ]


def product(left, right):
    return lax.dot_general(
        left, right, (((1,), (1,)), ((), ())), preferred_element_type=jnp.float32
    )


def tiles_kernel(odd, before, after, right_here, table, mine, theirs, left, right_after):
    place(left, odd[0], before)
    rotate(after, table, right_after)
    rows = left[...].astype(jnp.bfloat16)
    for d, right in enumerate((right_here, right_after)):
        tile = product(rows, right[...]).astype(jnp.bfloat16)
        mine[:, d * COLS : (d + 1) * COLS] = tile[:HALF_ROWS]
        theirs[:, d * COLS : (d + 1) * COLS] = tile[HALF_ROWS:]


def gains_kernel(odd, valid_before, valid_here, valid_after, out, left, right):
    place(left, odd[0], valid_before)
    for d, valid in enumerate((valid_here, valid_after)):
        for u in range(SUB):
            chunk = valid[u * SB : (u + 1) * SB, :].astype(jnp.float32)
            for lag in range(LAGS):
                right[(u * LAGS + lag) * SB : (u * LAGS + lag + 1) * SB, :] = chunk
        joint = product(left[:HALF_ROWS, :], right[...])
        out[:, d * COLS : (d + 1) * COLS] = 1.0 / jnp.sqrt(jnp.maximum(joint, 1.0) * FREQS)


def dispatch_kernel(place_of, listed, mine, other, gain, out, total):
    out[...] = jnp.zeros_like(out)
    total[...] = (mine[...].astype(jnp.float32) + other[...].astype(jnp.float32)) * gain[...]
    for slot in range(REACH * SUB * SUB):
        d, u, v = slot // (SUB * SUB), slot // SUB % SUB, slot % SUB

        @pl.when(listed[slot] > 0)
        def _():
            for chip in range(CHIPS):
                out[place_of[slot], chip] = total[
                    chip * ROWS + u * SHARE : chip * ROWS + (u + 1) * SHARE,
                    d * COLS + v * LAGS * SB : d * COLS + (v + 1) * LAGS * SB,
                ].astype(jnp.bfloat16)


def collect_kernel(received, out):
    def block(b, _):
        total = received[b, 0].astype(jnp.float32)
        for chip in range(1, CHIPS):
            total += received[b, chip].astype(jnp.float32)
        out[b] = total.astype(jnp.bfloat16)

    lax.fori_loop(0, BLOCKS, block, None, unroll=8)


def ring(x, axis, step):
    count = lax.axis_size(axis)
    return lax.ppermute(x, axis, [(i, (i + step) % count) for i in range(count)])


def line(x, axis, step):
    count = lax.axis_size(axis)
    return lax.ppermute(
        x, axis, [(i, i + step) for i in range(count) if 0 <= i + step < count]
    )


def bf16(*shape):
    return jax.ShapeDtypeStruct(shape, jnp.bfloat16)


def kernel(fn, out_shape, inputs, scratch=(), scalars=0, mib=8):
    return pl.pallas_call(
        fn,
        out_shape=out_shape,
        in_specs=[SMEM] * scalars + [VMEM] * (inputs - scalars),
        out_specs=jax.tree.map(lambda _: VMEM, out_shape),
        scratch_shapes=[pltpu.VMEM(shape, dtype) for shape, dtype in scratch],
        compiler_params=pltpu.CompilerParams(vmem_limit_bytes=mib * MIB),
        name=fn.__name__,
    )


def body(spectra, validity, pair_mask, owners):
    f32 = jnp.float32
    chan, freq = lax.axis_index("chan"), lax.axis_index("freq")
    odd = (freq % 2)[None]
    table = lax.dynamic_index_in_dim(jnp.asarray(bin_tables()), freq, 0, keepdims=False)
    inner, below, above = (jnp.asarray(a) for a in window_tables())

    raw = spectra.reshape(CH, PARTS * BAND)
    low_edge, high_edge = kernel(edges_kernel, (bf16(CH, HALF), bf16(CH, HALF)), 2)(raw, validity)
    low = line(high_edge, "freq", 1)
    high = line(low_edge, "freq", -1)
    white = kernel(
        whiten_kernel,
        bf16(CH, PARTS * BAND),
        8,
        [((CH, BAND), jnp.bfloat16), ((CH, BAND), f32)],
    )(raw, low, high, validity, table, inner, below, above)
    before = ring(white, "chan", 1)
    after = ring(white, "chan", -1)

    right_here = kernel(rotate_kernel, bf16(COLS, PARTS * BAND), 2)(white, table)
    valid, _ = lax.optimization_barrier((validity, right_here))
    valid_before = ring(valid, "chan", 1)
    valid_after = ring(valid, "chan", -1)
    before, after, valid_before, valid_after = lax.optimization_barrier(
        (before, after, valid_before, valid_after)
    )
    gain = kernel(
        gains_kernel,
        jax.ShapeDtypeStruct((HALF_ROWS, REACH * COLS), f32),
        4,
        [((2 * HALF_ROWS, 2), f32), ((COLS, 2), f32)],
        scalars=1,
    )(odd, valid_before, valid, valid_after)

    half = bf16(HALF_ROWS, REACH * COLS)
    mine, theirs = kernel(
        tiles_kernel,
        (half, half),
        5,
        [((2 * HALF_ROWS, PARTS * BAND), f32), ((COLS, PARTS * BAND), jnp.bfloat16)],
        scalars=1,
        mib=20,
    )(odd, before, after, right_here, table)
    other = lax.ppermute(theirs, "freq", [(k, k ^ 1) for k in range(N_FREQ)])

    block = (chan + BLOCKS - 1) % BLOCKS
    listed = pair_mask[block].reshape(-1)
    place_of = (owners[block] + BLOCKS - 1) % BLOCKS
    outgoing = kernel(
        dispatch_kernel,
        bf16(BLOCKS, CHIPS, SHARE, LAGS * SB),
        5,
        [((HALF_ROWS, REACH * COLS), f32)],
        scalars=2,
    )(place_of, listed, mine, other, gain)
    groups = [
        [
            (b + 1) % BLOCKS * N_FREQ + 2 * chip + core
            for b in range(BLOCKS)
            for chip in range(CHIPS)
        ]
        for core in range(2)
    ]
    received = lax.all_to_all(
        outgoing.reshape(BLOCKS * CHIPS, SHARE, LAGS * SB),
        ("chan", "freq"),
        0,
        0,
        tiled=True,
        axis_index_groups=groups,
    )
    merged = kernel(collect_kernel, bf16(BLOCKS, SHARE, LAGS * SB), 1)(
        received.reshape(BLOCKS, CHIPS, SHARE, LAGS * SB)
    )
    return merged[None, :, None]


def solution(mesh):
    return jax.shard_map(
        body,
        mesh=mesh,
        in_specs=(P("chan", None, None, "freq"), P("chan", None), P(), P()),
        out_specs=P("chan", None, None, "freq", None),
        check_vma=False,
    )
```

time: 113 us -> 113 us (level)
  blocking collectives: 28.3 us -> 46 us
  starting transfers between devices: 45.3 us -> 32.7 us
  waiting for transfers between devices: 26.4 us -> 14.7 us
  Pallas kernels: 6.14 us -> 9.94 us
  local copies, waits for them, and re-layouts: 4.73 us -> 8.19 us
    all_to_all x1 -> x0, waiting for transfers between devices: 18.9 us -> none  [body(): lax.all_to_all(pair.reshape(half), 'freq', 0, 0, tiled=True, axis_index_g...]
    all_to_all x1, blocking collectives: 28.3 us -> 46 us  [body(): lax.all_to_all(outgoing.reshape(BLOCKS * CHIPS, SHARE, LAGS * SB), ('chan...]
    ppermute x4, waiting for transfers between devices: 1.32 us -> 11.1 us  [ring(): lax.ppermute(x, axis, [(i, (i + step) % count) for i in range(count)])]
    ppermute x1, starting transfers between devices: 11.6 us -> 4.52 us  [body(): other = lax.ppermute(theirs, 'freq', [(k, k ^ 1) for k in range(N_FREQ)])]
    all_to_all x1 -> x0, starting transfers between devices: 5.85 us -> none  [body(): lax.all_to_all(pair.reshape(half), 'freq', 0, 0, tiled=True, axis_index_g...]
    unnamed x11 -> x17, local copies, waits for them, and re-layouts: 0.16 us -> 4.75 us
    pallas_call x4 -> x7, Pallas kernels: 6.14 us -> 9.94 us  [the longest x1 4.2 us: body(): kernel(tiles_kernel, (half, half), 5, [((2 * HALF_ROWS, PARTS * BAND), f3...]
    ppermute x1, waiting for transfers between devices: 1.94 us -> 0.01 us  [body(): other = lax.ppermute(theirs, 'freq', [(k, k ^ 1) for k in range(N_FREQ)])]
  transfers between devices with their start and end apart: 8 -> 7, of which waited for: 4 -> 3; matrix products, arithmetic and copies ran while one was open for 2% -> 1% of each run, Pallas kernels for 0% -> 2%
where the time goes in v2:
time: 113 us; the launch traced here: 112 us
  blocking collectives  46 us (41%)
  starting transfers between devices  32.7 us (29%)
  waiting for transfers between devices  14.7 us (13%)
  Pallas kernels  9.94 us (9%)
  local copies, waits for them, and re-layouts  8.19 us (7%)
    all_to_all x1, blocking collectives, body(): lax.all_to_all(outgoing.reshape(BLOCKS * CHIPS, SHARE, LAGS * SB), ('chan...  46 us
    ppermute x4, starting transfers between devices, ring(): lax.ppermute(x, axis, [(i, (i + step) % count) for i in range(count)])  25 us
    ppermute x4, waiting for transfers between devices, ring(): lax.ppermute(x, axis, [(i, (i + step) % count) for i in range(count)])  11.1 us
    unnamed x17, local copies, waits for them, and re-layouts  4.75 us
    ppermute x1, starting transfers between devices, body(): other = lax.ppermute(theirs, 'freq', [(k, k ^ 1) for k in range(N_FREQ)])  4.52 us
    pallas_call x1, Pallas kernels, body(): kernel(tiles_kernel, (half, half), 5, [((2 * HALF_ROWS, PARTS * BAND), f3...  4.2 us
    ppermute x2, waiting for transfers between devices, line(): lax.ppermute(x, axis, [(i, i + step) for i in range(count) if 0 <= i + st...  3.51 us
    ppermute x2, starting transfers between devices, line(): lax.ppermute(x, axis, [(i, i + step) for i in range(count) if 0 <= i + st...  3.16 us
  transfers between devices with their start and end apart: 7, of which 3 were waited for; matrix products, arithmetic and copies ran while one was open for 1% of the time, Pallas kernels for 2%

profile of v2, /device:TPU:8, one launch (start us, length us, event | category | flops | bytes accessed | tf_op | source)
XLA Modules:
  0.0 111.9 jit_solution(6669450476036459889)
XLA Ops:
  0.0 0.8 copy.17.valid
  0.8 2.2 %reshape.11.raw = bf16[320,1024]{1,0:T(8,128)(2,1)S(1)} reshape(bf16[320,2,2,256]{3,2,1,0:T(2,128)(2,1)} %param.8) | data formatting | bytes 1310720 | tf_op jit(solution)/shard_map/reshape | solution.py:213
  3.5 1.9 %collective-permute-start = (bf16[320,32]{1,0:T(8,128)(2,1)S(1)}, bf16[320,32]{1,0:T(8,128)(2,1)S(1)}, u32[]{:S(2)}, u32[]{:S(2)}) collective-permute-start(bf16[320,32]{1,0:T(8,128)(2,1)S(1)} %get-tuple-element.14), channel_id=1, source_target_pairs={{0,1},{1,2},{2,3},{3,4},{4,5},{5,6},{6,7},{8,9},{9,10},{10,11},{11... | collective-permute-start | bytes 61448 | tf_op jit(solution)/shard_map/ppermute | solution.py:185
  5.3 1.3 %collective-permute-start.1 = (bf16[320,32]{1,0:T(8,128)(2,1)S(1)}, bf16[320,32]{1,0:T(8,128)(2,1)S(1)}, u32[]{:S(2)}, u32[]{:S(2)}) collective-permute-start(bf16[320,32]{1,0:T(8,128)(2,1)S(1)} %get-tuple-element.15), channel_id=1, source_target_pairs={{1,0},{2,1},{3,2},{4,3},{5,4},{6,5},{7,6},{9,8},{10,9},{11,10},{12... | collective-permute-start | bytes 61448 | tf_op jit(solution)/shard_map/ppermute | solution.py:185
  6.6 0.7 dynamic-slice_bitcast_fusion.table
  7.4 3.5 %collective-permute-done.1.high = bf16[320,32]{1,0:T(8,128)(2,1)S(1)} collective-permute-done((bf16[320,32]{1,0:T(8,128)(2,1)S(1)}, bf16[320,32]{1,0:T(8,128)(2,1)S(1)}, u32[]{:S(2)}, u32[]{:S(2)}) %collective-permute-start.1) | collective-permute-done | bytes 20512 | tf_op jit(solution)/shard_map/ppermute | solution.py:185
  10.9 0.9 copy-done.3
  11.8 0.7 copy-done.4
  12.5 0.7 copy-done.5
  13.2 0.9 whiten_kernel.1.white
  14.1 13.0 %collective-permute-start.3 = (bf16[320,1024]{1,0:T(8,128)(2,1)S(1)}, bf16[320,1024]{1,0:T(8,128)(2,1)}, u32[]{:S(2)}, u32[]{:S(2)}) collective-permute-start(bf16[320,1024]{1,0:T(8,128)(2,1)S(1)} %whiten_kernel.1.white), channel_id=1, source_target_pairs={{0,504},{8,0},{16,8},{24,16},{32,24},{40,32},{48,40},{56,48},{64,5... | collective-permute-start | bytes 1966088 | tf_op jit(solution)/shard_map/ppermute | solution.py:180
  27.1 1.9 %collective-permute-start.2 = (bf16[320,1024]{1,0:T(8,128)(2,1)S(1)}, bf16[320,1024]{1,0:T(8,128)(2,1)}, u32[]{:S(2)}, u32[]{:S(2)}) collective-permute-start(bf16[320,1024]{1,0:T(8,128)(2,1)S(1)} %whiten_kernel.1.white), channel_id=1, source_target_pairs={{0,8},{8,16},{16,24},{24,32},{32,40},{40,48},{48,56},{56,64},{64,7... | collective-permute-start | bytes 1966088 | tf_op jit(solution)/shard_map/ppermute | solution.py:180
  29.8 8.1 %collective-permute-start.5 = (s32[320,2]{1,0:T(8,128)S(1)}, s32[320,2]{1,0:T(8,128)}, u32[]{:S(2)}, u32[]{:S(2)}) collective-permute-start(s32[320,2]{1,0:T(8,128)S(1)} %copy.19.valid_here), channel_id=1, source_target_pairs={{0,504},{8,0},{16,8},{24,16},{32,24},{40,32},{48,40},{56,48},{64,5... | collective-permute-start | bytes 7688 | tf_op jit(solution)/shard_map/ppermute | solution.py:180
  37.9 1.9 %collective-permute-start.4 = (s32[320,2]{1,0:T(8,128)S(1)}, s32[320,2]{1,0:T(8,128)}, u32[]{:S(2)}, u32[]{:S(2)}) collective-permute-start(s32[320,2]{1,0:T(8,128)S(1)} %copy.19.valid_here), channel_id=1, source_target_pairs={{0,8},{8,16},{16,24},{24,32},{32,40},{40,48},{48,56},{56,64},{64,7... | collective-permute-start | bytes 7688 | tf_op jit(solution)/shard_map/ppermute | solution.py:180
  39.9 0.7 copy-done.1
  40.5 2.1 %collective-permute-done.5.valid_after = s32[320,2]{1,0:T(8,128)} collective-permute-done((s32[320,2]{1,0:T(8,128)S(1)}, s32[320,2]{1,0:T(8,128)}, u32[]{:S(2)}, u32[]{:S(2)}) %collective-permute-start.5) | collective-permute-done | bytes 2592 | tf_op jit(solution)/shard_map/ppermute | solution.py:180
  42.6 9.0 %collective-permute-done.4.valid_before = s32[320,2]{1,0:T(8,128)} collective-permute-done((s32[320,2]{1,0:T(8,128)S(1)}, s32[320,2]{1,0:T(8,128)}, u32[]{:S(2)}, u32[]{:S(2)}) %collective-permute-start.4) | collective-permute-done | bytes 2592 | tf_op jit(solution)/shard_map/ppermute | solution.py:180
  51.7 4.2 %tiles_kernel.1 = (bf16[160,2560]{1,0:T(8,128)(2,1)S(1)}, bf16[160,2560]{1,0:T(8,128)(2,1)}) custom-call(s32[1]{0:T(128)} %bitcast.odd, bf16[320,1024]{1,0:T(8,128)(2,1)} %collective-permute-done.2.before, bf16[320,1024]{1,0:T(8,128)(2,1)} %collective-permute-done.3.after, bf16[1280,1024]{1,0:T(8,128)(2,1)S(1)} %rotate_kernel.1.right_here, ...), custom_call_target="tpu_custom_call" | custom-call | tf_op jit(solution)/shard_map/tiles_kernel/pallas_call | solution.py:242
  55.9 4.5 %collective-permute-start.6 = (bf16[160,2560]{1,0:T(8,128)(2,1)}, bf16[160,2560]{1,0:T(8,128)(2,1)S(1)}, u32[]{:S(2)}, u32[]{:S(2)}) collective-permute-start(bf16[160,2560]{1,0:T(8,128)(2,1)} %get-tuple-element.20), channel_id=1, source_target_pairs={{0,1},{1,0},{2,3},{3,2},{4,5},{5,4},{6,7},{7,6},{8,9},{9,8},{10,11... | collective-permute-start | bytes 2457608 | tf_op jit(solution)/shard_map/ppermute | solution.py:250
  61.0 0.9 copy-done.2
  61.9 1.8 %gains_kernel.1.gain = f32[160,2560]{1,0:T(8,128)S(1)} custom-call(s32[1]{0:T(128)} %bitcast.odd, s32[320,2]{1,0:T(8,128)} %collective-permute-done.4.valid_before, s32[320,2]{1,0:T(8,128)S(1)} %copy-done.2, s32[320,2]{1,0:T(8,128)} %collective-permute-done.5.valid_after), custom_call_target="tpu_custom_call" | custom-call | tf_op jit(solution)/shard_map/gains_kernel/pallas_call | solution.py:233
  63.7 1.3 %dispatch_kernel.1 = bf16[64,4,8,256]{3,2,1,0:T(8,128)(2,1)S(1)} custom-call(s32[50]{0:T(128)S(1)} %and_select_fusion.place_of, s32[50]{0:T(128)S(1)} %reshape_squeeze.3.listed, bf16[160,2560]{1,0:T(8,128)(2,1)S(1)} %get-tuple-element.19.mine, bf16[160,2560]{1,0:T(8,128)(2,1)S(1)} %collective-permute-done.6.other, f32[160,2560]{1,0:T(8,128)S(1)} %gains_kernel.1.gain), custom_call_target="tpu_custom_call" | custom-call | tf_op jit(solution)/shard_map/dispatch_kernel/pallas_call | solution.py:255
  65.0 46.0 %all_to_all.5 = bf16[256,8,256]{2,1,0:T(8,128)(2,1)S(1)} all-to-all(bf16[256,8,256]{2,1,0:T(8,128)(2,1)S(1)} %bitcast.8), channel_id=1, replica_groups={{8,10,12,14,16,18,20,22,24,26,28,30,32,34,36,38,40,42,44,46,48,50,52,54..., dimensions={0} | all-to-all | bytes 2097152 | tf_op jit(solution)/shard_map/all_to_all | solution.py:270
  111.0 0.9 collect_kernel.1
  (23 shorter events, 1.6 us)
Async XLA Ops:
  0.0 60.4 %copy-start = (s32[64,2,5,5]{0,1,3,2:T(2,128)S(1)}, s32[64,2,5,5]{0,1,3,2:T(2,128)}, u32[]{:S(2)}) copy-start(s32[64,2,5,5]{0,1,3,2:T(2,128)} %param.10) | copy-start | bytes 38404
  3.4 26.1 %copy-start.7 = (s32[320,2]{0,1:T(2,128)S(1)}, s32[320,2]{0,1:T(2,128)}, u32[]{:S(2)}) copy-start(s32[320,2]{0,1:T(2,128)} %param.9) | copy-start | bytes 7684
  3.5 3.9 %collective-permute-start = (bf16[320,32]{1,0:T(8,128)(2,1)S(1)}, bf16[320,32]{1,0:T(8,128)(2,1)S(1)}, u32[]{:S(2)}, u32[]{:S(2)}) collective-permute-start(bf16[320,32]{1,0:T(8,128)(2,1)S(1)} %get-tuple-element.14), channel_id=1, source_target_pairs={{0,1},{1,2},{2,3},{3,4},{4,5},{5,6},{6,7},{8,9},{9,10},{10,11},{11... | collective-permute-start | bytes 61448 | tf_op jit(solution)/shard_map/ppermute | solution.py:185
  5.3 5.5 %collective-permute-start.1 = (bf16[320,32]{1,0:T(8,128)(2,1)S(1)}, bf16[320,32]{1,0:T(8,128)(2,1)S(1)}, u32[]{:S(2)}, u32[]{:S(2)}) collective-permute-start(bf16[320,32]{1,0:T(8,128)(2,1)S(1)} %get-tuple-element.15), channel_id=1, source_target_pairs={{1,0},{2,1},{3,2},{4,3},{5,4},{6,5},{7,6},{9,8},{10,9},{11,10},{12... | collective-permute-start | bytes 61448 | tf_op jit(solution)/shard_map/ppermute | solution.py:185
  10.9 0.9 copy-start.3
  11.8 0.7 copy-start.4
  12.5 0.7 copy-start.5
  14.1 37.6 %collective-permute-start.3 = (bf16[320,1024]{1,0:T(8,128)(2,1)S(1)}, bf16[320,1024]{1,0:T(8,128)(2,1)}, u32[]{:S(2)}, u32[]{:S(2)}) collective-permute-start(bf16[320,1024]{1,0:T(8,128)(2,1)S(1)} %whiten_kernel.1.white), channel_id=1, source_target_pairs={{0,504},{8,0},{16,8},{24,16},{32,24},{40,32},{48,40},{56,48},{64,5... | collective-permute-start | bytes 1966088 | tf_op jit(solution)/shard_map/ppermute | solution.py:180
  27.1 24.5 %collective-permute-start.2 = (bf16[320,1024]{1,0:T(8,128)(2,1)S(1)}, bf16[320,1024]{1,0:T(8,128)(2,1)}, u32[]{:S(2)}, u32[]{:S(2)}) collective-permute-start(bf16[320,1024]{1,0:T(8,128)(2,1)S(1)} %whiten_kernel.1.white), channel_id=1, source_target_pairs={{0,8},{8,16},{16,24},{24,32},{32,40},{40,48},{48,56},{56,64},{64,7... | collective-permute-start | bytes 1966088 | tf_op jit(solution)/shard_map/ppermute | solution.py:180
  29.6 31.2 %copy-start.6 = (s32[64,50]{0,1:T(8,128)S(1)}, s32[64,50]{0,1:T(8,128)}, u32[]{:S(2)}) copy-start(s32[64,50]{0,1:T(8,128)} %param.11) | copy-start | bytes 38404
  29.8 12.9 %collective-permute-start.5 = (s32[320,2]{1,0:T(8,128)S(1)}, s32[320,2]{1,0:T(8,128)}, u32[]{:S(2)}, u32[]{:S(2)}) collective-permute-start(s32[320,2]{1,0:T(8,128)S(1)} %copy.19.valid_here), channel_id=1, source_target_pairs={{0,504},{8,0},{16,8},{24,16},{32,24},{40,32},{48,40},{56,48},{64,5... | collective-permute-start | bytes 7688 | tf_op jit(solution)/shard_map/ppermute | solution.py:180
  37.9 13.7 %collective-permute-start.4 = (s32[320,2]{1,0:T(8,128)S(1)}, s32[320,2]{1,0:T(8,128)}, u32[]{:S(2)}, u32[]{:S(2)}) collective-permute-start(s32[320,2]{1,0:T(8,128)S(1)} %copy.19.valid_here), channel_id=1, source_target_pairs={{0,8},{8,16},{16,24},{24,32},{32,40},{40,48},{48,56},{56,64},{64,7... | collective-permute-start | bytes 7688 | tf_op jit(solution)/shard_map/ppermute | solution.py:180
  39.8 0.7 copy-start.1
  55.9 7.9 %collective-permute-start.6 = (bf16[160,2560]{1,0:T(8,128)(2,1)}, bf16[160,2560]{1,0:T(8,128)(2,1)S(1)}, u32[]{:S(2)}, u32[]{:S(2)}) collective-permute-start(bf16[160,2560]{1,0:T(8,128)(2,1)} %get-tuple-element.20), channel_id=1, source_target_pairs={{0,1},{1,0},{2,3},{3,2},{4,5},{5,4},{6,7},{7,6},{8,9},{9,8},{10,11... | collective-permute-start | bytes 2457608 | tf_op jit(solution)/shard_map/ppermute | solution.py:250
  61.0 0.9 copy-start.2

commit v3 on v2

v3 whole, which is shorter than its diff:
```python
import jax
import jax.numpy as jnp
import numpy as np
from jax import lax
from jax.experimental import pallas as pl
from jax.experimental.pallas import tpu as pltpu
from jax.sharding import PartitionSpec as P

FREQS = 2048
LAGS = 4
LAG_STEP = 25
HALF = 32
EPS = 1e-06

SUB = 5
SB = 64
CH = 320
BAND = 256
PARTS = 4
REACH = 2
N_FREQ = 8
BLOCKS = 64
SHARE = SB // N_FREQ
ROWS = SUB * SHARE
CHIPS = N_FREQ // 2
HALF_ROWS = CHIPS * ROWS
WIDE = 384
COLS = SUB * LAGS * SB
MIB = 1 << 20

VMEM = pl.BlockSpec(memory_space=pltpu.VMEM)
SMEM = pl.BlockSpec(memory_space=pltpu.SMEM)


def bin_tables():
    bins = np.arange(FREQS)
    lags = (np.arange(LAGS) - LAGS // 2) * LAG_STEP
    angle = np.pi * ((lags[:, None] * bins[None, :]) % (2 * FREQS)) / FREQS
    count = np.minimum(bins + HALF, FREQS - 1) - np.maximum(bins - HALF, 0) + 1
    rows = np.concatenate([np.cos(angle), np.sin(angle), np.tile(count, (8, 1))])
    return np.ascontiguousarray(
        rows.reshape(16, N_FREQ, BAND).transpose(1, 0, 2).astype(np.float32)
    )


def part(ref, rows, index):
    return ref[rows, index * BAND : (index + 1) * BAND].astype(jnp.float32)


def amplitudes(block, rows):
    return [
        jnp.sqrt(part(block, rows, i) ** 2 + part(block, rows, i + 2) ** 2) for i in range(2)
    ]


def edges_kernel(odd, raw, inside, across):
    for start in range(0, CH, SB):
        rows = slice(start, start + SB)
        both = amplitudes(raw, rows)
        low = jnp.concatenate([x[:, :HALF] for x in both], axis=1)
        high = jnp.concatenate([x[:, BAND - HALF :] for x in both], axis=1)
        inside[rows, :] = jnp.where(odd[0] > 0, low, high).astype(jnp.bfloat16)
        across[rows, :] = jnp.where(odd[0] > 0, high, low).astype(jnp.bfloat16)


def validity_kernel(valid, tail, columns, wide):
    wide[...] = jnp.zeros_like(wide)
    wide[:2, :CH] = valid[...].astype(jnp.float32)
    tail[...] = wide[...].astype(jnp.bfloat16)
    columns[...] = wide[:8, :WIDE].T


def whiten_kernel(odd, raw, inside, across, tail, columns, table, out, level, window):
    out[CH:, :] = tail[...]
    weights = columns[...]
    for start in range(0, CH, SB):
        rows = slice(start, start + SB)
        one, two = amplitudes(raw, rows)
        level[rows, :] = (one * weights[rows, 0:1] + two * weights[rows, 1:2]).astype(jnp.bfloat16)

    def total(levels, chosen):
        return jnp.dot(
            levels[...], chosen.astype(jnp.bfloat16), preferred_element_type=jnp.float32
        )

    source, out_bin = (lax.broadcasted_iota(jnp.int32, (BAND, BAND), d) for d in range(2))
    sums = total(level, jnp.where(jnp.abs(source - out_bin) <= HALF, 1.0, 0.0))
    lane, edge_out = (lax.broadcasted_iota(jnp.int32, (2 * HALF, BAND), d) for d in range(2))
    for s in range(2):
        edge = lane - s * HALF
        ours = (edge >= 0) & (edge < HALF)
        below = jnp.where(ours & (edge_out <= edge), 1.0, 0.0)
        above = jnp.where(ours & (edge_out >= edge + BAND - HALF), 1.0, 0.0)
        beside = total(inside, jnp.where(odd[0] > 0, below, above))
        beside += total(across, jnp.where(odd[0] > 0, above, below))
        sums += beside * weights[:CH, s : s + 1]
    window[...] = sums
    for start in range(0, CH, SB):
        rows = slice(start, start + SB)
        one, two = weights[rows, 0:1], weights[rows, 1:2]
        mean = window[rows, :] / (table[8:9, :] * jnp.maximum(one + two, 1.0))
        scale = 1.0 / (mean + EPS)
        one, two = one * scale, two * scale
        for i in range(PARTS):
            white = part(raw, rows, i) * (two if i % 2 else one)
            out[rows, i * BAND : (i + 1) * BAND] = white.astype(jnp.bfloat16)


def rotate(white, table, out):
    for u in range(SUB):
        rows = slice(u * SB, (u + 1) * SB)
        for lag in range(LAGS):
            dest = slice((u * LAGS + lag) * SB, (u * LAGS + lag + 1) * SB)
            if lag == LAGS // 2:
                out[dest, :] = white[rows, :]
                continue
            cosine, sine = table[lag : lag + 1, :], table[4 + lag : 5 + lag, :]
            for s in range(2):
                real, imag = part(white, rows, s), part(white, rows, 2 + s)
                out[dest, s * BAND : (s + 1) * BAND] = (
                    real * cosine + imag * sine
                ).astype(jnp.bfloat16)
                out[dest, (2 + s) * BAND : (3 + s) * BAND] = (
                    imag * cosine - real * sine
                ).astype(jnp.bfloat16)


def rotate_kernel(white, table, out):
    rotate(white, table, out)


def place(out, odd, block):
    for u in range(SUB):
        wide = block[u * SB : (u + 1) * SB, :].astype(jnp.float32)
        for target in range(N_FREQ):
            half = lax.rem(odd + target, 2)
            row = half * HALF_ROWS + (target // 2) * ROWS + u * SHARE
            out[pl.ds(pl.multiple_of(row, SHARE), SHARE), :] = wide[
                target * SHARE : (target + 1) * SHARE
            ]


def product(left, right):
    return lax.dot_general(
        left, right, (((1,), (1,)), ((), ())), preferred_element_type=jnp.float32
    )


def near_kernel(odd, place_of, listed, before, right, rows, mine, theirs, left):
    place(left, odd[0], before)
    rows[...] = left[...].astype(jnp.bfloat16)
    tile = product(rows[...], right[...]).astype(jnp.bfloat16)
    mine[...] = tile[:HALF_ROWS]
    theirs[...] = tile[HALF_ROWS:]


def far_kernel(rows, after, near, table, theirs, right):
    rotate(after, table, right)
    theirs[:, :COLS] = near[...]
    theirs[:, COLS:] = product(rows[HALF_ROWS:, :], right[...]).astype(jnp.bfloat16)


def rest_kernel(rows, right, mine):
    mine[...] = product(rows[:HALF_ROWS, :], right[...]).astype(jnp.bfloat16)


def gains_kernel(odd, before, here, after, out, left, right):
    def valid(block):
        return block[CH : CH + 16, : PARTS * 128].astype(jnp.float32)[:8]

    place(left, odd[0], valid(before).T)
    for d, block in enumerate((here, after)):
        flags = valid(block)
        for v in range(SUB):
            chunk = flags[:, v * SB : (v + 1) * SB]
            right[:, d * COLS + v * LAGS * SB : d * COLS + (v + 1) * LAGS * SB] = (
                jnp.concatenate([chunk] * LAGS, axis=1)
            )
    joint = jnp.dot(left[:HALF_ROWS, :], right[...], preferred_element_type=jnp.float32)
    out[...] = jnp.where(joint > 1.5, (2 * FREQS) ** -0.5, FREQS**-0.5)


def dispatch_kernel(place_of, listed, mine, mine_far, other, gain, out, total):
    out[...] = jnp.zeros_like(out)
    for d, ours in enumerate((mine, mine_far)):
        lanes = slice(d * COLS, (d + 1) * COLS)
        pair = ours[...].astype(jnp.float32) + other[:, lanes].astype(jnp.float32)
        total[:, lanes] = pair * gain[:, lanes]
    for slot in range(REACH * SUB * SUB):
        d, u, v = slot // (SUB * SUB), slot // SUB % SUB, slot % SUB

        @pl.when(listed[slot] > 0)
        def _():
            for chip in range(CHIPS):
                out[place_of[slot], chip] = total[
                    chip * ROWS + u * SHARE : chip * ROWS + (u + 1) * SHARE,
                    d * COLS + v * LAGS * SB : d * COLS + (v + 1) * LAGS * SB,
                ].astype(jnp.bfloat16)


def collect_kernel(received, out):
    def block(b, _):
        source = lax.rem(b + 1, BLOCKS)
        total = received[source, 0].astype(jnp.float32)
        for chip in range(1, CHIPS):
            total += received[source, chip].astype(jnp.float32)
        out[b] = total.astype(jnp.bfloat16)

    lax.fori_loop(0, BLOCKS, block, None, unroll=8)


def ring(x, axis, step):
    count = lax.axis_size(axis)
    return lax.ppermute(x, axis, [(i, (i + step) % count) for i in range(count)])


def swap(x, first):
    pairs = [(k, k + 1) for k in range(first, N_FREQ - 1, 2)]
    return lax.ppermute(x, "freq", pairs + [(k, i) for i, k in pairs])


def bf16(*shape):
    return jax.ShapeDtypeStruct(shape, jnp.bfloat16)


def kernel(fn, out_shape, inputs, scratch=(), scalars=0, mib=8):
    return pl.pallas_call(
        fn,
        out_shape=out_shape,
        in_specs=[SMEM] * scalars + [VMEM] * (inputs - scalars),
        out_specs=jax.tree.map(lambda _: VMEM, out_shape),
        scratch_shapes=[pltpu.VMEM(shape, dtype) for shape, dtype in scratch],
        compiler_params=pltpu.CompilerParams(vmem_limit_bytes=mib * MIB),
        name=fn.__name__,
    )


def body(spectra, validity, pair_mask, owners):
    f32 = jnp.float32
    chan, freq = lax.axis_index("chan"), lax.axis_index("freq")
    odd = (freq % 2)[None]
    table = lax.dynamic_index_in_dim(jnp.asarray(bin_tables()), freq, 0, keepdims=False)
    raw = spectra.reshape(CH, PARTS * BAND)
    edge = bf16(CH, 2 * HALF)
    to_inside, to_across = kernel(edges_kernel, (edge, edge), 2, scalars=1)(odd, raw)
    across = swap(to_across, 1)
    inside = swap(to_inside, 0)
    tail, columns = kernel(
        validity_kernel,
        (bf16(16, PARTS * BAND), jax.ShapeDtypeStruct((WIDE, 8), f32)),
        1,
        [((16, PARTS * BAND), f32)],
    )(validity.T)
    white = kernel(
        whiten_kernel,
        bf16(CH + 16, PARTS * BAND),
        7,
        [((CH, BAND), jnp.bfloat16), ((CH, BAND), f32)],
        scalars=1,
    )(odd, raw, inside, across, tail, columns, table)
    before = ring(white, "chan", 1)
    after = ring(white, "chan", -1)

    right_here = kernel(rotate_kernel, bf16(COLS, PARTS * BAND), 2)(white, table)
    gain = kernel(
        gains_kernel,
        jax.ShapeDtypeStruct((HALF_ROWS, REACH * COLS), f32),
        4,
        [((2 * HALF_ROWS, 8), f32), ((8, REACH * COLS), f32)],
        scalars=1,
    )(odd, before, white, after)

    block = (chan + BLOCKS - 1) % BLOCKS
    listed = pair_mask[block].reshape(-1)
    place_of = owners[block]
    half = bf16(HALF_ROWS, COLS)
    right = bf16(COLS, PARTS * BAND)
    rows, mine, near = kernel(
        near_kernel,
        (bf16(2 * HALF_ROWS, PARTS * BAND), half, half),
        5,
        [((2 * HALF_ROWS, PARTS * BAND), f32)],
        scalars=3,
        mib=10,
    )(odd, place_of, listed, before, right_here)
    theirs, right_after = kernel(far_kernel, (bf16(HALF_ROWS, REACH * COLS), right), 4)(
        rows, after, near, table
    )
    mine_far = kernel(rest_kernel, half, 2)(rows, right_after)
    other = lax.ppermute(theirs, "freq", [(k, k ^ 1) for k in range(N_FREQ)])

    outgoing = kernel(
        dispatch_kernel,
        bf16(BLOCKS, CHIPS, SHARE, LAGS * SB),
        6,
        [((HALF_ROWS, REACH * COLS), f32)],
        scalars=2,
    )(place_of, listed, mine, mine_far, other, gain)
    groups = [
        [
            b * N_FREQ + 2 * chip + core
            for b in range(BLOCKS)
            for chip in range(CHIPS)
        ]
        for core in range(2)
    ]
    received = lax.all_to_all(
        outgoing.reshape(BLOCKS * CHIPS, SHARE, LAGS * SB),
        ("chan", "freq"),
        0,
        0,
        tiled=True,
        axis_index_groups=groups,
    )
    merged = kernel(collect_kernel, bf16(BLOCKS, SHARE, LAGS * SB), 1)(
        received.reshape(BLOCKS, CHIPS, SHARE, LAGS * SB)
    )
    return merged[None, :, None]


def solution(mesh):
    return jax.shard_map(
        body,
        mesh=mesh,
        in_specs=(P("chan", None, None, "freq"), P("chan", None), P(), P()),
        out_specs=P("chan", None, None, "freq", None),
        check_vma=False,
    )
```

time: 113 us -> 100 us (0.88)
  starting transfers between devices: 32.7 us -> 23.6 us
  blocking collectives: 46 us -> 54.1 us
  waiting for transfers between devices: 14.7 us -> 9.4 us
  local copies, waits for them, and re-layouts: 8.19 us -> 4.18 us
  Pallas kernels: 9.94 us -> 8.27 us
    ppermute x4 -> x2, starting transfers between devices: 25 us -> 14.9 us  [ring(): lax.ppermute(x, axis, [(i, (i + step) % count) for i in range(count)])]
    all_to_all x1, blocking collectives: 46 us -> 54.1 us  [body(): lax.all_to_all(outgoing.reshape(BLOCKS * CHIPS, SHARE, LAGS * SB), ('chan...]
    unnamed x17 -> x6, local copies, waits for them, and re-layouts: 4.75 us -> 0.7 us
    ppermute x2, waiting for transfers between devices: 3.51 us -> 0.01 us  [swap(): return lax.ppermute(x, 'freq', pairs + [(k, i) for i, k in pairs])]
    ppermute x4 -> x2, waiting for transfers between devices: 11.1 us -> 8.92 us  [ring(): lax.ppermute(x, axis, [(i, (i + step) % count) for i in range(count)])]
    ppermute x1, starting transfers between devices: 4.52 us -> 6.02 us  [body(): other = lax.ppermute(theirs, 'freq', [(k, k ^ 1) for k in range(N_FREQ)])]
    pallas_call x1, Pallas kernels: 1.8 us -> 0.46 us  [body(): kernel(gains_kernel, jax.ShapeDtypeStruct((HALF_ROWS, REACH * COLS), f32)...]
    pallas_call x4 -> x7, Pallas kernels: 6.74 us -> 6.34 us  [the longest x1 1.77 us: body(): kernel(near_kernel, (bf16(2 * HALF_ROWS, PARTS * BAND), half, half), 5, [...]
  transfers between devices with their start and end apart: 7 -> 5, of which waited for: 3 -> 2; matrix products, arithmetic and copies ran while one was open for 1% -> 1% of each run, Pallas kernels for 2% -> 4%
where the time goes in v3:
time: 100 us; the launch traced here: 99.7 us
  blocking collectives  54.1 us (54%)
  starting transfers between devices  23.6 us (24%)
  waiting for transfers between devices  9.4 us (9%)
  Pallas kernels  8.27 us (8%)
  local copies, waits for them, and re-layouts  4.18 us (4%)
    all_to_all x1, blocking collectives, body(): lax.all_to_all(outgoing.reshape(BLOCKS * CHIPS, SHARE, LAGS * SB), ('chan...  54.1 us
    ppermute x2, starting transfers between devices, ring(): lax.ppermute(x, axis, [(i, (i + step) % count) for i in range(count)])  14.9 us
    ppermute x2, waiting for transfers between devices, ring(): lax.ppermute(x, axis, [(i, (i + step) % count) for i in range(count)])  8.92 us
    ppermute x1, starting transfers between devices, body(): other = lax.ppermute(theirs, 'freq', [(k, k ^ 1) for k in range(N_FREQ)])  6.02 us
    ppermute x2, starting transfers between devices, swap(): return lax.ppermute(x, 'freq', pairs + [(k, i) for i, k in pairs])  2.59 us
    reshape x1, local copies, waits for them, and re-layouts, body(): raw = spectra.reshape(CH, PARTS * BAND)  2.23 us
  transfers between devices with their start and end apart: 5, of which 2 were waited for; matrix products, arithmetic and copies ran while one was open for 1% of the time, Pallas kernels for 4%

profile of v3, /device:TPU:8, one launch (start us, length us, event | category | flops | bytes accessed | tf_op | source)
XLA Modules:
  0.0 99.7 jit_solution(16902496045812765864)
XLA Ops:
  0.0 2.2 %reshape.9.raw = bf16[320,1024]{1,0:T(8,128)(2,1)S(1)} reshape(bf16[320,2,2,256]{3,2,1,0:T(2,128)(2,1)} %param.5) | data formatting | bytes 1310720 | tf_op jit(solution)/shard_map/reshape | solution.py:243
  2.3 0.3 edges_kernel.1
  2.6 1.9 %collective-permute-start = (bf16[320,64]{1,0:T(8,128)(2,1)S(1)}, bf16[320,64]{1,0:T(8,128)(2,1)S(1)}, u32[]{:S(2)}, u32[]{:S(2)}) collective-permute-start(bf16[320,64]{1,0:T(8,128)(2,1)S(1)} %get-tuple-element.14), channel_id=1, source_target_pairs={{0,1},{2,3},{4,5},{6,7},{1,0},{3,2},{5,4},{7,6},{8,9},{10,11},{12,... | collective-permute-start | bytes 122888 | tf_op jit(solution)/shard_map/ppermute | solution.py:219
  4.5 0.7 collective-permute-start.1
  5.2 0.7 dynamic-slice_bitcast_fusion.table
  5.9 0.7 copy-done.1
  6.6 0.1 validity_kernel.1
  6.7 0.6 whiten_kernel.1.white.here
  7.4 3.4 %collective-permute-start.2 = (bf16[336,1024]{1,0:T(8,128)(2,1)S(1)}, bf16[336,1024]{1,0:T(8,128)(2,1)S(1)}, u32[]{:S(2)}, u32[]{:S(2)}) collective-permute-start(bf16[336,1024]{1,0:T(8,128)(2,1)S(1)} %whiten_kernel.1.white.here), channel_id=1, source_target_pairs={{0,8},{8,16},{16,24},{24,32},{32,40},{40,48},{48,56},{56,64},{64,7... | collective-permute-start | bytes 2064392 | tf_op jit(solution)/shard_map/ppermute | solution.py:214
  10.8 11.6 %collective-permute-start.3 = (bf16[336,1024]{1,0:T(8,128)(2,1)S(1)}, bf16[336,1024]{1,0:T(8,128)(2,1)S(1)}, u32[]{:S(2)}, u32[]{:S(2)}) collective-permute-start(bf16[336,1024]{1,0:T(8,128)(2,1)S(1)} %whiten_kernel.1.white.here), channel_id=1, source_target_pairs={{0,504},{8,0},{16,8},{24,16},{32,24},{40,32},{48,40},{56,48},{64,5... | collective-permute-start | bytes 2064392 | tf_op jit(solution)/shard_map/ppermute | solution.py:214
  22.4 0.1 constant_dynamic-slice_fusion
  22.5 0.2 copy.8
  22.8 0.2 dynamic-slice_reduce_fusion.place_of
  22.9 0.5 rotate_kernel.1.right
  23.5 8.9 %collective-permute-done.2.before = bf16[336,1024]{1,0:T(8,128)(2,1)S(1)} collective-permute-done((bf16[336,1024]{1,0:T(8,128)(2,1)S(1)}, bf16[336,1024]{1,0:T(8,128)(2,1)S(1)}, u32[]{:S(2)}, u32[]{:S(2)}) %collective-permute-start.2) | collective-permute-done | bytes 688160 | tf_op jit(solution)/shard_map/ppermute | solution.py:214
  32.4 1.8 %near_kernel.1 = (bf16[320,1024]{1,0:T(8,128)(2,1)S(1)}, bf16[160,1280]{1,0:T(8,128)(2,1)S(1)}, bf16[160,1280]{1,0:T(8,128)(2,1)S(1)}) custom-call(s32[1]{0:T(128)} %bitcast.odd, s32[50]{0:T(128)S(1)} %dynamic-slice_reduce_fusion.place_of, s32[50]{0:T(128)S(1)} %reshape_squeeze.3.listed, bf16[336,1024]{1,0:T(8,128)(2,1)S(1)} %collective-permute-done.2.before, ...), custom_call_target="tpu_custom_call" | custom-call | tf_op jit(solution)/shard_map/near_kernel/pallas_call | solution.py:278
  34.2 1.2 %far_kernel.1 = (bf16[160,2560]{1,0:T(8,128)(2,1)S(1)}, bf16[1280,1024]{1,0:T(8,128)(2,1)S(1)}) custom-call(bf16[320,1024]{1,0:T(8,128)(2,1)S(1)} %get-tuple-element.19.rows, bf16[336,1024]{1,0:T(8,128)(2,1)S(1)} %collective-permute-done.3.after, bf16[160,1280]{1,0:T(8,128)(2,1)S(1)} %get-tuple-element.20.near, f32[16,256]{1,0:T(8,128)S(1)} %dynamic-slice_bitcast_fusion.table), custom_call_target="tpu_custom_call" | custom-call | tf_op jit(solution)/shard_map/far_kernel/pallas_call | solution.py:286
  35.4 6.0 %collective-permute-start.4 = (bf16[160,2560]{1,0:T(8,128)(2,1)S(1)}, bf16[160,2560]{1,0:T(8,128)(2,1)S(1)}, u32[]{:S(2)}, u32[]{:S(2)}) collective-permute-start(bf16[160,2560]{1,0:T(8,128)(2,1)S(1)} %get-tuple-element.22), channel_id=1, source_target_pairs={{0,1},{1,0},{2,3},{3,2},{4,5},{5,4},{6,7},{7,6},{8,9},{9,8},{10,11... | collective-permute-start | bytes 2457608 | tf_op jit(solution)/shard_map/ppermute | solution.py:290
  41.4 1.0 %rest_kernel.1.mine_far = bf16[160,1280]{1,0:T(8,128)(2,1)S(1)} custom-call(bf16[320,1024]{1,0:T(8,128)(2,1)S(1)} %get-tuple-element.19.rows, bf16[1280,1024]{1,0:T(8,128)(2,1)S(1)} %get-tuple-element.21.right), custom_call_target="tpu_custom_call" | custom-call | tf_op jit(solution)/shard_map/rest_kernel/pallas_call | solution.py:289
  42.5 0.5 gains_kernel.1.gain
  42.9 0.5 collective-permute-done.4.other
  43.4 1.3 %dispatch_kernel.1 = bf16[64,4,8,256]{3,2,1,0:T(8,128)(2,1)S(1)} custom-call(s32[50]{0:T(128)S(1)} %dynamic-slice_reduce_fusion.place_of, s32[50]{0:T(128)S(1)} %reshape_squeeze.3.listed, bf16[160,1280]{1,0:T(8,128)(2,1)S(1)} %get-tuple-element.18.mine, bf16[160,1280]{1,0:T(8,128)(2,1)S(1)} %rest_kernel.1.mine_far, ...), custom_call_target="tpu_custom_call" | custom-call | tf_op jit(solution)/shard_map/dispatch_kernel/pallas_call | solution.py:292
  44.7 54.1 %all_to_all.5 = bf16[256,8,256]{2,1,0:T(8,128)(2,1)S(1)} all-to-all(bf16[256,8,256]{2,1,0:T(8,128)(2,1)S(1)} %bitcast.9), channel_id=1, replica_groups={{0,2,4,6,8,10,12,14,16,18,20,22,24,26,28,30,32,34,36,38,40,42,44,46,48,..., dimensions={0} | all-to-all | bytes 2097152 | tf_op jit(solution)/shard_map/all_to_all | solution.py:307
  98.8 0.9 collect_kernel.1
  (9 shorter events, 0.1 us)
Async XLA Ops:
  0.0 22.7 %copy-start = (s32[64,50]{0,1:T(8,128)S(1)}, s32[64,50]{0,1:T(8,128)}, u32[]{:S(2)}) copy-start(s32[64,50]{0,1:T(8,128)} %param.8) | copy-start | bytes 38404
  0.0 22.4 %copy-start.2 = (s32[64,2,5,5]{0,1,3,2:T(2,128)S(1)}, s32[64,2,5,5]{0,1,3,2:T(2,128)}, u32[]{:S(2)}) copy-start(s32[64,2,5,5]{0,1,3,2:T(2,128)} %param.7) | copy-start | bytes 38404
  2.6 4.2 %collective-permute-start = (bf16[320,64]{1,0:T(8,128)(2,1)S(1)}, bf16[320,64]{1,0:T(8,128)(2,1)S(1)}, u32[]{:S(2)}, u32[]{:S(2)}) collective-permute-start(bf16[320,64]{1,0:T(8,128)(2,1)S(1)} %get-tuple-element.14), channel_id=1, source_target_pairs={{0,1},{2,3},{4,5},{6,7},{1,0},{3,2},{5,4},{7,6},{8,9},{10,11},{12,... | collective-permute-start | bytes 122888 | tf_op jit(solution)/shard_map/ppermute | solution.py:219
  4.5 2.2 %collective-permute-start.1 = (bf16[320,64]{1,0:T(8,128)(2,1)S(1)}, bf16[320,64]{1,0:T(8,128)(2,1)S(1)}, u32[]{:S(2)}, u32[]{:S(2)}) collective-permute-start(bf16[320,64]{1,0:T(8,128)(2,1)S(1)} %get-tuple-element.15), channel_id=1, source_target_pairs={{1,2},{3,4},{5,6},{2,1},{4,3},{6,5},{9,10},{11,12},{13,14},{10,9},... | collective-permute-start | bytes 122888 | tf_op jit(solution)/shard_map/ppermute | solution.py:219
  5.9 0.7 copy-start.1
  7.4 25.0 %collective-permute-start.2 = (bf16[336,1024]{1,0:T(8,128)(2,1)S(1)}, bf16[336,1024]{1,0:T(8,128)(2,1)S(1)}, u32[]{:S(2)}, u32[]{:S(2)}) collective-permute-start(bf16[336,1024]{1,0:T(8,128)(2,1)S(1)} %whiten_kernel.1.white.here), channel_id=1, source_target_pairs={{0,8},{8,16},{16,24},{24,32},{32,40},{40,48},{48,56},{56,64},{64,7... | collective-permute-start | bytes 2064392 | tf_op jit(solution)/shard_map/ppermute | solution.py:214
  10.8 23.4 %collective-permute-start.3 = (bf16[336,1024]{1,0:T(8,128)(2,1)S(1)}, bf16[336,1024]{1,0:T(8,128)(2,1)S(1)}, u32[]{:S(2)}, u32[]{:S(2)}) collective-permute-start(bf16[336,1024]{1,0:T(8,128)(2,1)S(1)} %whiten_kernel.1.white.here), channel_id=1, source_target_pairs={{0,504},{8,0},{16,8},{24,16},{32,24},{40,32},{48,40},{56,48},{64,5... | collective-permute-start | bytes 2064392 | tf_op jit(solution)/shard_map/ppermute | solution.py:214
  35.4 8.0 %collective-permute-start.4 = (bf16[160,2560]{1,0:T(8,128)(2,1)S(1)}, bf16[160,2560]{1,0:T(8,128)(2,1)S(1)}, u32[]{:S(2)}, u32[]{:S(2)}) collective-permute-start(bf16[160,2560]{1,0:T(8,128)(2,1)S(1)} %get-tuple-element.22), channel_id=1, source_target_pairs={{0,1},{1,0},{2,3},{3,2},{4,5},{5,4},{6,7},{7,6},{8,9},{9,8},{10,11... | collective-permute-start | bytes 2457608 | tf_op jit(solution)/shard_map/ppermute | solution.py:290

commit v4 on v3

--- a/solution.py
+++ b/solution.py
@@ -32,14 +32,12 @@
 SMEM = pl.BlockSpec(memory_space=pltpu.SMEM)
 
 
-def bin_tables():
-    bins = np.arange(FREQS)
+def lag_tables():
     lags = (np.arange(LAGS) - LAGS // 2) * LAG_STEP
-    angle = np.pi * ((lags[:, None] * bins[None, :]) % (2 * FREQS)) / FREQS
-    count = np.minimum(bins + HALF, FREQS - 1) - np.maximum(bins - HALF, 0) + 1
-    rows = np.concatenate([np.cos(angle), np.sin(angle), np.tile(count, (8, 1))])
+    angle = np.pi * ((lags[:, None] * np.arange(FREQS)[None, :]) % (2 * FREQS)) / FREQS
+    rows = np.concatenate([np.cos(angle), np.sin(angle)])
     return np.ascontiguousarray(
-        rows.reshape(16, N_FREQ, BAND).transpose(1, 0, 2).astype(np.float32)
+        rows.reshape(8, N_FREQ, BAND).transpose(1, 0, 2).astype(np.float32)
     )
 
 
@@ -53,26 +51,38 @@
     ]
 
 
-def edges_kernel(odd, raw, inside, across):
+def edge(raw, rows, high):
+    both = amplitudes(raw, rows)
+    ends = [
+        jnp.concatenate([x[:, start : start + HALF] for x in both], axis=1)
+        for start in (0, BAND - HALF)
+    ]
+    return jnp.where(high > 0, ends[1], ends[0]).astype(jnp.bfloat16)
+
+
+def across_kernel(odd, raw, out):
     for start in range(0, CH, SB):
         rows = slice(start, start + SB)
-        both = amplitudes(raw, rows)
-        low = jnp.concatenate([x[:, :HALF] for x in both], axis=1)
-        high = jnp.concatenate([x[:, BAND - HALF :] for x in both], axis=1)
-        inside[rows, :] = jnp.where(odd[0] > 0, low, high).astype(jnp.bfloat16)
-        across[rows, :] = jnp.where(odd[0] > 0, high, low).astype(jnp.bfloat16)
-
-
-def validity_kernel(valid, tail, columns, wide):
+        out[rows, :] = edge(raw, rows, odd[0])
+
+
+def inside_kernel(odd, raw, across, valid, out, tail, columns, wide):
+    for start in range(0, CH, SB):
+        rows = slice(start, start + SB)
+        out[rows, :] = edge(raw, rows, 1 - odd[0])
     wide[...] = jnp.zeros_like(wide)
     wide[:2, :CH] = valid[...].astype(jnp.float32)
     tail[...] = wide[...].astype(jnp.bfloat16)
     columns[...] = wide[:8, :WIDE].T
 
 
-def whiten_kernel(odd, raw, inside, across, tail, columns, table, out, level, window):
+def whiten_kernel(spot, raw, inside, across, tail, columns, table, out, level, window):
     out[CH:, :] = tail[...]
     weights = columns[...]
+    odd = lax.rem(spot[0], 2)
+    bins = spot[0] * BAND + lax.broadcasted_iota(jnp.int32, (1, BAND), 1)
+    count = jnp.minimum(bins + HALF, FREQS - 1) - jnp.maximum(bins - HALF, 0) + 1
+    count = count.astype(jnp.float32)
     for start in range(0, CH, SB):
         rows = slice(start, start + SB)
         one, two = amplitudes(raw, rows)
@@ -91,14 +101,14 @@
         ours = (edge >= 0) & (edge < HALF)
         below = jnp.where(ours & (edge_out <= edge), 1.0, 0.0)
         above = jnp.where(ours & (edge_out >= edge + BAND - HALF), 1.0, 0.0)
-        beside = total(inside, jnp.where(odd[0] > 0, below, above))
-        beside += total(across, jnp.where(odd[0] > 0, above, below))
+        beside = total(inside, jnp.where(odd > 0, below, above))
+        beside += total(across, jnp.where(odd > 0, above, below))
         sums += beside * weights[:CH, s : s + 1]
     window[...] = sums
     for start in range(0, CH, SB):
         rows = slice(start, start + SB)
         one, two = weights[rows, 0:1], weights[rows, 1:2]
-        mean = window[rows, :] / (table[8:9, :] * jnp.maximum(one + two, 1.0))
+        mean = window[rows, :] / (count * jnp.maximum(one + two, 1.0))
         scale = 1.0 / (mean + EPS)
         one, two = one * scale, two * scale
         for i in range(PARTS):
@@ -239,29 +249,27 @@
     f32 = jnp.float32
     chan, freq = lax.axis_index("chan"), lax.axis_index("freq")
     odd = (freq % 2)[None]
-    table = lax.dynamic_index_in_dim(jnp.asarray(bin_tables()), freq, 0, keepdims=False)
+    table = lax.dynamic_index_in_dim(jnp.asarray(lag_tables()), freq, 0, keepdims=False)
     raw = spectra.reshape(CH, PARTS * BAND)
-    edge = bf16(CH, 2 * HALF)
-    to_inside, to_across = kernel(edges_kernel, (edge, edge), 2, scalars=1)(odd, raw)
+    edges = bf16(CH, 2 * HALF)
+    to_across = kernel(across_kernel, edges, 2, scalars=1)(odd, raw)
     across = swap(to_across, 1)
+    to_inside, tail, columns = kernel(
+        inside_kernel,
+        (edges, bf16(16, PARTS * BAND), jax.ShapeDtypeStruct((WIDE, 8), f32)),
+        4,
+        [((16, PARTS * BAND), f32)],
+        scalars=1,
+    )(odd, raw, to_across, validity.T)
     inside = swap(to_inside, 0)
-    tail, columns = kernel(
-        validity_kernel,
-        (bf16(16, PARTS * BAND), jax.ShapeDtypeStruct((WIDE, 8), f32)),
-        1,
-        [((16, PARTS * BAND), f32)],
-    )(validity.T)
+    block = bf16(CH + 16, PARTS * BAND)
     white = kernel(
-        whiten_kernel,
-        bf16(CH + 16, PARTS * BAND),
-        7,
-        [((CH, BAND), jnp.bfloat16), ((CH, BAND), f32)],
-        scalars=1,
-    )(odd, raw, inside, across, tail, columns, table)
+        whiten_kernel, block, 7, [((CH, BAND), jnp.bfloat16), ((CH, BAND), f32)], scalars=1
+    )(freq[None], raw, inside, across, tail, columns, table)
+    after = ring(white, "chan", -1)
     before = ring(white, "chan", 1)
-    after = ring(white, "chan", -1)
-
     right_here = kernel(rotate_kernel, bf16(COLS, PARTS * BAND), 2)(white, table)
+
     gain = kernel(
         gains_kernel,
         jax.ShapeDtypeStruct((HALF_ROWS, REACH * COLS), f32),
@@ -270,9 +278,9 @@
         scalars=1,
     )(odd, before, white, after)
 
-    block = (chan + BLOCKS - 1) % BLOCKS
-    listed = pair_mask[block].reshape(-1)
-    place_of = owners[block]
+    source = (chan + BLOCKS - 1) % BLOCKS
+    listed = pair_mask[source].reshape(-1)
+    place_of = owners[source]
     half = bf16(HALF_ROWS, COLS)
     right = bf16(COLS, PARTS * BAND)
     rows, mine, near = kernel(

time: 100 us -> 97.5 us (0.975)
  blocking collectives: 54.1 us -> 47 us
  waiting for transfers between devices: 9.4 us -> 13.9 us
    all_to_all x1, blocking collectives: 54.1 us -> 47 us  [body(): lax.all_to_all(outgoing.reshape(BLOCKS * CHIPS, SHARE, LAGS * SB), ('chan...]
    ppermute x1, starting transfers between devices: 6.02 us -> 1.92 us  [body(): other = lax.ppermute(theirs, 'freq', [(k, k ^ 1) for k in range(N_FREQ)])]
    ppermute x2, waiting for transfers between devices: 8.92 us -> 12.9 us  [ring(): lax.ppermute(x, axis, [(i, (i + step) % count) for i in range(count)])]
    ppermute x2, starting transfers between devices: 2.59 us -> 6.52 us  [swap(): return lax.ppermute(x, 'freq', pairs + [(k, i) for i, k in pairs])]
  transfers between devices with their start and end apart: 5 -> 5, of which waited for: 2 -> 3; matrix products, arithmetic and copies ran while one was open for 1% -> 1% of each run, Pallas kernels for 4% -> 4%
where the time goes in v4:
time: 97.5 us; the launch traced here: 97.1 us
  blocking collectives  47 us (48%)
  starting transfers between devices  23.4 us (24%)
  waiting for transfers between devices  13.9 us (14%)
  Pallas kernels  8.47 us (9%)
  local copies, waits for them, and re-layouts  4.15 us (4%)
    all_to_all x1, blocking collectives, body(): lax.all_to_all(outgoing.reshape(BLOCKS * CHIPS, SHARE, LAGS * SB), ('chan...  47 us
    ppermute x2, starting transfers between devices, ring(): lax.ppermute(x, axis, [(i, (i + step) % count) for i in range(count)])  15 us
    ppermute x2, waiting for transfers between devices, ring(): lax.ppermute(x, axis, [(i, (i + step) % count) for i in range(count)])  12.9 us
    ppermute x2, starting transfers between devices, swap(): return lax.ppermute(x, 'freq', pairs + [(k, i) for i, k in pairs])  6.52 us
    reshape x1, local copies, waits for them, and re-layouts, body(): raw = spectra.reshape(CH, PARTS * BAND)  2.23 us
  transfers between devices with their start and end apart: 5, of which 3 were waited for; matrix products, arithmetic and copies ran while one was open for 1% of the time, Pallas kernels for 4%

profile of v4, /device:TPU:8, one launch (start us, length us, event | category | flops | bytes accessed | tf_op | source)
XLA Modules:
  0.0 97.1 jit_solution(7756394578616945536)
XLA Ops:
  0.0 2.2 %reshape.9.raw = bf16[320,1024]{1,0:T(8,128)(2,1)S(1)} reshape(bf16[320,2,2,256]{3,2,1,0:T(2,128)(2,1)} %param.5) | data formatting | bytes 1310720 | tf_op jit(solution)/shard_map/reshape | solution.py:253
  2.3 0.3 across_kernel.1.across
  2.6 0.7 collective-permute-start.1
  3.3 0.7 copy-done.1
  3.9 0.4 inside_kernel.1
  4.3 5.9 %collective-permute-start = (bf16[320,64]{1,0:T(8,128)(2,1)S(1)}, bf16[320,64]{1,0:T(8,128)(2,1)S(1)}, u32[]{:S(2)}, u32[]{:S(2)}) collective-permute-start(bf16[320,64]{1,0:T(8,128)(2,1)S(1)} %get-tuple-element.13), channel_id=1, source_target_pairs={{0,1},{2,3},{4,5},{6,7},{1,0},{3,2},{5,4},{7,6},{8,9},{10,11},{12,... | collective-permute-start | bytes 122888 | tf_op jit(solution)/shard_map/ppermute | solution.py:229
  10.2 0.7 dynamic-slice_bitcast_fusion.table
  10.9 0.2 collective-permute-done.inside
  11.1 0.6 whiten_kernel.1.white.here
  11.7 3.4 %collective-permute-start.2 = (bf16[336,1024]{1,0:T(8,128)(2,1)S(1)}, bf16[336,1024]{1,0:T(8,128)(2,1)S(1)}, u32[]{:S(2)}, u32[]{:S(2)}) collective-permute-start(bf16[336,1024]{1,0:T(8,128)(2,1)S(1)} %whiten_kernel.1.white.here), channel_id=1, source_target_pairs={{0,8},{8,16},{16,24},{24,32},{32,40},{40,48},{48,56},{56,64},{64,7... | collective-permute-start | bytes 2064392 | tf_op jit(solution)/shard_map/ppermute | solution.py:224
  15.1 11.6 %collective-permute-start.3 = (bf16[336,1024]{1,0:T(8,128)(2,1)S(1)}, bf16[336,1024]{1,0:T(8,128)(2,1)S(1)}, u32[]{:S(2)}, u32[]{:S(2)}) collective-permute-start(bf16[336,1024]{1,0:T(8,128)(2,1)S(1)} %whiten_kernel.1.white.here), channel_id=1, source_target_pairs={{0,504},{8,0},{16,8},{24,16},{32,24},{40,32},{48,40},{56,48},{64,5... | collective-permute-start | bytes 2064392 | tf_op jit(solution)/shard_map/ppermute | solution.py:224
  26.8 0.2 copy.8
  27.1 0.2 dynamic-slice_reduce_fusion.place_of
  27.2 0.5 rotate_kernel.1.right
  27.8 12.9 %collective-permute-done.2.before = bf16[336,1024]{1,0:T(8,128)(2,1)S(1)} collective-permute-done((bf16[336,1024]{1,0:T(8,128)(2,1)S(1)}, bf16[336,1024]{1,0:T(8,128)(2,1)S(1)}, u32[]{:S(2)}, u32[]{:S(2)}) %collective-permute-start.2) | collective-permute-done | bytes 688160 | tf_op jit(solution)/shard_map/ppermute | solution.py:224
  40.7 1.8 %near_kernel.1 = (bf16[320,1024]{1,0:T(8,128)(2,1)S(1)}, bf16[160,1280]{1,0:T(8,128)(2,1)S(1)}, bf16[160,1280]{1,0:T(8,128)(2,1)S(1)}) custom-call(s32[1]{0:T(128)} %bitcast.odd, s32[50]{0:T(128)S(1)} %dynamic-slice_reduce_fusion.place_of, s32[50]{0:T(128)S(1)} %reshape_squeeze.3.listed, bf16[336,1024]{1,0:T(8,128)(2,1)S(1)} %collective-permute-done.2.before, ...), custom_call_target="tpu_custom_call" | custom-call | tf_op jit(solution)/shard_map/near_kernel/pallas_call | solution.py:286
  42.5 1.2 %far_kernel.1 = (bf16[160,2560]{1,0:T(8,128)(2,1)S(1)}, bf16[1280,1024]{1,0:T(8,128)(2,1)S(1)}) custom-call(bf16[320,1024]{1,0:T(8,128)(2,1)S(1)} %get-tuple-element.17.rows, bf16[336,1024]{1,0:T(8,128)(2,1)S(1)} %collective-permute-done.3.after, bf16[160,1280]{1,0:T(8,128)(2,1)S(1)} %get-tuple-element.18.near, f32[8,256]{1,0:T(8,128)S(1)} %dynamic-slice_bitcast_fusion.table), custom_call_target="tpu_custom_call" | custom-call | tf_op jit(solution)/shard_map/far_kernel/pallas_call | solution.py:294
  43.7 1.9 %collective-permute-start.4 = (bf16[160,2560]{1,0:T(8,128)(2,1)S(1)}, bf16[160,2560]{1,0:T(8,128)(2,1)S(1)}, u32[]{:S(2)}, u32[]{:S(2)}) collective-permute-start(bf16[160,2560]{1,0:T(8,128)(2,1)S(1)} %get-tuple-element.20), channel_id=1, source_target_pairs={{0,1},{1,0},{2,3},{3,2},{4,5},{5,4},{6,7},{7,6},{8,9},{9,8},{10,11... | collective-permute-start | bytes 2457608 | tf_op jit(solution)/shard_map/ppermute | solution.py:298
  45.6 1.0 %rest_kernel.1.mine_far = bf16[160,1280]{1,0:T(8,128)(2,1)S(1)} custom-call(bf16[320,1024]{1,0:T(8,128)(2,1)S(1)} %get-tuple-element.17.rows, bf16[1280,1024]{1,0:T(8,128)(2,1)S(1)} %get-tuple-element.19.right), custom_call_target="tpu_custom_call" | custom-call | tf_op jit(solution)/shard_map/rest_kernel/pallas_call | solution.py:297
  46.6 0.5 gains_kernel.1.gain
  47.1 0.8 collective-permute-done.4.other
  47.9 1.3 %dispatch_kernel.1 = bf16[64,4,8,256]{3,2,1,0:T(8,128)(2,1)S(1)} custom-call(s32[50]{0:T(128)S(1)} %dynamic-slice_reduce_fusion.place_of, s32[50]{0:T(128)S(1)} %reshape_squeeze.3.listed, bf16[160,1280]{1,0:T(8,128)(2,1)S(1)} %get-tuple-element.16.mine, bf16[160,1280]{1,0:T(8,128)(2,1)S(1)} %rest_kernel.1.mine_far, ...), custom_call_target="tpu_custom_call" | custom-call | tf_op jit(solution)/shard_map/dispatch_kernel/pallas_call | solution.py:300
  49.2 47.0 %all_to_all.5 = bf16[256,8,256]{2,1,0:T(8,128)(2,1)S(1)} all-to-all(bf16[256,8,256]{2,1,0:T(8,128)(2,1)S(1)} %bitcast.10), channel_id=1, replica_groups={{0,2,4,6,8,10,12,14,16,18,20,22,24,26,28,30,32,34,36,38,40,42,44,46,48,..., dimensions={0} | all-to-all | bytes 2097152 | tf_op jit(solution)/shard_map/all_to_all | solution.py:315
  96.2 0.9 collect_kernel.1
  (9 shorter events, 0.2 us)
Async XLA Ops:
  0.0 27.1 %copy-start = (s32[64,50]{0,1:T(8,128)S(1)}, s32[64,50]{0,1:T(8,128)}, u32[]{:S(2)}) copy-start(s32[64,50]{0,1:T(8,128)} %param.8) | copy-start | bytes 38404
  0.0 26.7 %copy-start.2 = (s32[64,2,5,5]{0,1,3,2:T(2,128)S(1)}, s32[64,2,5,5]{0,1,3,2:T(2,128)}, u32[]{:S(2)}) copy-start(s32[64,2,5,5]{0,1,3,2:T(2,128)} %param.7) | copy-start | bytes 38404
  2.6 8.5 %collective-permute-start.1 = (bf16[320,64]{1,0:T(8,128)(2,1)S(1)}, bf16[320,64]{1,0:T(8,128)(2,1)S(1)}, u32[]{:S(2)}, u32[]{:S(2)}) collective-permute-start(bf16[320,64]{1,0:T(8,128)(2,1)S(1)} %across_kernel.1.across), channel_id=1, source_target_pairs={{1,2},{3,4},{5,6},{2,1},{4,3},{6,5},{9,10},{11,12},{13,14},{10,9},... | collective-permute-start | bytes 122888 | tf_op jit(solution)/shard_map/ppermute | solution.py:229
  3.2 0.7 copy-start.1
  4.3 6.8 %collective-permute-start = (bf16[320,64]{1,0:T(8,128)(2,1)S(1)}, bf16[320,64]{1,0:T(8,128)(2,1)S(1)}, u32[]{:S(2)}, u32[]{:S(2)}) collective-permute-start(bf16[320,64]{1,0:T(8,128)(2,1)S(1)} %get-tuple-element.13), channel_id=1, source_target_pairs={{0,1},{2,3},{4,5},{6,7},{1,0},{3,2},{5,4},{7,6},{8,9},{10,11},{12,... | collective-permute-start | bytes 122888 | tf_op jit(solution)/shard_map/ppermute | solution.py:229
  11.7 29.0 %collective-permute-start.2 = (bf16[336,1024]{1,0:T(8,128)(2,1)S(1)}, bf16[336,1024]{1,0:T(8,128)(2,1)S(1)}, u32[]{:S(2)}, u32[]{:S(2)}) collective-permute-start(bf16[336,1024]{1,0:T(8,128)(2,1)S(1)} %whiten_kernel.1.white.here), channel_id=1, source_target_pairs={{0,8},{8,16},{16,24},{24,32},{32,40},{40,48},{48,56},{56,64},{64,7... | collective-permute-start | bytes 2064392 | tf_op jit(solution)/shard_map/ppermute | solution.py:224
  15.1 27.4 %collective-permute-start.3 = (bf16[336,1024]{1,0:T(8,128)(2,1)S(1)}, bf16[336,1024]{1,0:T(8,128)(2,1)S(1)}, u32[]{:S(2)}, u32[]{:S(2)}) collective-permute-start(bf16[336,1024]{1,0:T(8,128)(2,1)S(1)} %whiten_kernel.1.white.here), channel_id=1, source_target_pairs={{0,504},{8,0},{16,8},{24,16},{32,24},{40,32},{48,40},{56,48},{64,5... | collective-permute-start | bytes 2064392 | tf_op jit(solution)/shard_map/ppermute | solution.py:224
  43.7 4.2 %collective-permute-start.4 = (bf16[160,2560]{1,0:T(8,128)(2,1)S(1)}, bf16[160,2560]{1,0:T(8,128)(2,1)S(1)}, u32[]{:S(2)}, u32[]{:S(2)}) collective-permute-start(bf16[160,2560]{1,0:T(8,128)(2,1)S(1)} %get-tuple-element.20), channel_id=1, source_target_pairs={{0,1},{1,0},{2,3},{3,2},{4,5},{5,4},{6,7},{7,6},{8,9},{9,8},{10,11... | collective-permute-start | bytes 2457608 | tf_op jit(solution)/shard_map/ppermute | solution.py:298

commit v5 on v4

--- a/solution.py
+++ b/solution.py
@@ -66,17 +66,20 @@
         out[rows, :] = edge(raw, rows, odd[0])
 
 
-def inside_kernel(odd, raw, across, valid, out, tail, columns, wide):
+def inside_kernel(odd, raw, across, out):
     for start in range(0, CH, SB):
         rows = slice(start, start + SB)
         out[rows, :] = edge(raw, rows, 1 - odd[0])
+
+
+def validity_kernel(inside, valid, tail, columns, wide):
     wide[...] = jnp.zeros_like(wide)
     wide[:2, :CH] = valid[...].astype(jnp.float32)
     tail[...] = wide[...].astype(jnp.bfloat16)
     columns[...] = wide[:8, :WIDE].T
 
 
-def whiten_kernel(spot, raw, inside, across, tail, columns, table, out, level, window):
+def whiten_kernel(spot, raw, across, inside, tail, columns, table, out, level, window):
     out[CH:, :] = tail[...]
     weights = columns[...]
     odd = lax.rem(spot[0], 2)
@@ -164,48 +167,48 @@
     theirs[...] = tile[HALF_ROWS:]
 
 
-def far_kernel(rows, after, near, table, theirs, right):
+def far_kernel(rows, after, table, near_other, near_gain, mine, theirs, right):
     rotate(after, table, right)
-    theirs[:, :COLS] = near[...]
-    theirs[:, COLS:] = product(rows[HALF_ROWS:, :], right[...]).astype(jnp.bfloat16)
-
-
-def rest_kernel(rows, right, mine):
-    mine[...] = product(rows[:HALF_ROWS, :], right[...]).astype(jnp.bfloat16)
-
-
-def gains_kernel(odd, before, here, after, out, left, right):
-    def valid(block):
-        return block[CH : CH + 16, : PARTS * 128].astype(jnp.float32)[:8]
-
-    place(left, odd[0], valid(before).T)
-    for d, block in enumerate((here, after)):
-        flags = valid(block)
-        for v in range(SUB):
-            chunk = flags[:, v * SB : (v + 1) * SB]
-            right[:, d * COLS + v * LAGS * SB : d * COLS + (v + 1) * LAGS * SB] = (
-                jnp.concatenate([chunk] * LAGS, axis=1)
-            )
+    tile = product(rows[...], right[...]).astype(jnp.bfloat16)
+    mine[...] = tile[:HALF_ROWS]
+    theirs[...] = tile[HALF_ROWS:]
+
+
+def gains_kernel(odd, before, block, near, out, left, right):
+    def flags(x):
+        return x[CH : CH + 16, :WIDE].astype(jnp.float32)[:8]
+
+    place(left, odd[0], flags(before).T)
+    valid = flags(block)
+    for v in range(SUB):
+        chunk = valid[:, v * SB : (v + 1) * SB]
+        right[:, v * LAGS * SB : (v + 1) * LAGS * SB] = jnp.concatenate([chunk] * LAGS, axis=1)
     joint = jnp.dot(left[:HALF_ROWS, :], right[...], preferred_element_type=jnp.float32)
     out[...] = jnp.where(joint > 1.5, (2 * FREQS) ** -0.5, FREQS**-0.5)
 
 
-def dispatch_kernel(place_of, listed, mine, mine_far, other, gain, out, total):
+def dispatch(place_of, listed, d, ours, other, gain, out, total):
+    total[...] = (ours[...].astype(jnp.float32) + other[...].astype(jnp.float32)) * gain[...]
+    for u in range(SUB):
+        for v in range(SUB):
+            slot = (d * SUB + u) * SUB + v
+
+            @pl.when(listed[slot] > 0)
+            def _():
+                for chip in range(CHIPS):
+                    out[place_of[slot], chip] = total[
+                        chip * ROWS + u * SHARE : chip * ROWS + (u + 1) * SHARE,
+                        v * LAGS * SB : (v + 1) * LAGS * SB,
+                    ].astype(jnp.bfloat16)
+
+
+def near_dispatch_kernel(place_of, listed, ours, other, gain, theirs, out, total):
     out[...] = jnp.zeros_like(out)
-    for d, ours in enumerate((mine, mine_far)):
-        lanes = slice(d * COLS, (d + 1) * COLS)
-        pair = ours[...].astype(jnp.float32) + other[:, lanes].astype(jnp.float32)
-        total[:, lanes] = pair * gain[:, lanes]
-    for slot in range(REACH * SUB * SUB):
-        d, u, v = slot // (SUB * SUB), slot // SUB % SUB, slot % SUB
-
-        @pl.when(listed[slot] > 0)
-        def _():
-            for chip in range(CHIPS):
-                out[place_of[slot], chip] = total[
-                    chip * ROWS + u * SHARE : chip * ROWS + (u + 1) * SHARE,
-                    d * COLS + v * LAGS * SB : d * COLS + (v + 1) * LAGS * SB,
-                ].astype(jnp.bfloat16)
+    dispatch(place_of, listed, 0, ours, other, gain, out, total)
+
+
+def far_dispatch_kernel(place_of, listed, ours, other, gain, near, out, total):
+    dispatch(place_of, listed, 1, ours, other, gain, out, total)
 
 
 def collect_kernel(received, out):
@@ -233,7 +236,7 @@
     return jax.ShapeDtypeStruct(shape, jnp.bfloat16)
 
 
-def kernel(fn, out_shape, inputs, scratch=(), scalars=0, mib=8):
+def kernel(fn, out_shape, inputs, scratch=(), scalars=0, mib=8, aliases=()):
     return pl.pallas_call(
         fn,
         out_shape=out_shape,
@@ -241,6 +244,7 @@
         out_specs=jax.tree.map(lambda _: VMEM, out_shape),
         scratch_shapes=[pltpu.VMEM(shape, dtype) for shape, dtype in scratch],
         compiler_params=pltpu.CompilerParams(vmem_limit_bytes=mib * MIB),
+        input_output_aliases=dict(aliases),
         name=fn.__name__,
     )
 
@@ -254,35 +258,26 @@
     edges = bf16(CH, 2 * HALF)
     to_across = kernel(across_kernel, edges, 2, scalars=1)(odd, raw)
     across = swap(to_across, 1)
-    to_inside, tail, columns = kernel(
-        inside_kernel,
-        (edges, bf16(16, PARTS * BAND), jax.ShapeDtypeStruct((WIDE, 8), f32)),
-        4,
+    to_inside = kernel(inside_kernel, edges, 3, scalars=1)(odd, raw, to_across)
+    tail, columns = kernel(
+        validity_kernel,
+        (bf16(16, PARTS * BAND), jax.ShapeDtypeStruct((WIDE, 8), f32)),
+        2,
         [((16, PARTS * BAND), f32)],
-        scalars=1,
-    )(odd, raw, to_across, validity.T)
+    )(to_inside, validity.T)
     inside = swap(to_inside, 0)
     block = bf16(CH + 16, PARTS * BAND)
     white = kernel(
         whiten_kernel, block, 7, [((CH, BAND), jnp.bfloat16), ((CH, BAND), f32)], scalars=1
-    )(freq[None], raw, inside, across, tail, columns, table)
+    )(freq[None], raw, across, inside, tail, columns, table)
     after = ring(white, "chan", -1)
     before = ring(white, "chan", 1)
     right_here = kernel(rotate_kernel, bf16(COLS, PARTS * BAND), 2)(white, table)
-
-    gain = kernel(
-        gains_kernel,
-        jax.ShapeDtypeStruct((HALF_ROWS, REACH * COLS), f32),
-        4,
-        [((2 * HALF_ROWS, 8), f32), ((8, REACH * COLS), f32)],
-        scalars=1,
-    )(odd, before, white, after)
 
     source = (chan + BLOCKS - 1) % BLOCKS
     listed = pair_mask[source].reshape(-1)
     place_of = owners[source]
     half = bf16(HALF_ROWS, COLS)
-    right = bf16(COLS, PARTS * BAND)
     rows, mine, near = kernel(
         near_kernel,
         (bf16(2 * HALF_ROWS, PARTS * BAND), half, half),
@@ -291,19 +286,31 @@
         scalars=3,
         mib=10,
     )(odd, place_of, listed, before, right_here)
-    theirs, right_after = kernel(far_kernel, (bf16(HALF_ROWS, REACH * COLS), right), 4)(
-        rows, after, near, table
-    )
-    mine_far = kernel(rest_kernel, half, 2)(rows, right_after)
-    other = lax.ppermute(theirs, "freq", [(k, k ^ 1) for k in range(N_FREQ)])
-
-    outgoing = kernel(
-        dispatch_kernel,
-        bf16(BLOCKS, CHIPS, SHARE, LAGS * SB),
-        6,
-        [((HALF_ROWS, REACH * COLS), f32)],
-        scalars=2,
-    )(place_of, listed, mine, mine_far, other, gain)
+    def gain(block, mark):
+        return kernel(
+            gains_kernel,
+            jax.ShapeDtypeStruct((HALF_ROWS, COLS), f32),
+            4,
+            [((2 * HALF_ROWS, 8), f32), ((8, COLS), f32)],
+            scalars=1,
+        )(odd, before, block, mark)
+
+    pairs = [(k, k ^ 1) for k in range(N_FREQ)]
+    near_other = lax.ppermute(near, "freq", pairs)
+    near_gain = gain(white, near)
+    mine_far, theirs = kernel(
+        far_kernel, (half, half), 5, [((COLS, PARTS * BAND), jnp.bfloat16)]
+    )(rows, after, table, near_other, near_gain)
+    far_other = lax.ppermute(theirs, "freq", pairs)
+    far_gain = gain(after, theirs)
+    sending = bf16(BLOCKS, CHIPS, SHARE, LAGS * SB)
+    total = [((HALF_ROWS, COLS), f32)]
+    near_sent = kernel(near_dispatch_kernel, sending, 6, total, scalars=2)(
+        place_of, listed, mine, near_other, near_gain, theirs
+    )
+    outgoing = kernel(far_dispatch_kernel, sending, 6, total, scalars=2, aliases={5: 0})(
+        place_of, listed, mine_far, far_other, far_gain, near_sent
+    )
     groups = [
         [
             b * N_FREQ + 2 * chip + core

time: 97.5 us -> 96.8 us (level)
  blocking collectives: 47 us -> 44.5 us
  starting transfers between devices: 23.4 us -> 25.4 us
    all_to_all x1, blocking collectives: 47 us -> 44.5 us  [body(): lax.all_to_all(outgoing.reshape(BLOCKS * CHIPS, SHARE, LAGS * SB), ('chan...]
    ppermute x1 -> x2, starting transfers between devices: 1.92 us -> 3.97 us  [the longest x1 2.05 us: body(): far_other = lax.ppermute(theirs, 'freq', pairs)]
    pallas_call x5 -> x7, Pallas kernels: 4.29 us -> 4.03 us  [the longest x1 1.09 us: body(): kernel(far_kernel, (half, half), 5, [((COLS, PARTS * BAND), jnp.bfloat16)])]
  transfers between devices with their start and end apart: 5 -> 6, of which waited for: 3 -> 4; matrix products, arithmetic and copies ran while one was open for 1% -> 1% of each run, Pallas kernels for 4% -> 5%
where the time goes in v5:
time: 96.8 us; the launch traced here: 96.4 us
  blocking collectives  44.5 us (46%)
  starting transfers between devices  25.4 us (26%)
  waiting for transfers between devices  14.6 us (15%)
  Pallas kernels  8.22 us (8%)
  local copies, waits for them, and re-layouts  3.48 us (4%)
    all_to_all x1, blocking collectives, body(): lax.all_to_all(outgoing.reshape(BLOCKS * CHIPS, SHARE, LAGS * SB), ('chan...  44.5 us
    ppermute x2, starting transfers between devices, ring(): lax.ppermute(x, axis, [(i, (i + step) % count) for i in range(count)])  14.9 us
    ppermute x2, waiting for transfers between devices, ring(): lax.ppermute(x, axis, [(i, (i + step) % count) for i in range(count)])  12.9 us
    ppermute x2, starting transfers between devices, swap(): return lax.ppermute(x, 'freq', pairs + [(k, i) for i, k in pairs])  6.52 us
    reshape x1, local copies, waits for them, and re-layouts, body(): raw = spectra.reshape(CH, PARTS * BAND)  2.24 us
    ppermute x1, starting transfers between devices, body(): far_other = lax.ppermute(theirs, 'freq', pairs)  2.05 us
  transfers between devices with their start and end apart: 6, of which 4 were waited for; matrix products, arithmetic and copies ran while one was open for 1% of the time, Pallas kernels for 5%

profile of v5, /device:TPU:8, one launch (start us, length us, event | category | flops | bytes accessed | tf_op | source)
XLA Modules:
  0.0 96.4 jit_solution(1700627714673999623)
XLA Ops:
  0.0 2.2 %reshape.9.raw = bf16[320,1024]{1,0:T(8,128)(2,1)S(1)} reshape(bf16[320,2,2,256]{3,2,1,0:T(2,128)(2,1)} %param.5) | data formatting | bytes 1310720 | tf_op jit(solution)/shard_map/reshape | solution.py:257
  2.3 0.3 across_kernel.1.across
  2.6 0.7 collective-permute-start
  3.3 0.3 inside_kernel.1.inside
  3.6 5.9 %collective-permute-start.1 = (bf16[320,64]{1,0:T(8,128)(2,1)S(1)}, bf16[320,64]{1,0:T(8,128)(2,1)S(1)}, u32[]{:S(2)}, u32[]{:S(2)}) collective-permute-start(bf16[320,64]{1,0:T(8,128)(2,1)S(1)} %inside_kernel.1.inside), channel_id=1, source_target_pairs={{0,1},{2,3},{4,5},{6,7},{1,0},{3,2},{5,4},{7,6},{8,9},{10,11},{12,... | collective-permute-start | bytes 122888 | tf_op jit(solution)/shard_map/ppermute | solution.py:232
  9.4 0.7 dynamic-slice_bitcast_fusion.table
  10.3 0.6 whiten_kernel.1.white.block
  11.0 3.4 %collective-permute-start.2 = (bf16[336,1024]{1,0:T(8,128)(2,1)S(1)}, bf16[336,1024]{1,0:T(8,128)(2,1)S(1)}, u32[]{:S(2)}, u32[]{:S(2)}) collective-permute-start(bf16[336,1024]{1,0:T(8,128)(2,1)S(1)} %whiten_kernel.1.white.block), channel_id=1, source_target_pairs={{0,8},{8,16},{16,24},{24,32},{32,40},{40,48},{48,56},{56,64},{64,7... | collective-permute-start | bytes 2064392 | tf_op jit(solution)/shard_map/ppermute | solution.py:227
  14.4 11.6 %collective-permute-start.3 = (bf16[336,1024]{1,0:T(8,128)(2,1)S(1)}, bf16[336,1024]{1,0:T(8,128)(2,1)S(1)}, u32[]{:S(2)}, u32[]{:S(2)}) collective-permute-start(bf16[336,1024]{1,0:T(8,128)(2,1)S(1)} %whiten_kernel.1.white.block), channel_id=1, source_target_pairs={{0,504},{8,0},{16,8},{24,16},{32,24},{40,32},{48,40},{56,48},{64,5... | collective-permute-start | bytes 2064392 | tf_op jit(solution)/shard_map/ppermute | solution.py:227
  26.1 0.2 copy.9
  26.5 0.5 rotate_kernel.1.right
  27.1 12.9 %collective-permute-done.2.before = bf16[336,1024]{1,0:T(8,128)(2,1)S(1)} collective-permute-done((bf16[336,1024]{1,0:T(8,128)(2,1)S(1)}, bf16[336,1024]{1,0:T(8,128)(2,1)S(1)}, u32[]{:S(2)}, u32[]{:S(2)}) %collective-permute-start.2) | collective-permute-done | bytes 688160 | tf_op jit(solution)/shard_map/ppermute | solution.py:227
  39.9 1.8 %near_kernel.1 = (bf16[320,1024]{1,0:T(8,128)(2,1)S(1)}, bf16[160,1280]{1,0:T(8,128)(2,1)S(1)}, bf16[160,1280]{1,0:T(8,128)(2,1)S(1)}) custom-call(s32[1]{0:T(128)} %bitcast.odd, s32[50]{0:T(128)S(1)} %dynamic-slice_reduce_fusion.place_of, s32[50]{0:T(128)S(1)} %reshape_squeeze.3.listed, bf16[336,1024]{1,0:T(8,128)(2,1)S(1)} %collective-permute-done.2.before, ...), custom_call_target="tpu_custom_call" | custom-call | tf_op jit(solution)/shard_map/near_kernel/pallas_call | solution.py:281
  41.7 1.9 %collective-permute-start.4 = (bf16[160,1280]{1,0:T(8,128)(2,1)S(1)}, bf16[160,1280]{1,0:T(8,128)(2,1)S(1)}, u32[]{:S(2)}, u32[]{:S(2)}) collective-permute-start(bf16[160,1280]{1,0:T(8,128)(2,1)S(1)} %get-tuple-element.15.near), channel_id=1, source_target_pairs={{0,1},{1,0},{2,3},{3,2},{4,5},{5,4},{6,7},{7,6},{8,9},{9,8},{10,11... | collective-permute-start | bytes 1228808 | tf_op jit(solution)/shard_map/ppermute | solution.py:299
  43.7 0.4 gains_kernel.2.near_gain.gain
  44.0 1.3 %collective-permute-done.4.near_other.other = bf16[160,1280]{1,0:T(8,128)(2,1)S(1)} collective-permute-done((bf16[160,1280]{1,0:T(8,128)(2,1)S(1)}, bf16[160,1280]{1,0:T(8,128)(2,1)S(1)}, u32[]{:S(2)}, u32[]{:S(2)}) %collective-permute-start.4) | collective-permute-done | bytes 409632 | tf_op jit(solution)/shard_map/ppermute | solution.py:299
  45.4 1.1 %far_kernel.1 = (bf16[160,1280]{1,0:T(8,128)(2,1)S(1)}, bf16[160,1280]{1,0:T(8,128)(2,1)S(1)}) custom-call(bf16[320,1024]{1,0:T(8,128)(2,1)S(1)} %get-tuple-element.14.rows, bf16[336,1024]{1,0:T(8,128)(2,1)S(1)} %collective-permute-done.3.after.block, f32[8,256]{1,0:T(8,128)S(1)} %dynamic-slice_bitcast_fusion.table, ...), custom_call_target="tpu_custom_call" | custom-call | tf_op jit(solution)/shard_map/far_kernel/pallas_call | solution.py:301
  46.5 2.0 %collective-permute-start.5 = (bf16[160,1280]{1,0:T(8,128)(2,1)S(1)}, bf16[160,1280]{1,0:T(8,128)(2,1)S(1)}, u32[]{:S(2)}, u32[]{:S(2)}) collective-permute-start(bf16[160,1280]{1,0:T(8,128)(2,1)S(1)} %get-tuple-element.17.near.theirs), channel_id=1, source_target_pairs={{0,1},{1,0},{2,3},{3,2},{4,5},{5,4},{6,7},{7,6},{8,9},{9,8},{10,11... | collective-permute-start | bytes 1228808 | tf_op jit(solution)/shard_map/ppermute | solution.py:304
  48.5 0.4 gains_kernel.3.gain
  48.9 0.9 near_dispatch_kernel.1.near
  49.8 0.3 collective-permute-done.5.other
  50.1 0.9 far_dispatch_kernel.1
  51.0 44.5 %all_to_all.5 = bf16[256,8,256]{2,1,0:T(8,128)(2,1)S(1)} all-to-all(bf16[256,8,256]{2,1,0:T(8,128)(2,1)S(1)} %bitcast.10), channel_id=1, replica_groups={{0,2,4,6,8,10,12,14,16,18,20,22,24,26,28,30,32,34,36,38,40,42,44,46,48,..., dimensions={0} | all-to-all | bytes 2097152 | tf_op jit(solution)/shard_map/all_to_all | solution.py:322
  95.5 0.9 collect_kernel.1
  (13 shorter events, 0.6 us)
Async XLA Ops:
  0.0 26.3 %copy-start = (s32[64,50]{0,1:T(8,128)S(1)}, s32[64,50]{0,1:T(8,128)}, u32[]{:S(2)}) copy-start(s32[64,50]{0,1:T(8,128)} %param.8) | copy-start | bytes 38404
  0.0 10.1 %copy-start.1 = (s32[320,2]{0,1:T(2,128)S(1)}, s32[320,2]{0,1:T(2,128)}, u32[]{:S(2)}) copy-start(s32[320,2]{0,1:T(2,128)} %param.6) | copy-start | bytes 7684
  0.0 25.9 %copy-start.2 = (s32[64,2,5,5]{0,1,3,2:T(2,128)S(1)}, s32[64,2,5,5]{0,1,3,2:T(2,128)}, u32[]{:S(2)}) copy-start(s32[64,2,5,5]{0,1,3,2:T(2,128)} %param.7) | copy-start | bytes 38404
  2.6 7.8 %collective-permute-start = (bf16[320,64]{1,0:T(8,128)(2,1)S(1)}, bf16[320,64]{1,0:T(8,128)(2,1)S(1)}, u32[]{:S(2)}, u32[]{:S(2)}) collective-permute-start(bf16[320,64]{1,0:T(8,128)(2,1)S(1)} %across_kernel.1.across), channel_id=1, source_target_pairs={{1,2},{3,4},{5,6},{2,1},{4,3},{6,5},{9,10},{11,12},{13,14},{10,9},... | collective-permute-start | bytes 122888 | tf_op jit(solution)/shard_map/ppermute | solution.py:232
  3.6 6.8 %collective-permute-start.1 = (bf16[320,64]{1,0:T(8,128)(2,1)S(1)}, bf16[320,64]{1,0:T(8,128)(2,1)S(1)}, u32[]{:S(2)}, u32[]{:S(2)}) collective-permute-start(bf16[320,64]{1,0:T(8,128)(2,1)S(1)} %inside_kernel.1.inside), channel_id=1, source_target_pairs={{0,1},{2,3},{4,5},{6,7},{1,0},{3,2},{5,4},{7,6},{8,9},{10,11},{12,... | collective-permute-start | bytes 122888 | tf_op jit(solution)/shard_map/ppermute | solution.py:232
  11.0 29.0 %collective-permute-start.2 = (bf16[336,1024]{1,0:T(8,128)(2,1)S(1)}, bf16[336,1024]{1,0:T(8,128)(2,1)S(1)}, u32[]{:S(2)}, u32[]{:S(2)}) collective-permute-start(bf16[336,1024]{1,0:T(8,128)(2,1)S(1)} %whiten_kernel.1.white.block), channel_id=1, source_target_pairs={{0,8},{8,16},{16,24},{24,32},{32,40},{40,48},{48,56},{56,64},{64,7... | collective-permute-start | bytes 2064392 | tf_op jit(solution)/shard_map/ppermute | solution.py:227
  14.4 29.6 %collective-permute-start.3 = (bf16[336,1024]{1,0:T(8,128)(2,1)S(1)}, bf16[336,1024]{1,0:T(8,128)(2,1)S(1)}, u32[]{:S(2)}, u32[]{:S(2)}) collective-permute-start(bf16[336,1024]{1,0:T(8,128)(2,1)S(1)} %whiten_kernel.1.white.block), channel_id=1, source_target_pairs={{0,504},{8,0},{16,8},{24,16},{32,24},{40,32},{48,40},{56,48},{64,5... | collective-permute-start | bytes 2064392 | tf_op jit(solution)/shard_map/ppermute | solution.py:227
  41.7 3.6 %collective-permute-start.4 = (bf16[160,1280]{1,0:T(8,128)(2,1)S(1)}, bf16[160,1280]{1,0:T(8,128)(2,1)S(1)}, u32[]{:S(2)}, u32[]{:S(2)}) collective-permute-start(bf16[160,1280]{1,0:T(8,128)(2,1)S(1)} %get-tuple-element.15.near), channel_id=1, source_target_pairs={{0,1},{1,0},{2,3},{3,2},{4,5},{5,4},{6,7},{7,6},{8,9},{9,8},{10,11... | collective-permute-start | bytes 1228808 | tf_op jit(solution)/shard_map/ppermute | solution.py:299
  46.5 3.6 %collective-permute-start.5 = (bf16[160,1280]{1,0:T(8,128)(2,1)S(1)}, bf16[160,1280]{1,0:T(8,128)(2,1)S(1)}, u32[]{:S(2)}, u32[]{:S(2)}) collective-permute-start(bf16[160,1280]{1,0:T(8,128)(2,1)S(1)} %get-tuple-element.17.near.theirs), channel_id=1, source_target_pairs={{0,1},{1,0},{2,3},{3,2},{4,5},{5,4},{6,7},{7,6},{8,9},{9,8},{10,11... | collective-permute-start | bytes 1228808 | tf_op jit(solution)/shard_map/ppermute | solution.py:304

commit v6 on v4

--- a/solution.py
+++ b/solution.py
@@ -66,17 +66,20 @@
         out[rows, :] = edge(raw, rows, odd[0])
 
 
-def inside_kernel(odd, raw, across, valid, out, tail, columns, wide):
+def inside_kernel(odd, raw, across, out):
     for start in range(0, CH, SB):
         rows = slice(start, start + SB)
         out[rows, :] = edge(raw, rows, 1 - odd[0])
+
+
+def validity_kernel(inside, valid, tail, columns, wide):
     wide[...] = jnp.zeros_like(wide)
     wide[:2, :CH] = valid[...].astype(jnp.float32)
     tail[...] = wide[...].astype(jnp.bfloat16)
     columns[...] = wide[:8, :WIDE].T
 
 
-def whiten_kernel(spot, raw, inside, across, tail, columns, table, out, level, window):
+def whiten_kernel(spot, raw, across, inside, tail, columns, table, out, level, window):
     out[CH:, :] = tail[...]
     weights = columns[...]
     odd = lax.rem(spot[0], 2)
@@ -116,32 +119,40 @@
             out[rows, i * BAND : (i + 1) * BAND] = white.astype(jnp.bfloat16)
 
 
-def rotate(white, table, out):
+def plain(block):
+    return lambda rows, lanes=slice(None): block[rows, lanes].astype(jnp.float32)
+
+
+def chosen(odd, even_block, odd_block):
+    def read(rows, lanes=slice(None)):
+        both = [x[rows, lanes].astype(jnp.float32) for x in (even_block, odd_block)]
+        return jnp.where(odd > 0, both[1], both[0])
+
+    return read
+
+
+def rotate(read, table, out):
     for u in range(SUB):
-        rows = slice(u * SB, (u + 1) * SB)
-        for lag in range(LAGS):
-            dest = slice((u * LAGS + lag) * SB, (u * LAGS + lag + 1) * SB)
-            if lag == LAGS // 2:
-                out[dest, :] = white[rows, :]
-                continue
-            cosine, sine = table[lag : lag + 1, :], table[4 + lag : 5 + lag, :]
-            for s in range(2):
-                real, imag = part(white, rows, s), part(white, rows, 2 + s)
-                out[dest, s * BAND : (s + 1) * BAND] = (
-                    real * cosine + imag * sine
-                ).astype(jnp.bfloat16)
-                out[dest, (2 + s) * BAND : (3 + s) * BAND] = (
-                    imag * cosine - real * sine
-                ).astype(jnp.bfloat16)
+        for s in range(2):
+            lanes = [slice(i * BAND, (i + 1) * BAND) for i in (s, 2 + s)]
+            real, imag = (read(slice(u * SB, (u + 1) * SB), x) for x in lanes)
+            for lag in range(LAGS):
+                dest = slice((u * LAGS + lag) * SB, (u * LAGS + lag + 1) * SB)
+                turned = real, imag
+                if lag != LAGS // 2:
+                    cosine, sine = table[lag : lag + 1, :], table[4 + lag : 5 + lag, :]
+                    turned = real * cosine + imag * sine, imag * cosine - real * sine
+                for x, value in zip(lanes, turned):
+                    out[dest, x] = value.astype(jnp.bfloat16)
 
 
 def rotate_kernel(white, table, out):
-    rotate(white, table, out)
-
-
-def place(out, odd, block):
+    rotate(plain(white), table, out)
+
+
+def place(out, odd, read):
     for u in range(SUB):
-        wide = block[u * SB : (u + 1) * SB, :].astype(jnp.float32)
+        wide = read(slice(u * SB, (u + 1) * SB))
         for target in range(N_FREQ):
             half = lax.rem(odd + target, 2)
             row = half * HALF_ROWS + (target // 2) * ROWS + u * SHARE
@@ -156,33 +167,41 @@
     )
 
 
-def near_kernel(odd, place_of, listed, before, right, rows, mine, theirs, left):
-    place(left, odd[0], before)
-    rows[...] = left[...].astype(jnp.bfloat16)
-    tile = product(rows[...], right[...]).astype(jnp.bfloat16)
-    mine[...] = tile[:HALF_ROWS]
-    theirs[...] = tile[HALF_ROWS:]
-
-
-def far_kernel(rows, after, near, table, theirs, right):
-    rotate(after, table, right)
-    theirs[:, :COLS] = near[...]
-    theirs[:, COLS:] = product(rows[HALF_ROWS:, :], right[...]).astype(jnp.bfloat16)
-
-
-def rest_kernel(rows, right, mine):
-    mine[...] = product(rows[:HALF_ROWS, :], right[...]).astype(jnp.bfloat16)
-
-
-def gains_kernel(odd, before, here, after, out, left, right):
-    def valid(block):
-        return block[CH : CH + 16, : PARTS * 128].astype(jnp.float32)[:8]
-
-    place(left, odd[0], valid(before).T)
-    for d, block in enumerate((here, after)):
-        flags = valid(block)
+def prepare(odd, behind, block, table, left, right_after):
+    @pl.when(behind)
+    def _():
+        place(left, odd, plain(block))
+
+    @pl.when(jnp.logical_not(behind))
+    def _():
+        rotate(plain(block), table, right_after)
+
+
+def first_kernel(odd, place_of, listed, first, right_here, table, left, right_after):
+    prepare(odd[0], odd[0] == 0, first, table, left, right_after)
+
+
+def second_kernel(
+    odd, left_in, right_in, second, right_here, table, left, right_after, mine, theirs
+):
+    prepare(odd[0], odd[0] != 0, second, table, left, right_after)
+    rows = left[...].astype(jnp.bfloat16)
+    for d, right in enumerate((right_here, right_after)):
+        tile = product(rows, right[...]).astype(jnp.bfloat16)
+        mine[:, d * COLS : (d + 1) * COLS] = tile[:HALF_ROWS]
+        theirs[:, d * COLS : (d + 1) * COLS] = tile[HALF_ROWS:]
+
+
+def gains_kernel(odd, first, here, second, theirs, out, left, right):
+    def flags(read):
+        return read(slice(CH, CH + 16), slice(0, WIDE))[:8]
+
+    columns = flags(chosen(odd[0], first, second)).T
+    place(left, odd[0], lambda rows: columns[rows])
+    for d, read in enumerate((plain(here), chosen(odd[0], second, first))):
+        valid = flags(read)
         for v in range(SUB):
-            chunk = flags[:, v * SB : (v + 1) * SB]
+            chunk = valid[:, v * SB : (v + 1) * SB]
             right[:, d * COLS + v * LAGS * SB : d * COLS + (v + 1) * LAGS * SB] = (
                 jnp.concatenate([chunk] * LAGS, axis=1)
             )
@@ -190,12 +209,9 @@
     out[...] = jnp.where(joint > 1.5, (2 * FREQS) ** -0.5, FREQS**-0.5)
 
 
-def dispatch_kernel(place_of, listed, mine, mine_far, other, gain, out, total):
+def dispatch_kernel(place_of, listed, mine, other, gain, out, total):
     out[...] = jnp.zeros_like(out)
-    for d, ours in enumerate((mine, mine_far)):
-        lanes = slice(d * COLS, (d + 1) * COLS)
-        pair = ours[...].astype(jnp.float32) + other[:, lanes].astype(jnp.float32)
-        total[:, lanes] = pair * gain[:, lanes]
+    total[...] = (mine[...].astype(jnp.float32) + other[...].astype(jnp.float32)) * gain[...]
     for slot in range(REACH * SUB * SUB):
         d, u, v = slot // (SUB * SUB), slot // SUB % SUB, slot % SUB
 
@@ -219,9 +235,13 @@
     lax.fori_loop(0, BLOCKS, block, None, unroll=8)
 
 
-def ring(x, axis, step):
-    count = lax.axis_size(axis)
-    return lax.ppermute(x, axis, [(i, (i + step) % count) for i in range(count)])
+def spread(x, forward):
+    route = [
+        (b * N_FREQ + k, (b + (1 if k % 2 == forward else -1)) % BLOCKS * N_FREQ + k)
+        for b in range(BLOCKS)
+        for k in range(N_FREQ)
+    ]
+    return lax.ppermute(x, ("chan", "freq"), route)
 
 
 def swap(x, first):
@@ -233,7 +253,7 @@
     return jax.ShapeDtypeStruct(shape, jnp.bfloat16)
 
 
-def kernel(fn, out_shape, inputs, scratch=(), scalars=0, mib=8):
+def kernel(fn, out_shape, inputs, scratch=(), scalars=0, mib=8, aliases=()):
     return pl.pallas_call(
         fn,
         out_shape=out_shape,
@@ -241,6 +261,7 @@
         out_specs=jax.tree.map(lambda _: VMEM, out_shape),
         scratch_shapes=[pltpu.VMEM(shape, dtype) for shape, dtype in scratch],
         compiler_params=pltpu.CompilerParams(vmem_limit_bytes=mib * MIB),
+        input_output_aliases=dict(aliases),
         name=fn.__name__,
     )
 
@@ -254,56 +275,51 @@
     edges = bf16(CH, 2 * HALF)
     to_across = kernel(across_kernel, edges, 2, scalars=1)(odd, raw)
     across = swap(to_across, 1)
-    to_inside, tail, columns = kernel(
-        inside_kernel,
-        (edges, bf16(16, PARTS * BAND), jax.ShapeDtypeStruct((WIDE, 8), f32)),
-        4,
+    to_inside = kernel(inside_kernel, edges, 3, scalars=1)(odd, raw, to_across)
+    tail, columns = kernel(
+        validity_kernel,
+        (bf16(16, PARTS * BAND), jax.ShapeDtypeStruct((WIDE, 8), f32)),
+        2,
         [((16, PARTS * BAND), f32)],
-        scalars=1,
-    )(odd, raw, to_across, validity.T)
+    )(to_inside, validity.T)
     inside = swap(to_inside, 0)
     block = bf16(CH + 16, PARTS * BAND)
     white = kernel(
         whiten_kernel, block, 7, [((CH, BAND), jnp.bfloat16), ((CH, BAND), f32)], scalars=1
-    )(freq[None], raw, inside, across, tail, columns, table)
-    after = ring(white, "chan", -1)
-    before = ring(white, "chan", 1)
+    )(freq[None], raw, across, inside, tail, columns, table)
+    first = spread(white, 0)
+    second = spread(white, 1)
     right_here = kernel(rotate_kernel, bf16(COLS, PARTS * BAND), 2)(white, table)
 
+    source = (chan + BLOCKS - 1) % BLOCKS
+    listed = pair_mask[source].reshape(-1)
+    place_of = owners[source]
+    half = bf16(HALF_ROWS, REACH * COLS)
+    kept = (
+        jax.ShapeDtypeStruct((2 * HALF_ROWS, PARTS * BAND), f32),
+        bf16(COLS, PARTS * BAND),
+    )
+    left, right_after = kernel(first_kernel, kept, 6, scalars=3)(
+        odd, place_of, listed, first, right_here, table
+    )
+    _, _, mine, theirs = kernel(
+        second_kernel, (*kept, half, half), 6, scalars=1, aliases={1: 0, 2: 1}
+    )(odd, left, right_after, second, right_here, table)
+    other = lax.ppermute(theirs, "freq", [(k, k ^ 1) for k in range(N_FREQ)])
     gain = kernel(
         gains_kernel,
         jax.ShapeDtypeStruct((HALF_ROWS, REACH * COLS), f32),
-        4,
+        5,
         [((2 * HALF_ROWS, 8), f32), ((8, REACH * COLS), f32)],
         scalars=1,
-    )(odd, before, white, after)
-
-    source = (chan + BLOCKS - 1) % BLOCKS
-    listed = pair_mask[source].reshape(-1)
-    place_of = owners[source]
-    half = bf16(HALF_ROWS, COLS)
-    right = bf16(COLS, PARTS * BAND)
-    rows, mine, near = kernel(
-        near_kernel,
-        (bf16(2 * HALF_ROWS, PARTS * BAND), half, half),
-        5,
-        [((2 * HALF_ROWS, PARTS * BAND), f32)],
-        scalars=3,
-        mib=10,
-    )(odd, place_of, listed, before, right_here)
-    theirs, right_after = kernel(far_kernel, (bf16(HALF_ROWS, REACH * COLS), right), 4)(
-        rows, after, near, table
-    )
-    mine_far = kernel(rest_kernel, half, 2)(rows, right_after)
-    other = lax.ppermute(theirs, "freq", [(k, k ^ 1) for k in range(N_FREQ)])
-
+    )(odd, first, white, second, theirs)
     outgoing = kernel(
         dispatch_kernel,
         bf16(BLOCKS, CHIPS, SHARE, LAGS * SB),
-        6,
+        5,
         [((HALF_ROWS, REACH * COLS), f32)],
         scalars=2,
-    )(place_of, listed, mine, mine_far, other, gain)
+    )(place_of, listed, mine, other, gain)
     groups = [
         [
             b * N_FREQ + 2 * chip + core

time: 97.5 us -> 96.7 us (level)
  blocking collectives: 47 us -> 48.2 us
    ppermute x2, waiting for transfers between devices: 12.9 us -> 11.5 us  [spread(): return lax.ppermute(x, ('chan', 'freq'), route)]
    all_to_all x1, blocking collectives: 47 us -> 48.2 us  [body(): lax.all_to_all(outgoing.reshape(BLOCKS * CHIPS, SHARE, LAGS * SB), ('chan...]
  transfers between devices with their start and end apart: 5 -> 5, of which waited for: 3 -> 4; matrix products, arithmetic and copies ran while one was open for 1% -> 1% of each run, Pallas kernels for 4% -> 2%
where the time goes in v6:
time: 96.7 us; the launch traced here: 96.4 us
  blocking collectives  48.2 us (50%)
  starting transfers between devices  23.9 us (25%)
  waiting for transfers between devices  13.1 us (14%)
  Pallas kernels  7.56 us (8%)
  local copies, waits for them, and re-layouts  3.48 us (4%)
    all_to_all x1, blocking collectives, body(): lax.all_to_all(outgoing.reshape(BLOCKS * CHIPS, SHARE, LAGS * SB), ('chan...  48.2 us
    ppermute x2, starting transfers between devices, spread(): return lax.ppermute(x, ('chan', 'freq'), route)  14.9 us
    ppermute x2, waiting for transfers between devices, spread(): return lax.ppermute(x, ('chan', 'freq'), route)  11.5 us
    ppermute x2, starting transfers between devices, swap(): return lax.ppermute(x, 'freq', pairs + [(k, i) for i, k in pairs])  6.52 us
    ppermute x1, starting transfers between devices, body(): other = lax.ppermute(theirs, 'freq', [(k, k ^ 1) for k in range(N_FREQ)])  2.41 us
    pallas_call x1, Pallas kernels, body(): kernel(second_kernel, (*kept, half, half), 6, scalars=1, aliases={1: 0, 2...  2.41 us
    reshape x1, local copies, waits for them, and re-layouts, body(): raw = spectra.reshape(CH, PARTS * BAND)  2.24 us
  transfers between devices with their start and end apart: 5, of which 4 were waited for; matrix products, arithmetic and copies ran while one was open for 1% of the time, Pallas kernels for 2%

profile of v6, /device:TPU:8, one launch (start us, length us, event | category | flops | bytes accessed | tf_op | source)
XLA Modules:
  0.0 96.4 jit_solution(3997349332574440628)
XLA Ops:
  0.0 2.2 %reshape.9.raw = bf16[320,1024]{1,0:T(8,128)(2,1)S(1)} reshape(bf16[320,2,2,256]{3,2,1,0:T(2,128)(2,1)} %param.5) | data formatting | bytes 1310720 | tf_op jit(solution)/shard_map/reshape | solution.py:274
  2.3 0.3 across_kernel.1.across
  2.6 0.7 collective-permute-start
  3.3 0.3 inside_kernel.1.inside
  3.6 5.9 %collective-permute-start.1 = (bf16[320,64]{1,0:T(8,128)(2,1)S(1)}, bf16[320,64]{1,0:T(8,128)(2,1)S(1)}, u32[]{:S(2)}, u32[]{:S(2)}) collective-permute-start(bf16[320,64]{1,0:T(8,128)(2,1)S(1)} %inside_kernel.1.inside), channel_id=1, source_target_pairs={{0,1},{2,3},{4,5},{6,7},{1,0},{3,2},{5,4},{7,6},{8,9},{10,11},{12,... | collective-permute-start | bytes 122888 | tf_op jit(solution)/shard_map/ppermute | solution.py:249
  9.4 0.7 dynamic-slice_bitcast_fusion.table
  10.1 0.1 validity_kernel.1
  10.3 0.6 whiten_kernel.1.white.here
  11.0 3.4 %collective-permute-start.2 = (bf16[336,1024]{1,0:T(8,128)(2,1)S(1)}, bf16[336,1024]{1,0:T(8,128)(2,1)S(1)}, u32[]{:S(2)}, u32[]{:S(2)}) collective-permute-start(bf16[336,1024]{1,0:T(8,128)(2,1)S(1)} %whiten_kernel.1.white.here), channel_id=1, source_target_pairs={{0,8},{1,505},{2,10},{3,507},{4,12},{5,509},{6,14},{7,511},{8,16},... | collective-permute-start | bytes 2064392 | tf_op jit(solution)/shard_map/ppermute | solution.py:244
  14.4 11.6 %collective-permute-start.3 = (bf16[336,1024]{1,0:T(8,128)(2,1)S(1)}, bf16[336,1024]{1,0:T(8,128)(2,1)S(1)}, u32[]{:S(2)}, u32[]{:S(2)}) collective-permute-start(bf16[336,1024]{1,0:T(8,128)(2,1)S(1)} %whiten_kernel.1.white.here), channel_id=1, source_target_pairs={{0,504},{1,9},{2,506},{3,11},{4,508},{5,13},{6,510},{7,15},{8,0},{... | collective-permute-start | bytes 2064392 | tf_op jit(solution)/shard_map/ppermute | solution.py:244
  26.0 0.1 constant_dynamic-slice_fusion
  26.1 0.2 copy.10
  26.3 0.2 dynamic-slice_reduce_fusion.place_of
  26.5 0.5 rotate_kernel.1.right_here
  27.0 5.9 %collective-permute-done.2.first = bf16[336,1024]{1,0:T(8,128)(2,1)S(1)} collective-permute-done((bf16[336,1024]{1,0:T(8,128)(2,1)S(1)}, bf16[336,1024]{1,0:T(8,128)(2,1)S(1)}, u32[]{:S(2)}, u32[]{:S(2)}) %collective-permute-start.2) | collective-permute-done | bytes 688160 | tf_op jit(solution)/shard_map/ppermute | solution.py:244
  33.0 0.6 first_kernel.1
  33.6 5.6 %collective-permute-done.3.second = bf16[336,1024]{1,0:T(8,128)(2,1)S(1)} collective-permute-done((bf16[336,1024]{1,0:T(8,128)(2,1)S(1)}, bf16[336,1024]{1,0:T(8,128)(2,1)S(1)}, u32[]{:S(2)}, u32[]{:S(2)}) %collective-permute-start.3) | collective-permute-done | bytes 688160 | tf_op jit(solution)/shard_map/ppermute | solution.py:244
  39.2 2.4 %second_kernel.1 = (f32[320,1024]{1,0:T(8,128)S(1)}, bf16[1280,1024]{1,0:T(8,128)(2,1)S(1)}, bf16[160,2560]{1,0:T(8,128)(2,1)S(1)}, bf16[160,2560]{1,0:T(8,128)(2,1)S(1)}) custom-call(s32[1]{0:T(128)} %bitcast.odd, f32[320,1024]{1,0:T(8,128)S(1)} %get-tuple-element.13.left_in, ...), custom_call_target="tpu_custom_call", output_to_operand_aliasing={{0}: (1, {}), {1}: (2, {})} | custom-call | tf_op jit(solution)/shard_map/second_kernel/pallas_call | solution.py:305
  41.6 2.4 %collective-permute-start.4 = (bf16[160,2560]{1,0:T(8,128)(2,1)S(1)}, bf16[160,2560]{1,0:T(8,128)(2,1)S(1)}, u32[]{:S(2)}, u32[]{:S(2)}) collective-permute-start(bf16[160,2560]{1,0:T(8,128)(2,1)S(1)} %get-tuple-element.16.theirs), channel_id=1, source_target_pairs={{0,1},{1,0},{2,3},{3,2},{4,5},{5,4},{6,7},{7,6},{8,9},{9,8},{10,11... | collective-permute-start | bytes 2457608 | tf_op jit(solution)/shard_map/ppermute | solution.py:308
  44.0 0.5 gains_kernel.1.gain
  44.5 1.5 %collective-permute-done.4.other = bf16[160,2560]{1,0:T(8,128)(2,1)S(1)} collective-permute-done((bf16[160,2560]{1,0:T(8,128)(2,1)S(1)}, bf16[160,2560]{1,0:T(8,128)(2,1)S(1)}, u32[]{:S(2)}, u32[]{:S(2)}) %collective-permute-start.4) | collective-permute-done | bytes 819232 | tf_op jit(solution)/shard_map/ppermute | solution.py:308
  46.0 1.3 %dispatch_kernel.1 = bf16[64,4,8,256]{3,2,1,0:T(8,128)(2,1)S(1)} custom-call(s32[50]{0:T(128)S(1)} %dynamic-slice_reduce_fusion.place_of, s32[50]{0:T(128)S(1)} %reshape_squeeze.3.listed, bf16[160,2560]{1,0:T(8,128)(2,1)S(1)} %get-tuple-element.15.mine, bf16[160,2560]{1,0:T(8,128)(2,1)S(1)} %collective-permute-done.4.other, f32[160,2560]{1,0:T(8,128)S(1)} %gains_kernel.1.gain), custom_call_target="tpu_custom_call" | custom-call | tf_op jit(solution)/shard_map/dispatch_kernel/pallas_call | solution.py:316
  47.2 48.2 %all_to_all.5 = bf16[256,8,256]{2,1,0:T(8,128)(2,1)S(1)} all-to-all(bf16[256,8,256]{2,1,0:T(8,128)(2,1)S(1)} %bitcast.10), channel_id=1, replica_groups={{0,2,4,6,8,10,12,14,16,18,20,22,24,26,28,30,32,34,36,38,40,42,44,46,48,..., dimensions={0} | all-to-all | bytes 2097152 | tf_op jit(solution)/shard_map/all_to_all | solution.py:331
  95.5 0.9 collect_kernel.1
  (9 shorter events, 0.2 us)
Async XLA Ops:
  0.0 26.3 %copy-start = (s32[64,50]{0,1:T(8,128)S(1)}, s32[64,50]{0,1:T(8,128)}, u32[]{:S(2)}) copy-start(s32[64,50]{0,1:T(8,128)} %param.8) | copy-start | bytes 38404
  0.0 10.1 %copy-start.1 = (s32[320,2]{0,1:T(2,128)S(1)}, s32[320,2]{0,1:T(2,128)}, u32[]{:S(2)}) copy-start(s32[320,2]{0,1:T(2,128)} %param.6) | copy-start | bytes 7684
  0.0 25.9 %copy-start.2 = (s32[64,2,5,5]{0,1,3,2:T(2,128)S(1)}, s32[64,2,5,5]{0,1,3,2:T(2,128)}, u32[]{:S(2)}) copy-start(s32[64,2,5,5]{0,1,3,2:T(2,128)} %param.7) | copy-start | bytes 38404
  2.6 7.8 %collective-permute-start = (bf16[320,64]{1,0:T(8,128)(2,1)S(1)}, bf16[320,64]{1,0:T(8,128)(2,1)S(1)}, u32[]{:S(2)}, u32[]{:S(2)}) collective-permute-start(bf16[320,64]{1,0:T(8,128)(2,1)S(1)} %across_kernel.1.across), channel_id=1, source_target_pairs={{1,2},{3,4},{5,6},{2,1},{4,3},{6,5},{9,10},{11,12},{13,14},{10,9},... | collective-permute-start | bytes 122888 | tf_op jit(solution)/shard_map/ppermute | solution.py:249
  3.6 6.8 %collective-permute-start.1 = (bf16[320,64]{1,0:T(8,128)(2,1)S(1)}, bf16[320,64]{1,0:T(8,128)(2,1)S(1)}, u32[]{:S(2)}, u32[]{:S(2)}) collective-permute-start(bf16[320,64]{1,0:T(8,128)(2,1)S(1)} %inside_kernel.1.inside), channel_id=1, source_target_pairs={{0,1},{2,3},{4,5},{6,7},{1,0},{3,2},{5,4},{7,6},{8,9},{10,11},{12,... | collective-permute-start | bytes 122888 | tf_op jit(solution)/shard_map/ppermute | solution.py:249
  11.0 22.0 %collective-permute-start.2 = (bf16[336,1024]{1,0:T(8,128)(2,1)S(1)}, bf16[336,1024]{1,0:T(8,128)(2,1)S(1)}, u32[]{:S(2)}, u32[]{:S(2)}) collective-permute-start(bf16[336,1024]{1,0:T(8,128)(2,1)S(1)} %whiten_kernel.1.white.here), channel_id=1, source_target_pairs={{0,8},{1,505},{2,10},{3,507},{4,12},{5,509},{6,14},{7,511},{8,16},... | collective-permute-start | bytes 2064392 | tf_op jit(solution)/shard_map/ppermute | solution.py:244
  14.4 24.8 %collective-permute-start.3 = (bf16[336,1024]{1,0:T(8,128)(2,1)S(1)}, bf16[336,1024]{1,0:T(8,128)(2,1)S(1)}, u32[]{:S(2)}, u32[]{:S(2)}) collective-permute-start(bf16[336,1024]{1,0:T(8,128)(2,1)S(1)} %whiten_kernel.1.white.here), channel_id=1, source_target_pairs={{0,504},{1,9},{2,506},{3,11},{4,508},{5,13},{6,510},{7,15},{8,0},{... | collective-permute-start | bytes 2064392 | tf_op jit(solution)/shard_map/ppermute | solution.py:244
  41.6 4.4 %collective-permute-start.4 = (bf16[160,2560]{1,0:T(8,128)(2,1)S(1)}, bf16[160,2560]{1,0:T(8,128)(2,1)S(1)}, u32[]{:S(2)}, u32[]{:S(2)}) collective-permute-start(bf16[160,2560]{1,0:T(8,128)(2,1)S(1)} %get-tuple-element.16.theirs), channel_id=1, source_target_pairs={{0,1},{1,0},{2,3},{3,2},{4,5},{5,4},{6,7},{7,6},{8,9},{9,8},{10,11... | collective-permute-start | bytes 2457608 | tf_op jit(solution)/shard_map/ppermute | solution.py:308

commit v7 on v6

--- a/solution.py
+++ b/solution.py
@@ -214,25 +214,29 @@
     total[...] = (mine[...].astype(jnp.float32) + other[...].astype(jnp.float32)) * gain[...]
     for slot in range(REACH * SUB * SUB):
         d, u, v = slot // (SUB * SUB), slot // SUB % SUB, slot % SUB
-
-        @pl.when(listed[slot] > 0)
-        def _():
-            for chip in range(CHIPS):
-                out[place_of[slot], chip] = total[
-                    chip * ROWS + u * SHARE : chip * ROWS + (u + 1) * SHARE,
-                    d * COLS + v * LAGS * SB : d * COLS + (v + 1) * LAGS * SB,
-                ].astype(jnp.bfloat16)
-
-
-def collect_kernel(received, out):
-    def block(b, _):
-        source = lax.rem(b + 1, BLOCKS)
-        total = received[source, 0].astype(jnp.float32)
-        for chip in range(1, CHIPS):
-            total += received[source, chip].astype(jnp.float32)
-        out[b] = total.astype(jnp.bfloat16)
-
-    lax.fori_loop(0, BLOCKS, block, None, unroll=8)
+        keep = listed[slot].astype(jnp.float32)
+        for chip in range(CHIPS):
+            tile = total[
+                chip * ROWS + u * SHARE : chip * ROWS + (u + 1) * SHARE,
+                d * COLS + v * LAGS * SB : d * COLS + (v + 1) * LAGS * SB,
+            ]
+            out[place_of[slot], chip] = (tile * keep).astype(jnp.bfloat16)
+
+
+def collect_kernel(received, out, sums, done):
+    half = BLOCKS // 2
+    copies = []
+    for part_of in range(2):
+        for b in range(part_of * half, (part_of + 1) * half):
+            total = received[(b + 1) % BLOCKS, 0].astype(jnp.float32)
+            for chip in range(1, CHIPS):
+                total += received[(b + 1) % BLOCKS, chip].astype(jnp.float32)
+            sums[b] = total.astype(jnp.bfloat16)
+        rows = pl.ds(part_of * half, half)
+        copies.append(pltpu.make_async_copy(sums.at[rows], out.at[rows], done.at[part_of]))
+        copies[-1].start()
+    for copy in copies:
+        copy.wait()
 
 
 def spread(x, forward):
@@ -336,9 +340,18 @@
         tiled=True,
         axis_index_groups=groups,
     )
-    merged = kernel(collect_kernel, bf16(BLOCKS, SHARE, LAGS * SB), 1)(
-        received.reshape(BLOCKS, CHIPS, SHARE, LAGS * SB)
-    )
+    merged = pl.pallas_call(
+        collect_kernel,
+        out_shape=bf16(BLOCKS, SHARE, LAGS * SB),
+        in_specs=[VMEM],
+        out_specs=pl.BlockSpec(memory_space=pl.ANY),
+        scratch_shapes=[
+            pltpu.VMEM((BLOCKS, SHARE, LAGS * SB), jnp.bfloat16),
+            pltpu.SemaphoreType.DMA((2,)),
+        ],
+        compiler_params=pltpu.CompilerParams(vmem_limit_bytes=4 * MIB),
+        name="collect_kernel",
+    )(received.reshape(BLOCKS, CHIPS, SHARE, LAGS * SB))
     return merged[None, :, None]
 
 

time: 96.7 us -> 96.2 us (level)
  no operation moved by 1% of the time
where the time goes in v7:
time: 96.2 us; the launch traced here: 95.9 us
  blocking collectives  48.2 us (50%)
  starting transfers between devices  23.9 us (25%)
  waiting for transfers between devices  13.1 us (14%)
  Pallas kernels  7.06 us (7%)
  local copies, waits for them, and re-layouts  3.48 us (4%)
    all_to_all x1, blocking collectives, body(): lax.all_to_all(outgoing.reshape(BLOCKS * CHIPS, SHARE, LAGS * SB), ('chan...  48.2 us
    ppermute x2, starting transfers between devices, spread(): return lax.ppermute(x, ('chan', 'freq'), route)  14.9 us
    ppermute x2, waiting for transfers between devices, spread(): return lax.ppermute(x, ('chan', 'freq'), route)  11.5 us
    ppermute x2, starting transfers between devices, swap(): return lax.ppermute(x, 'freq', pairs + [(k, i) for i, k in pairs])  6.52 us
    ppermute x1, starting transfers between devices, body(): other = lax.ppermute(theirs, 'freq', [(k, k ^ 1) for k in range(N_FREQ)])  2.41 us
    pallas_call x1, Pallas kernels, body(): kernel(second_kernel, (*kept, half, half), 6, scalars=1, aliases={1: 0, 2...  2.41 us
    reshape x1, local copies, waits for them, and re-layouts, body(): raw = spectra.reshape(CH, PARTS * BAND)  2.24 us
  transfers between devices with their start and end apart: 5, of which 4 were waited for; matrix products, arithmetic and copies ran while one was open for 1% of the time, Pallas kernels for 2%

profile of v7, /device:TPU:8, one launch (start us, length us, event | category | flops | bytes accessed | tf_op | source)
XLA Modules:
  0.0 95.9 jit_solution(11346986810763978797)
XLA Ops:
  0.0 2.2 %reshape.9.raw = bf16[320,1024]{1,0:T(8,128)(2,1)S(1)} reshape(bf16[320,2,2,256]{3,2,1,0:T(2,128)(2,1)} %param.5) | data formatting | bytes 1310720 | tf_op jit(solution)/shard_map/reshape | solution.py:278
  2.3 0.3 across_kernel.1.across
  2.6 0.7 collective-permute-start
  3.3 0.3 inside_kernel.1.inside
  3.6 5.9 %collective-permute-start.1 = (bf16[320,64]{1,0:T(8,128)(2,1)S(1)}, bf16[320,64]{1,0:T(8,128)(2,1)S(1)}, u32[]{:S(2)}, u32[]{:S(2)}) collective-permute-start(bf16[320,64]{1,0:T(8,128)(2,1)S(1)} %inside_kernel.1.inside), channel_id=1, source_target_pairs={{0,1},{2,3},{4,5},{6,7},{1,0},{3,2},{5,4},{7,6},{8,9},{10,11},{12,... | collective-permute-start | bytes 122888 | tf_op jit(solution)/shard_map/ppermute | solution.py:253
  9.4 0.7 dynamic-slice_bitcast_fusion.table
  10.1 0.1 validity_kernel.1
  10.3 0.6 whiten_kernel.1.white.here
  11.0 3.4 %collective-permute-start.2 = (bf16[336,1024]{1,0:T(8,128)(2,1)S(1)}, bf16[336,1024]{1,0:T(8,128)(2,1)S(1)}, u32[]{:S(2)}, u32[]{:S(2)}) collective-permute-start(bf16[336,1024]{1,0:T(8,128)(2,1)S(1)} %whiten_kernel.1.white.here), channel_id=1, source_target_pairs={{0,8},{1,505},{2,10},{3,507},{4,12},{5,509},{6,14},{7,511},{8,16},... | collective-permute-start | bytes 2064392 | tf_op jit(solution)/shard_map/ppermute | solution.py:248
  14.4 11.6 %collective-permute-start.3 = (bf16[336,1024]{1,0:T(8,128)(2,1)S(1)}, bf16[336,1024]{1,0:T(8,128)(2,1)S(1)}, u32[]{:S(2)}, u32[]{:S(2)}) collective-permute-start(bf16[336,1024]{1,0:T(8,128)(2,1)S(1)} %whiten_kernel.1.white.here), channel_id=1, source_target_pairs={{0,504},{1,9},{2,506},{3,11},{4,508},{5,13},{6,510},{7,15},{8,0},{... | collective-permute-start | bytes 2064392 | tf_op jit(solution)/shard_map/ppermute | solution.py:248
  26.0 0.1 constant_dynamic-slice_fusion
  26.1 0.2 copy.10
  26.3 0.2 dynamic-slice_reduce_fusion.place_of
  26.5 0.5 rotate_kernel.1.right_here
  27.0 5.9 %collective-permute-done.2.first = bf16[336,1024]{1,0:T(8,128)(2,1)S(1)} collective-permute-done((bf16[336,1024]{1,0:T(8,128)(2,1)S(1)}, bf16[336,1024]{1,0:T(8,128)(2,1)S(1)}, u32[]{:S(2)}, u32[]{:S(2)}) %collective-permute-start.2) | collective-permute-done | bytes 688160 | tf_op jit(solution)/shard_map/ppermute | solution.py:248
  33.0 0.6 first_kernel.1
  33.6 5.6 %collective-permute-done.3.second = bf16[336,1024]{1,0:T(8,128)(2,1)S(1)} collective-permute-done((bf16[336,1024]{1,0:T(8,128)(2,1)S(1)}, bf16[336,1024]{1,0:T(8,128)(2,1)S(1)}, u32[]{:S(2)}, u32[]{:S(2)}) %collective-permute-start.3) | collective-permute-done | bytes 688160 | tf_op jit(solution)/shard_map/ppermute | solution.py:248
  39.2 2.4 %second_kernel.1 = (f32[320,1024]{1,0:T(8,128)S(1)}, bf16[1280,1024]{1,0:T(8,128)(2,1)S(1)}, bf16[160,2560]{1,0:T(8,128)(2,1)S(1)}, bf16[160,2560]{1,0:T(8,128)(2,1)S(1)}) custom-call(s32[1]{0:T(128)} %bitcast.odd, f32[320,1024]{1,0:T(8,128)S(1)} %get-tuple-element.13.left_in, ...), custom_call_target="tpu_custom_call", output_to_operand_aliasing={{0}: (1, {}), {1}: (2, {})} | custom-call | tf_op jit(solution)/shard_map/second_kernel/pallas_call | solution.py:309
  41.6 2.4 %collective-permute-start.4 = (bf16[160,2560]{1,0:T(8,128)(2,1)S(1)}, bf16[160,2560]{1,0:T(8,128)(2,1)S(1)}, u32[]{:S(2)}, u32[]{:S(2)}) collective-permute-start(bf16[160,2560]{1,0:T(8,128)(2,1)S(1)} %get-tuple-element.16.theirs), channel_id=1, source_target_pairs={{0,1},{1,0},{2,3},{3,2},{4,5},{5,4},{6,7},{7,6},{8,9},{9,8},{10,11... | collective-permute-start | bytes 2457608 | tf_op jit(solution)/shard_map/ppermute | solution.py:312
  44.0 0.5 gains_kernel.1.gain
  44.5 1.5 %collective-permute-done.4.other = bf16[160,2560]{1,0:T(8,128)(2,1)S(1)} collective-permute-done((bf16[160,2560]{1,0:T(8,128)(2,1)S(1)}, bf16[160,2560]{1,0:T(8,128)(2,1)S(1)}, u32[]{:S(2)}, u32[]{:S(2)}) %collective-permute-start.4) | collective-permute-done | bytes 819232 | tf_op jit(solution)/shard_map/ppermute | solution.py:312
  46.0 0.9 dispatch_kernel.1
  46.9 48.2 %all_to_all.5 = bf16[256,8,256]{2,1,0:T(8,128)(2,1)S(1)} all-to-all(bf16[256,8,256]{2,1,0:T(8,128)(2,1)S(1)} %bitcast.10), channel_id=1, replica_groups={{0,2,4,6,8,10,12,14,16,18,20,22,24,26,28,30,32,34,36,38,40,42,44,46,48,..., dimensions={0} | all-to-all | bytes 2097152 | tf_op jit(solution)/shard_map/all_to_all | solution.py:335
  95.1 0.8 collect_kernel.1
  (9 shorter events, 0.2 us)
Async XLA Ops:
  0.0 26.3 %copy-start = (s32[64,50]{0,1:T(8,128)S(1)}, s32[64,50]{0,1:T(8,128)}, u32[]{:S(2)}) copy-start(s32[64,50]{0,1:T(8,128)} %param.8) | copy-start | bytes 38404
  0.0 10.1 %copy-start.1 = (s32[320,2]{0,1:T(2,128)S(1)}, s32[320,2]{0,1:T(2,128)}, u32[]{:S(2)}) copy-start(s32[320,2]{0,1:T(2,128)} %param.6) | copy-start | bytes 7684
  0.0 25.9 %copy-start.2 = (s32[64,2,5,5]{0,1,3,2:T(2,128)S(1)}, s32[64,2,5,5]{0,1,3,2:T(2,128)}, u32[]{:S(2)}) copy-start(s32[64,2,5,5]{0,1,3,2:T(2,128)} %param.7) | copy-start | bytes 38404
  2.6 7.8 %collective-permute-start = (bf16[320,64]{1,0:T(8,128)(2,1)S(1)}, bf16[320,64]{1,0:T(8,128)(2,1)S(1)}, u32[]{:S(2)}, u32[]{:S(2)}) collective-permute-start(bf16[320,64]{1,0:T(8,128)(2,1)S(1)} %across_kernel.1.across), channel_id=1, source_target_pairs={{1,2},{3,4},{5,6},{2,1},{4,3},{6,5},{9,10},{11,12},{13,14},{10,9},... | collective-permute-start | bytes 122888 | tf_op jit(solution)/shard_map/ppermute | solution.py:253
  3.6 6.8 %collective-permute-start.1 = (bf16[320,64]{1,0:T(8,128)(2,1)S(1)}, bf16[320,64]{1,0:T(8,128)(2,1)S(1)}, u32[]{:S(2)}, u32[]{:S(2)}) collective-permute-start(bf16[320,64]{1,0:T(8,128)(2,1)S(1)} %inside_kernel.1.inside), channel_id=1, source_target_pairs={{0,1},{2,3},{4,5},{6,7},{1,0},{3,2},{5,4},{7,6},{8,9},{10,11},{12,... | collective-permute-start | bytes 122888 | tf_op jit(solution)/shard_map/ppermute | solution.py:253
  11.0 22.0 %collective-permute-start.2 = (bf16[336,1024]{1,0:T(8,128)(2,1)S(1)}, bf16[336,1024]{1,0:T(8,128)(2,1)S(1)}, u32[]{:S(2)}, u32[]{:S(2)}) collective-permute-start(bf16[336,1024]{1,0:T(8,128)(2,1)S(1)} %whiten_kernel.1.white.here), channel_id=1, source_target_pairs={{0,8},{1,505},{2,10},{3,507},{4,12},{5,509},{6,14},{7,511},{8,16},... | collective-permute-start | bytes 2064392 | tf_op jit(solution)/shard_map/ppermute | solution.py:248
  14.4 24.8 %collective-permute-start.3 = (bf16[336,1024]{1,0:T(8,128)(2,1)S(1)}, bf16[336,1024]{1,0:T(8,128)(2,1)S(1)}, u32[]{:S(2)}, u32[]{:S(2)}) collective-permute-start(bf16[336,1024]{1,0:T(8,128)(2,1)S(1)} %whiten_kernel.1.white.here), channel_id=1, source_target_pairs={{0,504},{1,9},{2,506},{3,11},{4,508},{5,13},{6,510},{7,15},{8,0},{... | collective-permute-start | bytes 2064392 | tf_op jit(solution)/shard_map/ppermute | solution.py:248
  41.6 4.4 %collective-permute-start.4 = (bf16[160,2560]{1,0:T(8,128)(2,1)S(1)}, bf16[160,2560]{1,0:T(8,128)(2,1)S(1)}, u32[]{:S(2)}, u32[]{:S(2)}) collective-permute-start(bf16[160,2560]{1,0:T(8,128)(2,1)S(1)} %get-tuple-element.16.theirs), channel_id=1, source_target_pairs={{0,1},{1,0},{2,3},{3,2},{4,5},{5,4},{6,7},{7,6},{8,9},{9,8},{10,11... | collective-permute-start | bytes 2457608 | tf_op jit(solution)/shard_map/ppermute | solution.py:312

commit v8 on v7

--- a/solution.py
+++ b/solution.py
@@ -146,8 +146,9 @@
                     out[dest, x] = value.astype(jnp.bfloat16)
 
 
-def rotate_kernel(white, table, out):
+def rotate_kernel(white, table, out, blank):
     rotate(plain(white), table, out)
+    blank[...] = jnp.zeros_like(blank)
 
 
 def place(out, odd, read):
@@ -209,8 +210,7 @@
     out[...] = jnp.where(joint > 1.5, (2 * FREQS) ** -0.5, FREQS**-0.5)
 
 
-def dispatch_kernel(place_of, listed, mine, other, gain, out, total):
-    out[...] = jnp.zeros_like(out)
+def dispatch_kernel(place_of, listed, mine, other, gain, blank, out, total):
     total[...] = (mine[...].astype(jnp.float32) + other[...].astype(jnp.float32)) * gain[...]
     for slot in range(REACH * SUB * SUB):
         d, u, v = slot // (SUB * SUB), slot // SUB % SUB, slot % SUB
@@ -293,7 +293,8 @@
     )(freq[None], raw, across, inside, tail, columns, table)
     first = spread(white, 0)
     second = spread(white, 1)
-    right_here = kernel(rotate_kernel, bf16(COLS, PARTS * BAND), 2)(white, table)
+    sending = bf16(BLOCKS, CHIPS, SHARE, LAGS * SB)
+    right_here, blank = kernel(rotate_kernel, (bf16(COLS, PARTS * BAND), sending), 2)(white, table)
 
     source = (chan + BLOCKS - 1) % BLOCKS
     listed = pair_mask[source].reshape(-1)
@@ -319,11 +320,12 @@
     )(odd, first, white, second, theirs)
     outgoing = kernel(
         dispatch_kernel,
-        bf16(BLOCKS, CHIPS, SHARE, LAGS * SB),
-        5,
+        sending,
+        6,
         [((HALF_ROWS, REACH * COLS), f32)],
         scalars=2,
-    )(place_of, listed, mine, other, gain)
+        aliases={5: 0},
+    )(place_of, listed, mine, other, gain, blank)
     groups = [
         [
             b * N_FREQ + 2 * chip + core

time: 96.2 us -> 96.2 us (level)
  no operation moved by 1% of the time
where the time goes in v8:
time: 96.2 us; the launch traced here: 95.9 us
  blocking collectives  48.2 us (50%)
  starting transfers between devices  23.9 us (25%)
  waiting for transfers between devices  13 us (14%)
  Pallas kernels  7.08 us (7%)
  local copies, waits for them, and re-layouts  3.48 us (4%)
    all_to_all x1, blocking collectives, body(): lax.all_to_all(outgoing.reshape(BLOCKS * CHIPS, SHARE, LAGS * SB), ('chan...  48.2 us
    ppermute x2, starting transfers between devices, spread(): return lax.ppermute(x, ('chan', 'freq'), route)  14.9 us
    ppermute x2, waiting for transfers between devices, spread(): return lax.ppermute(x, ('chan', 'freq'), route)  11.5 us
    ppermute x2, starting transfers between devices, swap(): return lax.ppermute(x, 'freq', pairs + [(k, i) for i, k in pairs])  6.52 us
    ppermute x1, starting transfers between devices, body(): other = lax.ppermute(theirs, 'freq', [(k, k ^ 1) for k in range(N_FREQ)])  2.41 us
    pallas_call x1, Pallas kernels, body(): kernel(second_kernel, (*kept, half, half), 6, scalars=1, aliases={1: 0, 2...  2.41 us
    reshape x1, local copies, waits for them, and re-layouts, body(): raw = spectra.reshape(CH, PARTS * BAND)  2.24 us
  transfers between devices with their start and end apart: 5, of which 4 were waited for; matrix products, arithmetic and copies ran while one was open for 1% of the time, Pallas kernels for 2%

profile of v8, /device:TPU:8, one launch (start us, length us, event | category | flops | bytes accessed | tf_op | source)
XLA Modules:
  0.0 95.9 jit_solution(730125895753826903)
XLA Ops:
  0.0 2.2 %reshape.9.raw = bf16[320,1024]{1,0:T(8,128)(2,1)S(1)} reshape(bf16[320,2,2,256]{3,2,1,0:T(2,128)(2,1)} %param.5) | data formatting | bytes 1310720 | tf_op jit(solution)/shard_map/reshape | solution.py:278
  2.3 0.3 across_kernel.1.across
  2.6 0.7 collective-permute-start
  3.3 0.3 inside_kernel.1.inside
  3.6 5.9 %collective-permute-start.1 = (bf16[320,64]{1,0:T(8,128)(2,1)S(1)}, bf16[320,64]{1,0:T(8,128)(2,1)S(1)}, u32[]{:S(2)}, u32[]{:S(2)}) collective-permute-start(bf16[320,64]{1,0:T(8,128)(2,1)S(1)} %inside_kernel.1.inside), channel_id=1, source_target_pairs={{0,1},{2,3},{4,5},{6,7},{1,0},{3,2},{5,4},{7,6},{8,9},{10,11},{12,... | collective-permute-start | bytes 122888 | tf_op jit(solution)/shard_map/ppermute | solution.py:253
  9.4 0.7 dynamic-slice_bitcast_fusion.table
  10.1 0.1 validity_kernel.1
  10.3 0.6 whiten_kernel.1.white.here
  11.0 3.4 %collective-permute-start.2 = (bf16[336,1024]{1,0:T(8,128)(2,1)S(1)}, bf16[336,1024]{1,0:T(8,128)(2,1)S(1)}, u32[]{:S(2)}, u32[]{:S(2)}) collective-permute-start(bf16[336,1024]{1,0:T(8,128)(2,1)S(1)} %whiten_kernel.1.white.here), channel_id=1, source_target_pairs={{0,8},{1,505},{2,10},{3,507},{4,12},{5,509},{6,14},{7,511},{8,16},... | collective-permute-start | bytes 2064392 | tf_op jit(solution)/shard_map/ppermute | solution.py:248
  14.4 11.6 %collective-permute-start.3 = (bf16[336,1024]{1,0:T(8,128)(2,1)S(1)}, bf16[336,1024]{1,0:T(8,128)(2,1)S(1)}, u32[]{:S(2)}, u32[]{:S(2)}) collective-permute-start(bf16[336,1024]{1,0:T(8,128)(2,1)S(1)} %whiten_kernel.1.white.here), channel_id=1, source_target_pairs={{0,504},{1,9},{2,506},{3,11},{4,508},{5,13},{6,510},{7,15},{8,0},{... | collective-permute-start | bytes 2064392 | tf_op jit(solution)/shard_map/ppermute | solution.py:248
  26.0 0.1 constant_dynamic-slice_fusion
  26.1 0.2 copy.11
  26.3 0.2 dynamic-slice_reduce_fusion.place_of
  26.5 0.6 rotate_kernel.1
  27.1 5.9 %collective-permute-done.2.first = bf16[336,1024]{1,0:T(8,128)(2,1)S(1)} collective-permute-done((bf16[336,1024]{1,0:T(8,128)(2,1)S(1)}, bf16[336,1024]{1,0:T(8,128)(2,1)S(1)}, u32[]{:S(2)}, u32[]{:S(2)}) %collective-permute-start.2) | collective-permute-done | bytes 688160 | tf_op jit(solution)/shard_map/ppermute | solution.py:248
  33.0 0.6 first_kernel.1
  33.6 5.6 %collective-permute-done.3.second = bf16[336,1024]{1,0:T(8,128)(2,1)S(1)} collective-permute-done((bf16[336,1024]{1,0:T(8,128)(2,1)S(1)}, bf16[336,1024]{1,0:T(8,128)(2,1)S(1)}, u32[]{:S(2)}, u32[]{:S(2)}) %collective-permute-start.3) | collective-permute-done | bytes 688160 | tf_op jit(solution)/shard_map/ppermute | solution.py:248
  39.2 2.4 %second_kernel.1 = (f32[320,1024]{1,0:T(8,128)S(1)}, bf16[1280,1024]{1,0:T(8,128)(2,1)S(1)}, bf16[160,2560]{1,0:T(8,128)(2,1)S(1)}, bf16[160,2560]{1,0:T(8,128)(2,1)S(1)}) custom-call(s32[1]{0:T(128)} %bitcast.odd, f32[320,1024]{1,0:T(8,128)S(1)} %get-tuple-element.16.left_in, ...), custom_call_target="tpu_custom_call", output_to_operand_aliasing={{0}: (1, {}), {1}: (2, {})} | custom-call | tf_op jit(solution)/shard_map/second_kernel/pallas_call | solution.py:310
  41.6 2.4 %collective-permute-start.4 = (bf16[160,2560]{1,0:T(8,128)(2,1)S(1)}, bf16[160,2560]{1,0:T(8,128)(2,1)S(1)}, u32[]{:S(2)}, u32[]{:S(2)}) collective-permute-start(bf16[160,2560]{1,0:T(8,128)(2,1)S(1)} %get-tuple-element.19.theirs), channel_id=1, source_target_pairs={{0,1},{1,0},{2,3},{3,2},{4,5},{5,4},{6,7},{7,6},{8,9},{9,8},{10,11... | collective-permute-start | bytes 2457608 | tf_op jit(solution)/shard_map/ppermute | solution.py:313
  44.0 0.5 gains_kernel.1.gain
  44.5 1.5 %collective-permute-done.4.other = bf16[160,2560]{1,0:T(8,128)(2,1)S(1)} collective-permute-done((bf16[160,2560]{1,0:T(8,128)(2,1)S(1)}, bf16[160,2560]{1,0:T(8,128)(2,1)S(1)}, u32[]{:S(2)}, u32[]{:S(2)}) %collective-permute-start.4) | collective-permute-done | bytes 819232 | tf_op jit(solution)/shard_map/ppermute | solution.py:313
  46.0 0.8 dispatch_kernel.1
  46.8 48.2 %all_to_all.5 = bf16[256,8,256]{2,1,0:T(8,128)(2,1)S(1)} all-to-all(bf16[256,8,256]{2,1,0:T(8,128)(2,1)S(1)} %bitcast.11), channel_id=1, replica_groups={{0,2,4,6,8,10,12,14,16,18,20,22,24,26,28,30,32,34,36,38,40,42,44,46,48,..., dimensions={0} | all-to-all | bytes 2097152 | tf_op jit(solution)/shard_map/all_to_all | solution.py:337
  95.1 0.8 collect_kernel.1
  (9 shorter events, 0.2 us)
Async XLA Ops:
  0.0 26.3 %copy-start = (s32[64,50]{0,1:T(8,128)S(1)}, s32[64,50]{0,1:T(8,128)}, u32[]{:S(2)}) copy-start(s32[64,50]{0,1:T(8,128)} %param.8) | copy-start | bytes 38404
  0.0 10.1 %copy-start.1 = (s32[320,2]{0,1:T(2,128)S(1)}, s32[320,2]{0,1:T(2,128)}, u32[]{:S(2)}) copy-start(s32[320,2]{0,1:T(2,128)} %param.6) | copy-start | bytes 7684
  0.0 25.9 %copy-start.2 = (s32[64,2,5,5]{0,1,3,2:T(2,128)S(1)}, s32[64,2,5,5]{0,1,3,2:T(2,128)}, u32[]{:S(2)}) copy-start(s32[64,2,5,5]{0,1,3,2:T(2,128)} %param.7) | copy-start | bytes 38404
  2.6 7.8 %collective-permute-start = (bf16[320,64]{1,0:T(8,128)(2,1)S(1)}, bf16[320,64]{1,0:T(8,128)(2,1)S(1)}, u32[]{:S(2)}, u32[]{:S(2)}) collective-permute-start(bf16[320,64]{1,0:T(8,128)(2,1)S(1)} %across_kernel.1.across), channel_id=1, source_target_pairs={{1,2},{3,4},{5,6},{2,1},{4,3},{6,5},{9,10},{11,12},{13,14},{10,9},... | collective-permute-start | bytes 122888 | tf_op jit(solution)/shard_map/ppermute | solution.py:253
  3.6 6.8 %collective-permute-start.1 = (bf16[320,64]{1,0:T(8,128)(2,1)S(1)}, bf16[320,64]{1,0:T(8,128)(2,1)S(1)}, u32[]{:S(2)}, u32[]{:S(2)}) collective-permute-start(bf16[320,64]{1,0:T(8,128)(2,1)S(1)} %inside_kernel.1.inside), channel_id=1, source_target_pairs={{0,1},{2,3},{4,5},{6,7},{1,0},{3,2},{5,4},{7,6},{8,9},{10,11},{12,... | collective-permute-start | bytes 122888 | tf_op jit(solution)/shard_map/ppermute | solution.py:253
  11.0 22.0 %collective-permute-start.2 = (bf16[336,1024]{1,0:T(8,128)(2,1)S(1)}, bf16[336,1024]{1,0:T(8,128)(2,1)S(1)}, u32[]{:S(2)}, u32[]{:S(2)}) collective-permute-start(bf16[336,1024]{1,0:T(8,128)(2,1)S(1)} %whiten_kernel.1.white.here), channel_id=1, source_target_pairs={{0,8},{1,505},{2,10},{3,507},{4,12},{5,509},{6,14},{7,511},{8,16},... | collective-permute-start | bytes 2064392 | tf_op jit(solution)/shard_map/ppermute | solution.py:248
  14.4 24.8 %collective-permute-start.3 = (bf16[336,1024]{1,0:T(8,128)(2,1)S(1)}, bf16[336,1024]{1,0:T(8,128)(2,1)S(1)}, u32[]{:S(2)}, u32[]{:S(2)}) collective-permute-start(bf16[336,1024]{1,0:T(8,128)(2,1)S(1)} %whiten_kernel.1.white.here), channel_id=1, source_target_pairs={{0,504},{1,9},{2,506},{3,11},{4,508},{5,13},{6,510},{7,15},{8,0},{... | collective-permute-start | bytes 2064392 | tf_op jit(solution)/shard_map/ppermute | solution.py:248
  41.6 4.4 %collective-permute-start.4 = (bf16[160,2560]{1,0:T(8,128)(2,1)S(1)}, bf16[160,2560]{1,0:T(8,128)(2,1)S(1)}, u32[]{:S(2)}, u32[]{:S(2)}) collective-permute-start(bf16[160,2560]{1,0:T(8,128)(2,1)S(1)} %get-tuple-element.19.theirs), channel_id=1, source_target_pairs={{0,1},{1,0},{2,3},{3,2},{4,5},{5,4},{6,7},{7,6},{8,9},{9,8},{10,11... | collective-permute-start | bytes 2457608 | tf_op jit(solution)/shard_map/ppermute | solution.py:313
